TPU v7x, 128 devices: a whole 4x4x4 slice. The times are simulated.
128 devices in a mesh: gx: 4 (over x), gy: 32 (over z, y, core).
Axes of the slice: x: 4, y: 4, z: 4, core: 2. Of those that a mesh axis runs over, the one named last changes fastest.
Arguments:
- a_tiles: float32 [6144, 3, 128, 128], P(('gx', 'gy')), may hold values from -0.5 to 0.5
- a_cols: int32 [6144, 3], P(('gx', 'gy')), may hold values from 0 to 6143, as said below
- a_len: int32 [6144], P(('gx', 'gy')), may hold values from 1 to 3, as said below
- p_tiles: float32 [6144, 2, 128, 128], P(('gx', 'gy')), may hold values from -1 to 1
- aggregate: int32 [6144], replicated, may hold values from 0 to 2047, as said below
- owner: int32 [2048], replicated, may hold values from 0 to 127, as said below
Outputs:
- coarse_operator: float32 [2048, 7, 128, 128], P(('gx', 'gy'))
Inputs may be any that keep to these rules, and one draw needn't show every extreme that they name: For k < a_len[i] the a_cols[i, k] are distinct among i - 1, i, i + 1 modulo 6144, the first being i; the later slots hold the remaining ones of these and belong to no operator. a_len[i] = 3 where i mod 48 is 0 or 47. aggregate[i] is i // 3 or i // 3 - 1, modulo 2048. The owner of row r of the 16 coarse rows of the device at (x, y) is the device at ((x + u[r]) mod 4, (v[y] + t[r]) mod 32), where u takes each value 16 // 4 times, v is a permutation and t takes no value more than 1 times, that many in every draw; each device owns exactly 16 coarse rows.
All inputs are finite; a program needn't handle non-finite values.
Results may differ from a plain program's by a relative error of at most 0.0003.
Values sent between devices are 32-bit elements; how exact they have to be, the bound alone decides.
No kernel may reach another device: no remote copies, remote signals or barrier semaphores. Data moves between devices by JAX's collectives and lax.ppermute only.
A program may use at most 192 MiB of HBM per device.

v0:
```python
import jax
import jax.numpy as jnp
from jax import lax
from jax.sharding import PartitionSpec as P

KA = 3
KP = 2
AWIN = 5
CWIN = 7


highest = lax.Precision.HIGHEST


def with_halo(x, sides, width):
    for axis, dim in sides:
        size, length = (lax.axis_size(axis), x.shape[dim])
        up = [(i, (i + 1) % size) for i in range(size)]
        down = [(j, i) for i, j in up]
        last = lax.slice_in_dim(x, length - width, length, axis=dim)
        initial = lax.slice_in_dim(x, 0, width, axis=dim)
        before = lax.ppermute(last, axis, up)
        after = lax.ppermute(initial, axis, down)
        x = jnp.concatenate([before, x, after], axis=dim)
    return x


def slot_rank(target, valid, count, depth):
    length = target.shape[0]
    order = jnp.arange(length)
    earlier = (
        (target[None, :] == target[:, None]) & valid[None, :] & (order[None, :] < order[:, None])
    )
    rank = jnp.sum(earlier.astype(jnp.int32), axis=1)
    place = jnp.where(valid, target * depth + rank, -1)
    hits = place[None, :] == jnp.arange(count * depth)[:, None]
    anchor = jnp.sum(jnp.where(hits, order[None, :], 0), axis=1)
    filled = jnp.any(hits, axis=1)
    return (anchor.reshape(count, depth), filled.reshape(count, depth))


def pack_rows(rows, anchor, filled):
    picked = rows[anchor.reshape(-1)] * filled.reshape(-1)[:, None, None, None].astype(jnp.float32)
    return picked.reshape(anchor.shape + rows.shape[1:])


def received_ids(held, valid, target, receiver, count, depth):

    def single(held_row, valid_row, target_row):
        anchor, filled = slot_rank(target_row, valid_row, count, depth)
        mine = filled[receiver]
        return (jnp.where(mine, held_row[anchor[receiver]], -1), mine)

    return jax.vmap(single)(held, valid, target)


def product_rows(a_rows, hot_rows, source, index_rows):
    chosen = source[index_rows]
    pieces = jnp.einsum("rkab,rkmbc->rkmac", a_rows, chosen, precision=highest)
    return jnp.einsum("rkms,rkmac->rsac", hot_rows, pieces, precision=highest)


def shards(a_tiles, a_cols, a_len, p_tiles, aggregate, owner):
    count_x = lax.axis_size("gx")
    count_y = lax.axis_size("gy")
    index_x = lax.axis_index("gx")
    index_y = lax.axis_index("gy")
    device = index_x * count_y + index_y
    fine_rows = a_tiles.shape[0]
    coarse_rows = fine_rows // 3
    fine_total = fine_rows * count_x * count_y
    coarse_total = coarse_rows * count_x * count_y
    first_row = device * fine_rows
    global_rows = first_row + jnp.arange(fine_rows)
    center = global_rows // 3
    column_coarse = (aggregate[a_cols][:, :, None] + jnp.arange(KP)) % coarse_total
    slots = (column_coarse - center[:, None, None] + 2) % coarse_total
    active = jnp.arange(KA)[None, :] < a_len[:, None]
    selector = ((slots[..., None] == jnp.arange(AWIN)) & active[:, :, None, None]).astype(
        jnp.float32
    )
    nearby = (a_cols - first_row + 1) % fine_total
    extended = with_halo(p_tiles, ((("gx", "gy"), 0),), 1)
    applied = product_rows(a_tiles, selector, extended, nearby)
    own_coarse = (aggregate[global_rows][:, None] + jnp.arange(KP)) % coarse_total
    window_row = (own_coarse - device * coarse_rows + 1) % coarse_total
    window_col = (
        center[:, None, None] + jnp.arange(AWIN) - 2 - own_coarse[:, :, None] + 3
    ) % coarse_total

    def accumulate(partial_rows, block):
        first = block * 12
        ap_block = lax.dynamic_slice_in_dim(applied, first, 12, 0)
        p_block = lax.dynamic_slice_in_dim(p_tiles, first, 12, 0)
        row_block = lax.dynamic_slice_in_dim(window_row, first, 12, 0) - block * 4
        col_block = lax.dynamic_slice_in_dim(window_col, first, 12, 0)
        paired = jnp.einsum("imba,isbc->imsac", p_block, ap_block, precision=highest)
        col_hot = (col_block[..., None] == jnp.arange(CWIN)).astype(jnp.float32)
        placed = jnp.einsum("imsw,imsac->imwac", col_hot, paired, precision=highest)
        row_hot = (row_block[..., None] == jnp.arange(6)).astype(jnp.float32)
        added = jnp.einsum("imr,imwac->rwac", row_hot, placed, precision=highest)
        current = lax.dynamic_slice_in_dim(partial_rows, block * 4, 6, 0)
        return (lax.dynamic_update_slice_in_dim(partial_rows, current + added, block * 4, 0), None)

    start_value = jnp.zeros((coarse_rows + 2, CWIN) + a_tiles.shape[2:], jnp.float32)
    partial_rows, unused = lax.scan(accumulate, start_value, jnp.arange(fine_rows // 12))
    padded = with_halo(partial_rows, ((("gx", "gy"), 0),), 1)
    complete = jnp.concatenate(
        [
            partial_rows[1:2] + padded[:1],
            partial_rows[2:coarse_rows],
            partial_rows[coarse_rows : coarse_rows + 1] + padded[-1:],
        ],
        axis=0,
    )
    held = device * coarse_rows + jnp.arange(coarse_rows)
    every = jnp.ones((coarse_rows,), bool)
    depth_y = max(1, coarse_rows // count_y)
    depth_x = coarse_rows // count_x
    anchor, filled = slot_rank(owner[held] // count_y, every, count_x, depth_x)
    moved = lax.all_to_all(
        pack_rows(complete, anchor, filled), "gx", split_axis=0, concat_axis=0, tiled=True
    )

    def slab_held(column):
        senders = ((jnp.arange(count_x) * count_y + column) * coarse_rows)[:, None] + jnp.arange(
            coarse_rows
        )
        row_ids, row_flags = received_ids(
            senders,
            jnp.ones(senders.shape, bool),
            owner[senders] // count_y,
            index_x,
            count_x,
            depth_x,
        )
        return (row_ids.reshape(-1), row_flags.reshape(-1))

    mid_ids, mid_flags = slab_held(index_y)
    mid_rows = moved.reshape((-1,) + moved.shape[2:])
    anchor, filled = slot_rank(
        owner[jnp.maximum(mid_ids, 0)] % count_y, mid_flags, count_y, depth_y
    )
    moved = lax.all_to_all(
        pack_rows(mid_rows, anchor, filled), "gy", split_axis=0, concat_axis=0, tiled=True
    )
    held_all, flags_all = jax.vmap(slab_held)(jnp.arange(count_y))
    final_ids, final_flags = received_ids(
        held_all, flags_all, owner[jnp.maximum(held_all, 0)] % count_y, index_y, count_y, depth_y
    )
    flat_rows = moved.reshape((-1,) + moved.shape[2:])
    flat_ids = final_ids.reshape(-1)
    flat_flags = final_flags.reshape(-1)
    below = (flat_ids[None, :] < flat_ids[:, None]) & flat_flags[None, :]
    rank = jnp.sum(below.astype(jnp.int32), axis=1)
    hits = (rank[None, :] == jnp.arange(coarse_rows)[:, None]) & flat_flags[None, :]
    picked = jnp.sum(jnp.where(hits, jnp.arange(flat_ids.shape[0])[None, :], 0), axis=1)
    return flat_rows[picked]


def solution(mesh):
    in_specs = (
        P(("gx", "gy"), None, None, None),
        P(("gx", "gy"), None),
        P(("gx", "gy")),
        P(("gx", "gy"), None, None, None),
        P(),
        P(),
    )
    out_specs = P(("gx", "gy"), None, None, None)
    return jax.shard_map(shards, mesh=mesh, in_specs=in_specs, out_specs=out_specs, check_vma=False)
```

profile of v0, /device:TPU:0, one launch (start us, length us, event | category | flops | bytes accessed | tf_op | source)
XLA Modules:
  0.0 728.4 jit_solution(9126406958303512082)
XLA Ops:
  1.1 8.3 %collective-permute-start.1 = (f32[1,2,128,128]{3,2,1,0:T(8,128)S(1)}, f32[1,2,128,128]{3,2,1,0:T(8,128)S(1)}, u32[]{:S(2)}, u32[]{:S(2)}) collective-permute-start(f32[1,2,128,128]{3,2,1,0:T(8,128)S(1)} %get-tuple-element.163), channel_id=1, source_target_pairs={{1,0},{2,1},{3,2},{4,3},{5,4},{6,5},{7,6},{8,7},{9,8},{10,9},{11,1... | collective-permute-start | bytes 393224 | tf_op jit(solution)/shard_map/ppermute | solution.py:23
  26.5 13.5 %gather_fusion.2 = f32[144,2,128,128]{3,2,1,0:T(8,128)} fusion(f32[50,2,128,128]{3,2,1,0:T(8,128)} %pad_maximum_fusion.1, s32[1024]{0:T(1024)S(1)} %pad_clamp_fusion.7), kind=kCustom, calls=%fused_computation.2 | custom fusion | bytes 37749312 | tf_op jit(solution)/shard_map/gather | solution.py:58
  40.0 38.9 %fusion.24 = f32[48,3,2,128,128]{3,4,2,1,0:T(8,128)} fusion(f32[48,3,2,128,128]{4,3,2,1,0:T(8,128)} %bitcast.140, f32[48,3,128,128]{3,2,1,0:T(8,128)} %param.8), kind=kOutput, calls=%fused_computation.40 | convolution fusion | flops 7247757312 | bytes 47185920 | tf_op jit(solution)/shard_map/rkab,rkmbc->rkmac/dot_general | solution.py:59
  78.9 25.6 %copy.76 = f32[48,3,2,128,128]{4,1,2,3,0:T(4,128)} copy(f32[48,3,2,128,128]{3,4,2,1,0:T(8,128)} %fusion.24) | data formatting | bytes 37748736 | tf_op jit(solution)/shard_map/rkab,rkmbc->rkmac/transpose | solution.py:59
  104.5 26.0 %convolution_bitcast_fusion = f32[48,5,128,128]{3,1,2,0:T(8,128)} fusion(f32[48,3,2,128,128]{4,1,2,3,0:T(4,128)} %copy.76, pred[48,3,2,5,1]{3,1,2,4,0:T(4,128)(4,1)S(1)} %fusion.74), kind=kOutput, calls=%fused_computation.41 | convolution fusion | flops 283115520 | bytes 34604448 | tf_op jit(solution)/shard_map/rkms,rkmac->rsac/dot_general | solution.py:60
  130.6 20.6 %copy.77 = f32[48,5,128,128]{2,3,1,0:T(8,128)} copy(f32[48,5,128,128]{3,1,2,0:T(8,128)} %convolution_bitcast_fusion) | data formatting | bytes 31457280 | tf_op jit(solution)/shard_map/while | solution.py:106
  155.6 233.1 %while.16 = (s32[]{:T(128)}, f32[18,7,128,128]{3,2,1,0:T(8,128)}, s32[4]{0:T(128)S(1)}, s32[48,2]{0,1:T(2,128)S(1)}, s32[48,2,5]{2,1,0:T(2,128)S(1)}, /*index=5*...) while((s32[]{:T(128)}, f32[18,7,128,128]{3,2,1,0:T(8,128)}, ...), condition=%wide.region_1.2_spmd, body=%wide.region_0.1_spmd.sunk | while | flops 3383919616 | bytes 75500464 | solution.py:106
  157.0 10.8 %fusion.91 = f32[12,2,5,128,128]{3,4,1,2,0:T(8,128)} fusion(f32[48,5,128,128]{2,3,1,0:T(8,128)} %get-tuple-element.246, s32[]{:T(128)S(6)} %select_n.469, f32[48,2,128,128]{3,2,1,0:T(8,128)} %get-tuple-element.247), kind=kOutput, calls=%fused_computation.20.clone.1 | convolution fusion | flops 3019898880 | bytes 13370368 | tf_op jit(solution)/shard_map/while/body/eval_jaxpr/imba,isbc->imsac/dot_general | solution.py:97
  167.7 11.0 %copy.121 = f32[12,2,5,128,128]{4,2,3,1,0:T(8,128)} copy(f32[12,2,5,128,128]{3,4,1,2,0:T(8,128)} %fusion.91) | data formatting | bytes 15728640 | tf_op jit(solution)/shard_map/while/body/eval_jaxpr/imba,isbc->imsac/transpose | solution.py:97
  178.7 11.4 %fusion.92 = f32[12,2,7,128,128]{4,2,3,1,0:T(8,128)} fusion(f32[12,2,5,128,128]{4,2,3,1,0:T(8,128)} %copy.121, s32[12,2,5]{2,1,0:T(2,128)S(1)} %constant_dynamic-slice_fusion.8), kind=kOutput, calls=%fused_computation.26.clone.1 | convolution fusion | flops 165151552 | bytes 18874848 | tf_op jit(solution)/shard_map/while/body/eval_jaxpr/imsw,imsac->imwac/dot_general | solution.py:99
  192.9 18.9 %copy_add_fusion.2 = f32[6,7,128,128]{3,0,2,1:T(8,128)S(1)} fusion(f32[6,7,128,128]{3,2,1,0:T(8,128)S(1)} %constant_dynamic-slice_fusion.7, f32[12,2,7,128,128]{4,2,3,1,0:T(8,128)} %fusion.92, s32[12,2]{0,1:T(2,128)S(1)} %fusion.93), kind=kOutput, calls=%fused_computation.19.clone.1 | convolution fusion | flops 198869136 | bytes 16515168 | tf_op jit(solution)/shard_map/while/body/eval_jaxpr/imr,imwac->rwac/dot_general | solution.py:101
  215.1 10.8 %fusion.91 = f32[12,2,5,128,128]{3,4,1,2,0:T(8,128)} fusion(f32[48,5,128,128]{2,3,1,0:T(8,128)} %get-tuple-element.246, s32[]{:T(128)S(6)} %select_n.469, f32[48,2,128,128]{3,2,1,0:T(8,128)} %get-tuple-element.247), kind=kOutput, calls=%fused_computation.20.clone.1 | convolution fusion | flops 3019898880 | bytes 13370368 | tf_op jit(solution)/shard_map/while/body/eval_jaxpr/imba,isbc->imsac/dot_general | solution.py:97
  225.9 11.0 %copy.121 = f32[12,2,5,128,128]{4,2,3,1,0:T(8,128)} copy(f32[12,2,5,128,128]{3,4,1,2,0:T(8,128)} %fusion.91) | data formatting | bytes 15728640 | tf_op jit(solution)/shard_map/while/body/eval_jaxpr/imba,isbc->imsac/transpose | solution.py:97
  236.9 11.4 %fusion.92 = f32[12,2,7,128,128]{4,2,3,1,0:T(8,128)} fusion(f32[12,2,5,128,128]{4,2,3,1,0:T(8,128)} %copy.121, s32[12,2,5]{2,1,0:T(2,128)S(1)} %constant_dynamic-slice_fusion.8), kind=kOutput, calls=%fused_computation.26.clone.1 | convolution fusion | flops 165151552 | bytes 18874848 | tf_op jit(solution)/shard_map/while/body/eval_jaxpr/imsw,imsac->imwac/dot_general | solution.py:99
  251.1 18.9 %copy_add_fusion.2 = f32[6,7,128,128]{3,0,2,1:T(8,128)S(1)} fusion(f32[6,7,128,128]{3,2,1,0:T(8,128)S(1)} %constant_dynamic-slice_fusion.7, f32[12,2,7,128,128]{4,2,3,1,0:T(8,128)} %fusion.92, s32[12,2]{0,1:T(2,128)S(1)} %fusion.93), kind=kOutput, calls=%fused_computation.19.clone.1 | convolution fusion | flops 198869136 | bytes 16515168 | tf_op jit(solution)/shard_map/while/body/eval_jaxpr/imr,imwac->rwac/dot_general | solution.py:101
  273.3 10.8 %fusion.91 = f32[12,2,5,128,128]{3,4,1,2,0:T(8,128)} fusion(f32[48,5,128,128]{2,3,1,0:T(8,128)} %get-tuple-element.246, s32[]{:T(128)S(6)} %select_n.469, f32[48,2,128,128]{3,2,1,0:T(8,128)} %get-tuple-element.247), kind=kOutput, calls=%fused_computation.20.clone.1 | convolution fusion | flops 3019898880 | bytes 13370368 | tf_op jit(solution)/shard_map/while/body/eval_jaxpr/imba,isbc->imsac/dot_general | solution.py:97
  284.0 11.0 %copy.121 = f32[12,2,5,128,128]{4,2,3,1,0:T(8,128)} copy(f32[12,2,5,128,128]{3,4,1,2,0:T(8,128)} %fusion.91) | data formatting | bytes 15728640 | tf_op jit(solution)/shard_map/while/body/eval_jaxpr/imba,isbc->imsac/transpose | solution.py:97
  295.0 11.4 %fusion.92 = f32[12,2,7,128,128]{4,2,3,1,0:T(8,128)} fusion(f32[12,2,5,128,128]{4,2,3,1,0:T(8,128)} %copy.121, s32[12,2,5]{2,1,0:T(2,128)S(1)} %constant_dynamic-slice_fusion.8), kind=kOutput, calls=%fused_computation.26.clone.1 | convolution fusion | flops 165151552 | bytes 18874848 | tf_op jit(solution)/shard_map/while/body/eval_jaxpr/imsw,imsac->imwac/dot_general | solution.py:99
  309.2 18.9 %copy_add_fusion.2 = f32[6,7,128,128]{3,0,2,1:T(8,128)S(1)} fusion(f32[6,7,128,128]{3,2,1,0:T(8,128)S(1)} %constant_dynamic-slice_fusion.7, f32[12,2,7,128,128]{4,2,3,1,0:T(8,128)} %fusion.92, s32[12,2]{0,1:T(2,128)S(1)} %fusion.93), kind=kOutput, calls=%fused_computation.19.clone.1 | convolution fusion | flops 198869136 | bytes 16515168 | tf_op jit(solution)/shard_map/while/body/eval_jaxpr/imr,imwac->rwac/dot_general | solution.py:101
  331.5 10.8 %fusion.91 = f32[12,2,5,128,128]{3,4,1,2,0:T(8,128)} fusion(f32[48,5,128,128]{2,3,1,0:T(8,128)} %get-tuple-element.246, s32[]{:T(128)S(6)} %select_n.469, f32[48,2,128,128]{3,2,1,0:T(8,128)} %get-tuple-element.247), kind=kOutput, calls=%fused_computation.20.clone.1 | convolution fusion | flops 3019898880 | bytes 13370368 | tf_op jit(solution)/shard_map/while/body/eval_jaxpr/imba,isbc->imsac/dot_general | solution.py:97
  342.3 11.0 %copy.121 = f32[12,2,5,128,128]{4,2,3,1,0:T(8,128)} copy(f32[12,2,5,128,128]{3,4,1,2,0:T(8,128)} %fusion.91) | data formatting | bytes 15728640 | tf_op jit(solution)/shard_map/while/body/eval_jaxpr/imba,isbc->imsac/transpose | solution.py:97
  353.3 11.4 %fusion.92 = f32[12,2,7,128,128]{4,2,3,1,0:T(8,128)} fusion(f32[12,2,5,128,128]{4,2,3,1,0:T(8,128)} %copy.121, s32[12,2,5]{2,1,0:T(2,128)S(1)} %constant_dynamic-slice_fusion.8), kind=kOutput, calls=%fused_computation.26.clone.1 | convolution fusion | flops 165151552 | bytes 18874848 | tf_op jit(solution)/shard_map/while/body/eval_jaxpr/imsw,imsac->imwac/dot_general | solution.py:99
  367.5 18.9 %copy_add_fusion.2 = f32[6,7,128,128]{3,0,2,1:T(8,128)S(1)} fusion(f32[6,7,128,128]{3,2,1,0:T(8,128)S(1)} %constant_dynamic-slice_fusion.7, f32[12,2,7,128,128]{4,2,3,1,0:T(8,128)} %fusion.92, s32[12,2]{0,1:T(2,128)S(1)} %fusion.93), kind=kOutput, calls=%fused_computation.19.clone.1 | convolution fusion | flops 198869136 | bytes 16515168 | tf_op jit(solution)/shard_map/while/body/eval_jaxpr/imr,imwac->rwac/dot_general | solution.py:101
  390.0 7.2 collective-permute-start.3
  408.2 7.1 gather_fusion.4
  415.2 7.6 %broadcast_multiply_fusion = f32[4,4,7,128,128]{4,3,2,1,0:T(8,128)} fusion(f32[4,4,7,128,128]{4,3,2,1,0:T(8,128)} %bitcast.141, f32[4,4]{1,0:T(4,128)S(1)} %reshape.834), kind=kLoop, calls=%fused_computation.44 | loop fusion | flops 1835008 | bytes 14680128 | tf_op jit(solution)/shard_map/mul | solution.py:43
  429.0 73.3 %all-to-all-done = f32[4,4,7,128,128]{4,3,2,1,0:T(8,128)} async-done(((f32[4,4,7,128,128]{4,3,2,1,0:T(8,128)}), f32[4,4,7,128,128]{4,3,2,1,0:T(8,128)}, u32[]{:S(2)}, u32[]{:S(2)}) %all-to-all-start) | async-done | bytes 7340064 | tf_op jit(solution)/shard_map/all_to_all | solution.py:121
  502.4 9.8 %gather_fusion.7 = f32[32,7,128,128]{3,2,1,0:T(8,128)} fusion(f32[16,7,128,128]{3,2,1,0:T(8,128)} %bitcast.26, s32[1024]{0:T(1024)S(1)} %pad_clamp_fusion.2), kind=kCustom, calls=%fused_computation.7 | custom fusion | bytes 29360256 | tf_op jit(solution)/shard_map/gather | solution.py:43
  512.1 13.8 %fusion.21 = f32[32,1,7,128,128]{4,3,2,1,0:T(8,128)} fusion(f32[32,7,128,128]{3,2,1,0:T(8,128)} %gather_fusion.7, f32[32]{0:T(128)S(1)} %convert_element_type.45), kind=kLoop, calls=%fused_computation.37 | loop fusion | flops 3670016 | bytes 29360256 | tf_op jit(solution)/shard_map/mul | solution.py:43
  532.6 11.8 %gather_fusion.8 = s32[2048]{0:T(1024)S(1)} fusion(s32[2048]{0:T(1024)S(1)} %copy-done.3, s32[2048]{0:T(1024)S(1)} %broadcast_clamp_fusion), kind=kCustom, calls=%fused_computation.8 | custom fusion | bytes 24576 | tf_op jit(solution)/shard_map/vmap()/gather | solution.py:132
  556.8 162.1 %all-to-all-done.1 = f32[32,1,7,128,128]{4,3,2,1,0:T(8,128)} async-done(((f32[32,1,7,128,128]{4,3,2,1,0:T(8,128)}), f32[32,1,7,128,128]{4,3,2,1,0:T(8,128)}, u32[]{:S(2)}, u32[]{:S(2)}) %all-to-all-start.1) | async-done | bytes 14680096 | tf_op jit(solution)/shard_map/all_to_all | solution.py:144
  719.0 9.2 %gather_fusion.10 = f32[16,7,128,128]{3,2,1,0:T(8,128)} fusion(f32[32,7,128,128]{3,2,1,0:T(8,128)} %bitcast.37, s32[1024]{0:T(1024)S(1)} %pad_clamp_fusion), kind=kCustom, calls=%fused_computation.10 | custom fusion | bytes 14680128 | tf_op jit(solution)/shard_map/gather | solution.py:158
  (175 shorter events, 78.8 us)
Async XLA Ops:
  0.0 12.7 %copy-start = (s32[6144]{0:T(1024)S(1)}, s32[6144]{0:T(1024)}, u32[]{:S(2)}) copy-start(s32[6144]{0:T(1024)} %param.12) | copy-start | bytes 73732
  1.0 19.1 %collective-permute-start = (f32[1,2,128,128]{3,2,1,0:T(8,128)S(1)}, f32[1,2,128,128]{3,2,1,0:T(8,128)S(1)}, u32[]{:S(2)}, u32[]{:S(2)}) collective-permute-start(f32[1,2,128,128]{3,2,1,0:T(8,128)S(1)} %get-tuple-element.162), channel_id=1, source_target_pairs={{0,1},{1,2},{2,3},{3,4},{4,5},{5,6},{6,7},{7,8},{8,9},{9,10},{10,1... | collective-permute-start | bytes 393224 | tf_op jit(solution)/shard_map/ppermute | solution.py:22
  1.1 19.0 %collective-permute-start.1 = (f32[1,2,128,128]{3,2,1,0:T(8,128)S(1)}, f32[1,2,128,128]{3,2,1,0:T(8,128)S(1)}, u32[]{:S(2)}, u32[]{:S(2)}) collective-permute-start(f32[1,2,128,128]{3,2,1,0:T(8,128)S(1)} %get-tuple-element.163), channel_id=1, source_target_pairs={{1,0},{2,1},{3,2},{4,3},{5,4},{6,5},{7,6},{8,7},{9,8},{10,9},{11,1... | collective-permute-start | bytes 393224 | tf_op jit(solution)/shard_map/ppermute | solution.py:23
  9.4 3.1 copy-start.4
  12.7 1.8 copy-start.11
  12.7 4.1 copy-start.2
  15.7 4.1 copy-start.6
  16.0 3.8 copy-start.9
  155.6 241.6 %copy-start.12 = (s32[16]{0:T(128)S(1)}, s32[16]{0:T(128)}, u32[]{:S(2)}) copy-start(s32[16]{0:T(128)} %multiply_add_fusion.2) | copy-start | bytes 196
  389.9 13.4 %collective-permute-start.2 = (f32[1,7,128,128]{3,2,1,0:T(8,128)S(1)}, f32[1,7,128,128]{3,2,1,0:T(8,128)S(1)}, u32[]{:S(2)}, u32[]{:S(2)}) collective-permute-start(f32[1,7,128,128]{3,2,1,0:T(8,128)S(1)} %get-tuple-element.160), channel_id=1, source_target_pairs={{0,1},{1,2},{2,3},{3,4},{4,5},{5,6},{6,7},{7,8},{8,9},{9,10},{10,1... | collective-permute-start | bytes 1376264 | tf_op jit(solution)/shard_map/ppermute | solution.py:22
  390.0 13.3 %collective-permute-start.3 = (f32[1,7,128,128]{3,2,1,0:T(8,128)S(1)}, f32[1,7,128,128]{3,2,1,0:T(8,128)S(1)}, u32[]{:S(2)}, u32[]{:S(2)}) collective-permute-start(f32[1,7,128,128]{3,2,1,0:T(8,128)S(1)} %get-tuple-element.161), channel_id=1, source_target_pairs={{1,0},{2,1},{3,2},{4,3},{5,4},{6,5},{7,6},{8,7},{9,8},{10,9},{11,1... | collective-permute-start | bytes 1376264 | tf_op jit(solution)/shard_map/ppermute | solution.py:23
  422.9 5.6 copy-start.10
  422.9 5.7 copy-start.8
  422.9 79.5 %all-to-all-start = ((f32[4,4,7,128,128]{4,3,2,1,0:T(8,128)}), f32[4,4,7,128,128]{4,3,2,1,0:T(8,128)}, u32[]{:S(2)}, u32[]{:S(2)}) async-start(f32[4,4,7,128,128]{4,3,2,1,0:T(8,128)} %broadcast_multiply_fusion), calls=%async_computation | async-start | bytes 14680064 | tf_op jit(solution)/shard_map/all_to_all | solution.py:121
  525.9 6.7 copy-start.3
  525.9 193.0 %all-to-all-start.1 = ((f32[32,1,7,128,128]{4,3,2,1,0:T(8,128)}), f32[32,1,7,128,128]{4,3,2,1,0:T(8,128)}, u32[]{:S(2)}, u32[]{:S(2)}) async-start(f32[32,1,7,128,128]{4,3,2,1,0:T(8,128)} %fusion.21), calls=%async_computation.1 | async-start | bytes 29360128 | tf_op jit(solution)/shard_map/all_to_all | solution.py:144
  532.6 12.0 %copy-start.5 = (pred[16,16]{1,0:T(8,128)(4,1)S(1)}, pred[16,16]{1,0:T(8,128)(4,1)}, u32[]{:S(2)}) copy-start(pred[16,16]{1,0:T(8,128)(4,1)} %copy-done.4) | copy-start | bytes 772
  532.6 12.4 %copy-start.7 = (s32[1,2]{1,0:T(1,128)S(1)}, s32[1,2]{1,0:T(1,128)}, u32[]{:S(2)}) copy-start(s32[1,2]{1,0:T(1,128)} %copy-done.6) | copy-start | bytes 28
  551.2 177.0 %copy-start.1 = (s32[6144]{0:T(1024)S(1)}, s32[6144]{0:T(1024)}, u32[]{:S(2)}) copy-start(s32[6144]{0:T(1024)} %param.12) | copy-start | bytes 73732
where the time goes:
time: 736 us; the launch traced here: 728 us
  waiting for transfers between devices  238 us (32%)
  matrix products  229 us (31%)
  local copies, waits for them, and re-layouts  188 us (26%)
  other arithmetic  39 us (5%)
  starting transfers between devices  27.6 us (4%)
    all_to_all x1, waiting for transfers between devices, shards(): lax.all_to_all(pack_rows(mid_rows, anchor, filled), 'gy', split_axis=0, c...  162 us
    dot_general x4, matrix products, accumulate(): added = jnp.einsum('imr,imwac->rwac', row_hot, placed, precision=highest)  75.7 us
    all_to_all x1, waiting for transfers between devices, shards(): lax.all_to_all(pack_rows(complete, anchor, filled), 'gx', split_axis=0, c...  73.3 us
    dot_general x4, matrix products, accumulate(): placed = jnp.einsum('imsw,imsac->imwac', col_hot, paired, precision=highest)  45.6 us
    transpose x4, local copies, waits for them, and re-layouts, accumulate(): jnp.einsum('imba,isbc->imsac', p_block, ap_block, precision=highest)  43.9 us
    dot_general x4, matrix products, accumulate(): jnp.einsum('imba,isbc->imsac', p_block, ap_block, precision=highest)  43.1 us
    dot_general x1, matrix products, product_rows(): pieces = jnp.einsum('rkab,rkmbc->rkmac', a_rows, chosen, precision=highest)  38.9 us
    dot_general x1, matrix products, product_rows(): return jnp.einsum('rkms,rkmac->rsac', hot_rows, pieces, precision=highest)  26 us
  transfers between devices with their start and end apart: 6, of which 3 were waited for; matrix products, arithmetic and copies ran while one was open for 5% of the time, Pallas kernels for 0%

commit v1 on v0

v1 whole, which is shorter than its diff:
```python
import functools

import jax
import jax.numpy as jnp
from jax import lax
from jax.experimental import pallas as pl
from jax.experimental.pallas import tpu as pltpu
from jax.sharding import PartitionSpec as P

B = 128
KP = 2
CWIN = 7
W = 6
HALF = B // 2
BF = jnp.bfloat16
F32 = jnp.float32
SMEM = pltpu.SMEM
VMEM = pltpu.VMEM


def split(x):
    high = x.astype(BF)
    return high, (x - high.astype(F32)).astype(BF)


def left_operand(x):
    high, low = split(x)
    return jnp.concatenate([high, low, high], axis=1)


def right_operand(x):
    high, low = split(x)
    return jnp.concatenate([high, high, low], axis=0)


def matmul(left, right):
    return jnp.dot(left, right, preferred_element_type=F32)


def spread(total, flag, base, pair, slots):
    first, second = pair
    values = {
        base - 1: jnp.where(flag, first, 0.0),
        base: jnp.where(flag, second, first),
        base + 1: jnp.where(flag, 0.0, second),
    }
    for s, value in values.items():
        if s in slots:
            total[s] = value if total.get(s) is None else total[s] + value


def row_product(p_pair, tiles):
    turned = jnp.concatenate([p_pair[0].T, p_pair[1].T], axis=0)
    return matmul(left_operand(turned), right_operand(jnp.concatenate(tiles, axis=1)))


SLOTS = {0: (0, 1, 2, 3), 1: (1, 2, 3), 2: (1, 2, 3, 4)}


def main_kernel(
    flag_ref, left_ref, right_ref, lon_ref, ron_ref, slot_a, slot_b,
    a_ref, p_ref, before_ref, after_ref,
    out_a, out_b,
    stage, carry, sems,
):
    step = pl.program_id(0)
    steps = pl.num_programs(0) - 1
    buf = lax.rem(step, 2)

    def copies(at, which, row):
        c = 2 * at - 1 + row
        return (
            pltpu.make_async_copy(
                stage.at[which, row, :, pl.ds(0, HALF)], out_a.at[slot_a[c]], sems.at[which, row, 0]
            ),
            pltpu.make_async_copy(
                stage.at[which, row, :, pl.ds(HALF, HALF)], out_b.at[slot_b[c]], sems.at[which, row, 1]
            ),
        )

    def drain(at):
        which = lax.rem(at, 2)
        for row in range(2):
            @pl.when((2 * at - 1 + row >= 0) & (2 * at - 1 + row < 2 * steps))
            def _():
                for copy in copies(at, which, row):
                    copy.wait()

    @pl.when(step >= 2)
    def _():
        drain(step - 2)

    @pl.when(step == 0)
    def _():
        carry[...] = jnp.zeros_like(carry)

    stage[buf, 0] = carry[0]
    stage[buf, 1] = carry[1]

    @pl.when(step < steps)
    def _():
        carry[...] = jnp.zeros_like(carry)
        first = step * W
        flags = {q: flag_ref[first + q + 1] > 0 for q in range(-1, W + 1)}

        def p_tile(q, m):
            if q < 0:
                return before_ref[0, m]
            if q >= W:
                return after_ref[0, m]
            return p_ref[q, m]

        lefts = {}
        for r in range(W):
            tiles = {
                0: jnp.where(lon_ref[first + r] > 0, a_ref[r, left_ref[first + r]], 0.0),
                1: a_ref[r, 0],
                2: jnp.where(ron_ref[first + r] > 0, a_ref[r, right_ref[first + r]], 0.0),
            }
            for k in range(3):
                lefts[r, r + k - 1] = left_operand(tiles[k])
        total = {r: {} for r in range(W)}
        for q in range(-1, W + 1):
            rows = [r for r in (q - 1, q, q + 1) if 0 <= r < W]
            right = right_operand(jnp.concatenate([p_tile(q, 0), p_tile(q, 1)], axis=1))
            product = matmul(jnp.concatenate([lefts[r, q] for r in rows], axis=0), right)
            for n, r in enumerate(rows):
                pair = (product[n * B : (n + 1) * B, :B], product[n * B : (n + 1) * B, B:])
                spread(total[r], flags[q], q // 3 - r // 3 + 2, pair, SLOTS[r % 3])
        for r in range(W):
            slots = SLOTS[r % 3]
            product = row_product((p_ref[r, 0], p_ref[r, 1]), [total[r][s] for s in slots])
            g = r // 3
            for n, s in enumerate(slots):
                one = product[:B, n * B : (n + 1) * B]
                two = product[B:, n * B : (n + 1) * B]
                for delta, value in (
                    (-1, jnp.where(flags[r], one, 0.0)),
                    (0, jnp.where(flags[r], two, one)),
                    (1, jnp.where(flags[r], 0.0, two)),
                ):
                    place = g + delta + 1
                    if place < 2:
                        stage[buf, place, s + 1 - delta] += value
                    else:
                        carry[place - 2, s + 1 - delta] += value

    for row in range(2):
        @pl.when((2 * step - 1 + row >= 0) & (2 * step - 1 + row < 2 * steps))
        def _():
            for copy in copies(step, buf, row):
                copy.start()

    @pl.when(step == steps)
    def _():
        drain(step - 1)
        drain(step)


def main_product(meta, slot_a, slot_b, a_tiles, p_tiles, count_b):
    rows = a_tiles.shape[0]
    steps = rows // W
    coarse = rows // 3
    last = steps - 1

    def spec(shape, index):
        return pl.BlockSpec(shape, index)

    half = (CWIN, HALF, B)
    return pl.pallas_call(
        main_kernel,
        grid_spec=pltpu.PrefetchScalarGridSpec(
            num_scalar_prefetch=7,
            grid=(steps + 1,),
            in_specs=[
                spec((W, 3, B, B), lambda s, *_: (jnp.minimum(s, last), 0, 0, 0)),
                spec((W, KP, B, B), lambda s, *_: (jnp.minimum(s, last), 0, 0, 0)),
                spec((1, KP, B, B), lambda s, *_: (jnp.maximum(jnp.minimum(s, last) * W - 1, 0), 0, 0, 0)),
                spec((1, KP, B, B), lambda s, *_: (jnp.minimum(s * W + W, rows - 1), 0, 0, 0)),
            ],
            out_specs=[pl.BlockSpec(memory_space=pl.ANY)] * 2,
            scratch_shapes=[
                VMEM((2, 2, CWIN, B, B), F32),
                VMEM((2, CWIN, B, B), F32),
                pltpu.SemaphoreType.DMA((2, 2, 2)),
            ],
        ),
        out_shape=[
            jax.ShapeDtypeStruct((coarse,) + half, F32),
            jax.ShapeDtypeStruct((count_b,) + half, F32),
        ],
        compiler_params=pltpu.CompilerParams(
            dimension_semantics=("arbitrary",), vmem_limit_bytes=56 << 20
        ),
        cost_estimate=pl.CostEstimate(
            flops=16_000_000_000, bytes_accessed=24_000_000, transcendentals=0
        ),
        name="triple_product",
    )(*meta, slot_a, slot_b, a_tiles, p_tiles, p_tiles, p_tiles)


def edge_kernel(
    flag_ref, slot_a, slot_b,
    a_before, a_after, p_before, p_after, a_edge, p_first, p_last, in_a, in_b,
    out_a, out_b,
    rows_ref, sems,
):
    coarse = slot_a.shape[0]
    held = (0, 1, coarse - 2, coarse - 1)

    def copies(n, back):
        c = held[n]
        pairs = (
            (out_a.at[slot_a[c]], rows_ref.at[n, :, pl.ds(0, HALF)], sems.at[n, 0]),
            (out_b.at[slot_b[c]], rows_ref.at[n, :, pl.ds(HALF, HALF)], sems.at[n, 1]),
        )
        return [
            pltpu.make_async_copy(here, there, sem) if back else pltpu.make_async_copy(there, here, sem)
            for there, here, sem in pairs
        ]

    for n in range(4):
        for copy in copies(n, False):
            copy.start()

    sums = []
    for side in range(2):
        a_ref, p_ref = ((a_before, p_before), (a_after, p_after))[side]
        own_p = (p_first, p_last)[side]
        own_flag = flag_ref[(4, 5)[side]] > 0
        flags, tiles, p_at = {}, {}, {}
        for n in range(4):
            q = n - 1 if side == 0 else n
            flags[q] = flag_ref[(0, 6)[side] + n] > 0
            p_at[q] = (p_ref[n, 0], p_ref[n, 1])
        near = 3 if side == 0 else -1
        flags[near] = own_flag
        p_at[near] = (own_p[0, 0], own_p[0, 1])
        total = {r: {} for r in range(3)}
        total[near] = {}
        for q in range(-1, 4):
            rows = [r for r in (q - 1, q, q + 1) if 0 <= r < 3]
            lefts = [left_operand(a_ref[r, q - r + 1]) for r in rows]
            if q == (2 if side == 0 else 0):
                rows.append(near)
                lefts.append(left_operand(a_edge[side]))
            right = right_operand(jnp.concatenate(p_at[q], axis=1))
            product = matmul(jnp.concatenate(lefts, axis=0), right)
            for n, r in enumerate(rows):
                pair = (product[n * B : (n + 1) * B, :B], product[n * B : (n + 1) * B, B:])
                base = q // 3 - r // 3 + 2
                slots = SLOTS[r % 3] if r != near else (base - 1, base, base + 1)
                spread(total[r], flags[q], base, pair, slots)
        outer, inner = {}, {}

        def put(target, w, value):
            target[w] = value if w not in target else target[w] + value

        for r in range(3):
            slots = sorted(total[r])
            pick = 1 if side == 0 else 0
            turned = left_operand(p_at[r][pick].T)
            product = matmul(turned, right_operand(jnp.concatenate([total[r][s] for s in slots], axis=1)))
            for n, s in enumerate(slots):
                value = product[:, n * B : (n + 1) * B]
                if side == 0:
                    put(outer, s, jnp.where(flags[r], 0.0, value))
                else:
                    put(outer, s + 2, jnp.where(flags[r], value, 0.0))
        slots = sorted(total[near])
        product = row_product(p_at[near], [total[near][s] for s in slots])
        for n, s in enumerate(slots):
            one = product[:B, n * B : (n + 1) * B]
            two = product[B:, n * B : (n + 1) * B]
            put(outer, s + 1, jnp.where(own_flag, two, one))
            if side == 0:
                put(inner, s, jnp.where(own_flag, 0.0, two))
            else:
                put(inner, s + 2, jnp.where(own_flag, one, 0.0))
        sums.append((outer, inner))

    for n in range(4):
        for copy in copies(n, False):
            copy.wait()
    for n, target in ((0, sums[0][0]), (1, sums[0][1]), (2, sums[1][1]), (3, sums[1][0])):
        for w, value in target.items():
            rows_ref[n, w] += value
    for n in range(4):
        for copy in copies(n, True):
            copy.start()
    for n in range(4):
        for copy in copies(n, True):
            copy.wait()


def edge_product(flags, slot_a, slot_b, a_before, a_after, p_before, p_after, a_edge, p_tiles, out_a, out_b):
    rows = p_tiles.shape[0]

    def whole(x):
        return pl.BlockSpec(x.shape, lambda *_: (0,) * x.ndim)

    anywhere = pl.BlockSpec(memory_space=pl.ANY)
    return pl.pallas_call(
        edge_kernel,
        grid_spec=pltpu.PrefetchScalarGridSpec(
            num_scalar_prefetch=3,
            grid=(1,),
            in_specs=[whole(x) for x in (a_before, a_after, p_before, p_after, a_edge)]
            + [
                pl.BlockSpec((1, KP, B, B), lambda *_: (0, 0, 0, 0)),
                pl.BlockSpec((1, KP, B, B), lambda *_: (rows - 1, 0, 0, 0)),
                anywhere,
                anywhere,
            ],
            out_specs=[anywhere, anywhere],
            scratch_shapes=[VMEM((4, CWIN, B, B), F32), pltpu.SemaphoreType.DMA((4, 2))],
        ),
        out_shape=[jax.ShapeDtypeStruct(x.shape, x.dtype) for x in (out_a, out_b)],
        input_output_aliases={10: 0, 11: 1},
        compiler_params=pltpu.CompilerParams(
            dimension_semantics=("arbitrary",), vmem_limit_bytes=56 << 20
        ),
        cost_estimate=pl.CostEstimate(flops=2_000_000_000, bytes_accessed=10_000_000, transcendentals=0),
        name="edge_rows",
    )(flags, slot_a, slot_b, a_before, a_after, p_before, p_after, a_edge, p_tiles, p_tiles, out_a, out_b)


def relay(pairs, sems_in, sems_out):
    inward = [pltpu.make_async_copy(x, y, sems_in.at[k]) for k, (x, y, z) in enumerate(pairs)]
    outward = [pltpu.make_async_copy(y, z, sems_out.at[k]) for k, (x, y, z) in enumerate(pairs)]
    for copy in inward:
        copy.start()
    for come, go in zip(inward, outward):
        come.wait()
        go.start()
    for copy in outward:
        copy.wait()


def move_kernel(source_ref, target_ref, rows_in, rows_out, stage, sems_in, sems_out):
    relay(
        [(rows_in.at[source_ref[k]], stage.at[k], rows_out.at[target_ref[k]]) for k in range(stage.shape[0])],
        sems_in,
        sems_out,
    )


def move_rows(source, target, rows, places):
    count = source.shape[0]
    anywhere = pl.BlockSpec(memory_space=pl.ANY)
    return pl.pallas_call(
        move_kernel,
        grid_spec=pltpu.PrefetchScalarGridSpec(
            num_scalar_prefetch=2,
            grid=(1,),
            in_specs=[anywhere],
            out_specs=anywhere,
            scratch_shapes=[
                VMEM((count,) + rows.shape[1:], F32),
                pltpu.SemaphoreType.DMA((count,)),
                pltpu.SemaphoreType.DMA((count,)),
            ],
        ),
        out_shape=jax.ShapeDtypeStruct((places,) + rows.shape[1:], F32),
        compiler_params=pltpu.CompilerParams(vmem_limit_bytes=56 << 20),
        cost_estimate=pl.CostEstimate(flops=0, bytes_accessed=8_000_000, transcendentals=0),
        name="move_rows",
    )(source, target, rows)


def join_kernel(source_a, source_b, rows_a, rows_b, out, stage, sems_in, sems_out):
    pairs = []
    for k in range(stage.shape[0]):
        for rows, source, first in ((rows_a, source_a, 0), (rows_b, source_b, HALF)):
            part = pl.ds(first, HALF)
            pairs.append((rows.at[source[k]], stage.at[k, :, part], out.at[k, :, part]))
    relay(pairs, sems_in, sems_out)


def join_rows(source_a, source_b, rows_a, rows_b):
    count = source_a.shape[0]
    anywhere = pl.BlockSpec(memory_space=pl.ANY)
    return pl.pallas_call(
        join_kernel,
        grid_spec=pltpu.PrefetchScalarGridSpec(
            num_scalar_prefetch=2,
            grid=(1,),
            in_specs=[anywhere, anywhere],
            out_specs=anywhere,
            scratch_shapes=[
                VMEM((count, CWIN, B, B), F32),
                pltpu.SemaphoreType.DMA((2 * count,)),
                pltpu.SemaphoreType.DMA((2 * count,)),
            ],
        ),
        out_shape=jax.ShapeDtypeStruct((count, CWIN, B, B), F32),
        compiler_params=pltpu.CompilerParams(vmem_limit_bytes=56 << 20),
        cost_estimate=pl.CostEstimate(flops=0, bytes_accessed=16_000_000, transcendentals=0),
        name="join_rows",
    )(source_a, source_b, rows_a, rows_b)


def shards(a_tiles, a_cols, a_len, p_tiles, aggregate, owner):
    count_x = lax.axis_size("gx")
    count_y = lax.axis_size("gy")
    index_x = lax.axis_index("gx")
    index_y = lax.axis_index("gy")
    device = index_x * count_y + index_y
    fine = a_tiles.shape[0]
    coarse = fine // 3
    fine_total = fine * count_x * count_y
    devices = count_x * count_y
    first_row = device * fine

    rows = jnp.arange(fine)
    here = first_row + rows
    second = a_cols[:, 1] == (here + fine_total - 1) % fine_total
    left_at = jnp.where(second, 1, 2).astype(jnp.int32)
    right_at = 3 - left_at
    left_on = (a_len > left_at).astype(jnp.int32)
    right_on = (a_len > right_at).astype(jnp.int32)
    wrapped = jnp.concatenate([aggregate[-4:], aggregate, aggregate[:4]])
    window = lax.dynamic_slice_in_dim(wrapped, first_row, fine + 8)
    around = (first_row - 4 + jnp.arange(fine + 8)) % fine_total
    flags = (window != around // 3).astype(jnp.int32)

    def normal(at):
        part = a_tiles[at : at + 3]
        chosen = jnp.stack([left_at[at : at + 3], jnp.zeros(3, jnp.int32), right_at[at : at + 3]], axis=1)
        on = jnp.stack([left_on[at : at + 3], jnp.ones(3, jnp.int32), right_on[at : at + 3]], axis=1)
        tiles = jnp.where(
            (chosen == 1)[:, :, None, None],
            part[:, 1:2],
            jnp.where((chosen == 2)[:, :, None, None], part[:, 2:3], part[:, :1]),
        )
        return jnp.where((on > 0)[:, :, None, None], tiles, 0.0)

    a_first, a_last = normal(0), normal(fine - 3)
    a_edge = jnp.stack([a_first[0, 0], a_last[2, 2]])
    up = [(i, (i + 1) % devices) for i in range(devices)]
    down = [(j, i) for i, j in up]
    axes = ("gx", "gy")
    a_before = lax.ppermute(a_last, axes, up)
    p_before = lax.ppermute(p_tiles[fine - 4 :], axes, up)
    a_after = lax.ppermute(a_first, axes, down)
    p_after = lax.ppermute(p_tiles[:4], axes, down)

    table = owner.reshape(devices, coarse)
    order = jnp.arange(coarse)
    shift = table[0] // count_y
    same = shift[None, :] == shift[:, None]
    rank = jnp.sum((same & (order[None, :] < order[:, None])).astype(jnp.int32), axis=1)
    depth = coarse // count_x
    mine = lax.dynamic_slice_in_dim(table, device, 1)[0]
    slot_a = (shift * depth + rank).astype(jnp.int32)
    slot_b = (mine % count_y).astype(jnp.int32)
    from_x = (index_x - shift) % count_x
    column = table.reshape(count_x, count_y, coarse)[:, index_y]
    mid_a_target = jnp.sum(
        jnp.where(jnp.arange(count_x)[:, None] == from_x[None, :], column % count_y, 0), axis=0
    ).astype(jnp.int32)
    mid_a_source = (shift * depth + rank).astype(jnp.int32)
    slab = lax.dynamic_slice_in_dim(table.reshape(count_x, count_y, coarse), index_x, 1)[0]
    hit = (slab % count_y) == index_y
    mid_b_source = jnp.sum(jnp.where(hit, jnp.arange(count_y)[:, None], 0), axis=0).astype(jnp.int32)
    mid_b_target = (shift * depth + rank).astype(jnp.int32)
    found = table == device
    sender = jnp.sum(jnp.where(found, jnp.arange(devices)[:, None], 0), axis=0)
    ids = sender * coarse + order
    place = jnp.sum((ids[None, :] < ids[:, None]).astype(jnp.int32), axis=1)
    at = place[None, :] == order[:, None]
    last_a = jnp.sum(jnp.where(at, (sender % count_y)[None, :], 0), axis=1).astype(jnp.int32)
    last_b = jnp.sum(
        jnp.where(at, (shift * depth + rank)[None, :], 0), axis=1
    ).astype(jnp.int32)

    outer_left = left_on * (rows > 0)
    outer_right = right_on * (rows < fine - 1)
    meta = (flags[3 : fine + 5], left_at, right_at, outer_left, outer_right)
    rows_a, rows_b = main_product(meta, slot_a, slot_b, a_tiles, p_tiles, count_y)
    edge_flags = jnp.concatenate([flags[0:5], flags[fine + 3 : fine + 8]])
    rows_a, rows_b = edge_product(
        edge_flags, slot_a, slot_b, a_before, a_after, p_before, p_after, a_edge, p_tiles, rows_a, rows_b
    )

    def over(x, axis):
        return lax.all_to_all(x, axis, split_axis=0, concat_axis=0, tiled=True)

    def along_x(x):
        parts = [x[:depth]]
        for k in range(1, count_x):
            pairs = [(i, (i + k) % count_x) for i in range(count_x)]
            parts.append(lax.ppermute(x[k * depth : (k + 1) * depth], "gx", pairs))
        return jnp.concatenate(parts, axis=0)

    got_b = over(rows_b, "gy")
    got_a = along_x(rows_a)
    next_a = move_rows(mid_a_source, mid_a_target, got_a, count_y)
    next_b = move_rows(mid_b_source, mid_b_target, got_b, coarse)
    end_a = over(next_a, "gy")
    end_b = along_x(next_b)
    return join_rows(last_a, last_b, end_a, end_b)


def solution(mesh):
    in_specs = (
        P(("gx", "gy"), None, None, None),
        P(("gx", "gy"), None),
        P(("gx", "gy")),
        P(("gx", "gy"), None, None, None),
        P(),
        P(),
    )
    out_specs = P(("gx", "gy"), None, None, None)
    return jax.shard_map(shards, mesh=mesh, in_specs=in_specs, out_specs=out_specs, check_vma=False)
```

time: 736 us -> 255 us (0.35)
  matrix products: 229 us -> 0 us
  local copies, waits for them, and re-layouts: 188 us -> 13.2 us
  waiting for transfers between devices: 238 us -> 157 us
  Pallas kernels: 0 us -> 40.5 us
  other arithmetic: 39 us -> 13.2 us
    dot_general x14 -> x0, matrix products: 229 us -> none  [the longest x4 75.7 us: accumulate(): added = jnp.einsum('imr,imwac->rwac', row_hot, placed, precision=highest)]
    all_to_all x2, waiting for transfers between devices: 235 us -> 75.6 us  [over(): return lax.all_to_all(x, axis, split_axis=0, concat_axis=0, tiled=True)]
    ppermute x4 -> x10, waiting for transfers between devices: 2.55 us -> 81.8 us  [the longest x6 81.7 us: along_x(): parts.append(lax.ppermute(x[k * depth:(k + 1) * depth], 'gx', pairs))]
    transpose x5 -> x0, local copies, waits for them, and re-layouts: 69.5 us -> none  [the longest x4 43.9 us: accumulate(): jnp.einsum('imba,isbc->imsac', p_block, ap_block, precision=highest)]
    gather x25 -> x0, local copies, waits for them, and re-layouts: 67.1 us -> none  [the longest x2 16.8 us: pack_rows(): rows[anchor.reshape(-1)]]
    pallas_call x0 -> x5, Pallas kernels: none -> 40.5 us  [the longest x1 18.2 us: main_product(): pl.pallas_call(main_kernel, grid_spec=pltpu.PrefetchScalarGridSpec(num_sc...]
    while x1 -> x0, local copies, waits for them, and re-layouts: 20.6 us -> none  [shards(): lax.scan(accumulate, start_value, jnp.arange(fine_rows // 12))]
    mul x5 -> x2, other arithmetic: 21.5 us -> 2.43 us  [the longest x1 1.29 us: shards(): outer_right = right_on * (rows < fine - 1)]
  transfers between devices with their start and end apart: 6 -> 12, of which waited for: 3 -> 8; matrix products, arithmetic and copies ran while one was open for 5% -> 9% of each run, Pallas kernels for 0% -> 11%
where the time goes in v1:
time: 255 us; the launch traced here: 254 us
  waiting for transfers between devices  157 us (62%)
  Pallas kernels  40.5 us (16%)
  starting transfers between devices  29.5 us (12%)
  local copies, waits for them, and re-layouts  13.2 us (5%)
  other arithmetic  13.2 us (5%)
    ppermute x6, waiting for transfers between devices, along_x(): parts.append(lax.ppermute(x[k * depth:(k + 1) * depth], 'gx', pairs))  81.7 us
    all_to_all x2, waiting for transfers between devices, over(): return lax.all_to_all(x, axis, split_axis=0, concat_axis=0, tiled=True)  75.6 us
    pallas_call x1, Pallas kernels, main_product(): pl.pallas_call(main_kernel, grid_spec=pltpu.PrefetchScalarGridSpec(num_sc...  18.2 us
    all_to_all x2, starting transfers between devices, over(): return lax.all_to_all(x, axis, split_axis=0, concat_axis=0, tiled=True)  9.88 us
    pallas_call x2, Pallas kernels, move_rows(): pl.pallas_call(move_kernel, grid_spec=pltpu.PrefetchScalarGridSpec(num_sc...  8.92 us
    ppermute x1, starting transfers between devices, shards(): p_after = lax.ppermute(p_tiles[:4], axes, down)  8.21 us
    ppermute x1, starting transfers between devices, shards(): a_after = lax.ppermute(a_first, axes, down)  7.24 us
    pallas_call x1, Pallas kernels, join_rows(): pl.pallas_call(join_kernel, grid_spec=pltpu.PrefetchScalarGridSpec(num_sc...  7.2 us
  transfers between devices with their start and end apart: 12, of which 8 were waited for; matrix products, arithmetic and copies ran while one was open for 9% of the time, Pallas kernels for 11%

profile of v1, /device:TPU:0, one launch (start us, length us, event | category | flops | bytes accessed | tf_op | source)
XLA Modules:
  0.0 253.9 jit_solution(2009373219577171822)
XLA Ops:
  0.0 2.3 fusion.14
  2.3 8.2 %collective-permute-start.3 = (f32[4,2,128,128]{3,2,1,0:T(8,128)}, f32[4,2,128,128]{3,2,1,0:T(8,128)S(1)}, u32[]{:S(2)}, u32[]{:S(2)}) collective-permute-start(f32[4,2,128,128]{3,2,1,0:T(8,128)} %get-tuple-element.28), channel_id=1, source_target_pairs={{1,0},{2,1},{3,2},{4,3},{5,4},{6,5},{7,6},{8,7},{9,8},{10,9},{11,1... | collective-permute-start | bytes 1572872 | tf_op jit(solution)/shard_map/ppermute | solution.py:446
  10.7 1.3 compare_select_fusion.6
  11.9 1.1 compare_select_fusion.7
  13.7 1.4 slice_bitcast_fusion.2
  16.0 7.2 %collective-permute-start.1 = (f32[3,3,128,128]{3,2,1,0:T(8,128)S(1)}, f32[3,3,128,128]{3,2,1,0:T(8,128)S(1)}, u32[]{:S(2)}, u32[]{:S(2)}) collective-permute-start(f32[3,3,128,128]{3,2,1,0:T(8,128)S(1)} %select_select_fusion), channel_id=1, source_target_pairs={{1,0},{2,1},{3,2},{4,3},{5,4},{6,5},{7,6},{8,7},{9,8},{10,9},{11,1... | collective-permute-start | bytes 1769480 | tf_op jit(solution)/shard_map/ppermute | solution.py:445
  23.5 0.6 slice.132.flag_ref
  25.1 18.2 %triple_product.1 = (f32[16,7,64,128]{3,2,1,0:T(8,128)}, f32[32,7,64,128]{3,2,1,0:T(8,128)}) custom-call(s32[50]{0:T(128)} %slice.132.flag_ref, s32[48]{0:T(128)} %copy-done.7, s32[48]{0:T(128)} %copy-done.8, s32[48]{0:T(128)} %get-tuple-element.18.lon_ref, s32[48]{0:T(128)} %get-tuple-element.15.ron_ref, s32[16]{0:T(128)} %get-tuple-element.66.slot_a.source_ref.target_ref, ...), custom_call_target="tpu_custom_call" | custom-call | flops 16000000000 | bytes 24000000 | tf_op jit(solution)/shard_map/triple_product/pallas_call | solution.py:170
  43.3 0.6 pad_add_fusion.2.flag_ref
  44.0 0.7 pad_maximum_fusion.2.a_edge
  44.7 0.7 copy-done.2
  46.0 6.2 %edge_rows.1 = (f32[16,7,64,128]{3,2,1,0:T(8,128)}, f32[32,7,64,128]{3,2,1,0:T(8,128)}) custom-call(s32[10]{0:T(128)} %pad_add_fusion.2.flag_ref, s32[16]{0:T(128)} %get-tuple-element.66.slot_a.source_ref.target_ref, s32[16]{0:T(128)} %get-tuple-element.65.slot_b, f32[3,3,128,128]{3,2,1,0:T(8,128)} %copy-done, ...), custom_call_target="tpu_custom_call", output_to_operand_aliasing={{0}: (10, {}), {1}: (11, {})} | custom-call | flops 2000000000 | bytes 10000000 | tf_op jit(solution)/shard_map/edge_rows/pallas_call | solution.py:303
  52.2 4.9 %all-to-all-start.1 = ((f32[32,7,64,128]{3,2,1,0:T(8,128)}), f32[32,7,64,128]{3,2,1,0:T(8,128)}, u32[]{:S(2)}, u32[]{:S(2)}) async-start(f32[32,7,64,128]{3,2,1,0:T(8,128)} %get-tuple-element.12), calls=%async_computation.1 | async-start | bytes 14680064 | tf_op jit(solution)/shard_map/all_to_all | solution.py:487
  57.2 3.7 %fusion.16 = (f32[4,7,64,128]{3,2,1,0:T(8,128)S(1)}, f32[4,7,64,128]{3,2,1,0:T(8,128)}, f32[4,7,64,128]{3,2,1,0:T(8,128)}, f32[4,7,64,128]{3,2,1,0:T(8,128)S(1)}) fusion(f32[16,7,64,128]{3,2,1,0:T(8,128)} %get-tuple-element.11), kind=kLoop, calls=%fused_computation.84 | loop fusion | bytes 7340032 | tf_op jit(solution)/shard_map/slice | solution.py:490
  61.0 1.9 collective-permute-start.4
  63.6 20.7 %collective-permute-done.6 = f32[4,7,64,128]{3,2,1,0:T(8,128)S(1)} collective-permute-done((f32[4,7,64,128]{3,2,1,0:T(8,128)}, f32[4,7,64,128]{3,2,1,0:T(8,128)S(1)}, u32[]{:S(2)}, u32[]{:S(2)}) %collective-permute-start.6) | collective-permute-done | bytes 917536 | tf_op jit(solution)/shard_map/ppermute | solution.py:493
  84.3 1.7 collective-permute-done.5
  85.9 18.8 %collective-permute-done.4 = f32[4,7,64,128]{3,2,1,0:T(8,128)} collective-permute-done((f32[4,7,64,128]{3,2,1,0:T(8,128)S(1)}, f32[4,7,64,128]{3,2,1,0:T(8,128)}, u32[]{:S(2)}, u32[]{:S(2)}) %collective-permute-start.4) | collective-permute-done | bytes 917536 | tf_op jit(solution)/shard_map/ppermute | solution.py:493
  104.7 3.6 %pad_maximum_fusion.rows_in = f32[16,7,64,128]{3,2,1,0:T(8,128)} fusion(f32[4,7,64,128]{3,2,1,0:T(8,128)S(1)} %collective-permute-done.6, f32[4,7,64,128]{3,2,1,0:T(8,128)} %collective-permute-done.5, f32[4,7,64,128]{3,2,1,0:T(8,128)} %collective-permute-done.4, f32[4,7,64,128]{3,2,1,0:T(8,128)S(1)} %get-tuple-element.34), kind=kLoop, calls=%fused_computation | loop fusion | flops 2752512 | bytes 7340032 | tf_op jit(solution)/shard_map/concatenate | solution.py:494
  108.3 4.5 %move_rows.2 = f32[32,7,64,128]{3,2,1,0:T(8,128)} custom-call(s32[16]{0:T(128)} %get-tuple-element.66.slot_a.source_ref.target_ref, s32[16]{0:T(128)} %fusion.5.target_ref, f32[16,7,64,128]{3,2,1,0:T(8,128)} %pad_maximum_fusion.rows_in), custom_call_target="tpu_custom_call" | custom-call | bytes 8000000 | tf_op jit(solution)/shard_map/move_rows/pallas_call | solution.py:351
  112.8 36.7 %all-to-all-done.1.rows_in = f32[32,7,64,128]{3,2,1,0:T(8,128)} async-done(((f32[32,7,64,128]{3,2,1,0:T(8,128)}), f32[32,7,64,128]{3,2,1,0:T(8,128)}, u32[]{:S(2)}, u32[]{:S(2)}) %all-to-all-start.1) | async-done | bytes 7340064 | tf_op jit(solution)/shard_map/all_to_all | solution.py:487
  149.5 4.9 %all-to-all-start = ((f32[32,7,64,128]{3,2,1,0:T(8,128)}), f32[32,7,64,128]{3,2,1,0:T(8,128)}, u32[]{:S(2)}, u32[]{:S(2)}) async-start(f32[32,7,64,128]{3,2,1,0:T(8,128)} %move_rows.2), calls=%async_computation | async-start | bytes 14680064 | tf_op jit(solution)/shard_map/all_to_all | solution.py:487
  155.0 4.4 %move_rows.3 = f32[16,7,64,128]{3,2,1,0:T(8,128)} custom-call(s32[16]{0:T(128)} %select_reduce_fusion.1.source_ref, s32[16]{0:T(128)} %get-tuple-element.66.slot_a.source_ref.target_ref, f32[32,7,64,128]{3,2,1,0:T(8,128)} %all-to-all-done.1.rows_in), custom_call_target="tpu_custom_call" | custom-call | bytes 8000000 | tf_op jit(solution)/shard_map/move_rows/pallas_call | solution.py:351
  159.5 2.5 fusion.15
  162.1 1.9 collective-permute-start.7
  164.3 0.7 select_reduce_fusion.2
  165.0 20.2 %collective-permute-done.9 = f32[4,7,64,128]{3,2,1,0:T(8,128)S(1)} collective-permute-done((f32[4,7,64,128]{3,2,1,0:T(8,128)S(1)}, f32[4,7,64,128]{3,2,1,0:T(8,128)S(1)}, u32[]{:S(2)}, u32[]{:S(2)}) %collective-permute-start.9) | collective-permute-done | bytes 917536 | tf_op jit(solution)/shard_map/ppermute | solution.py:493
  185.2 1.6 collective-permute-done.8
  186.8 18.8 %collective-permute-done.7 = f32[4,7,64,128]{3,2,1,0:T(8,128)S(1)} collective-permute-done((f32[4,7,64,128]{3,2,1,0:T(8,128)S(1)}, f32[4,7,64,128]{3,2,1,0:T(8,128)S(1)}, u32[]{:S(2)}, u32[]{:S(2)}) %collective-permute-start.7) | collective-permute-done | bytes 917536 | tf_op jit(solution)/shard_map/ppermute | solution.py:493
  205.6 2.2 pad_maximum_fusion.1.rows_b
  207.8 38.9 %all-to-all-done.rows_a = f32[32,7,64,128]{3,2,1,0:T(8,128)} async-done(((f32[32,7,64,128]{3,2,1,0:T(8,128)}), f32[32,7,64,128]{3,2,1,0:T(8,128)}, u32[]{:S(2)}, u32[]{:S(2)}) %all-to-all-start) | async-done | bytes 7340064 | tf_op jit(solution)/shard_map/all_to_all | solution.py:487
  246.7 7.2 %join_rows.1 = f32[16,7,128,128]{3,2,1,0:T(8,128)} custom-call(s32[16]{0:T(128)} %get-tuple-element.14.source_a, s32[16]{0:T(128)} %get-tuple-element.13.source_b, f32[32,7,64,128]{3,2,1,0:T(8,128)} %all-to-all-done.rows_a, f32[16,7,64,128]{3,2,1,0:T(8,128)} %pad_maximum_fusion.1.rows_b), custom_call_target="tpu_custom_call" | custom-call | bytes 16000000 | tf_op jit(solution)/shard_map/join_rows/pallas_call | solution.py:383
  (58 shorter events, 5.2 us)
Async XLA Ops:
  0.0 23.3 %copy-start.5 = (s32[6144]{0:T(1024)S(1)}, s32[6144]{0:T(1024)}, u32[]{:S(2)}) copy-start(s32[6144]{0:T(1024)} %param.10) | copy-start | bytes 73732
  0.0 24.2 %copy-start.4 = (s32[2048]{0:T(1024)S(1)}, s32[2048]{0:T(1024)}, u32[]{:S(2)}) copy-start(s32[2048]{0:T(1024)} %param.11) | copy-start | bytes 24580
  2.3 42.3 %collective-permute-start.3 = (f32[4,2,128,128]{3,2,1,0:T(8,128)}, f32[4,2,128,128]{3,2,1,0:T(8,128)S(1)}, u32[]{:S(2)}, u32[]{:S(2)}) collective-permute-start(f32[4,2,128,128]{3,2,1,0:T(8,128)} %get-tuple-element.28), channel_id=1, source_target_pairs={{1,0},{2,1},{3,2},{4,3},{5,4},{6,5},{7,6},{8,7},{9,8},{10,9},{11,1... | collective-permute-start | bytes 1572872 | tf_op jit(solution)/shard_map/ppermute | solution.py:446
  10.5 34.1 %collective-permute-start.2 = (f32[4,2,128,128]{3,2,1,0:T(8,128)}, f32[4,2,128,128]{3,2,1,0:T(8,128)S(1)}, u32[]{:S(2)}, u32[]{:S(2)}) collective-permute-start(f32[4,2,128,128]{3,2,1,0:T(8,128)} %get-tuple-element.29), channel_id=1, source_target_pairs={{0,1},{1,2},{2,3},{3,4},{4,5},{5,6},{6,7},{7,8},{8,9},{9,10},{10,1... | collective-permute-start | bytes 1572872 | tf_op jit(solution)/shard_map/ppermute | solution.py:444
  11.9 13.2 %copy-start.7 = (s32[48]{0:T(128)}, s32[48]{0:T(128)S(1)}, u32[]{:S(2)}) copy-start(s32[48]{0:T(128)S(1)} %get-tuple-element.17.left_ref) | copy-start | bytes 580
  13.1 12.0 %copy-start.8 = (s32[48]{0:T(128)}, s32[48]{0:T(128)S(1)}, u32[]{:S(2)}) copy-start(s32[48]{0:T(128)S(1)} %get-tuple-element.56.right_ref) | copy-start | bytes 580
  15.4 29.3 %collective-permute-start = (f32[3,3,128,128]{3,2,1,0:T(8,128)S(1)}, f32[3,3,128,128]{3,2,1,0:T(8,128)S(1)}, u32[]{:S(2)}, u32[]{:S(2)}) collective-permute-start(f32[3,3,128,128]{3,2,1,0:T(8,128)S(1)} %select_select_fusion.1), channel_id=1, source_target_pairs={{0,1},{1,2},{2,3},{3,4},{4,5},{5,6},{6,7},{7,8},{8,9},{9,10},{10,1... | collective-permute-start | bytes 1769480 | tf_op jit(solution)/shard_map/ppermute | solution.py:443
  16.0 28.6 %collective-permute-start.1 = (f32[3,3,128,128]{3,2,1,0:T(8,128)S(1)}, f32[3,3,128,128]{3,2,1,0:T(8,128)S(1)}, u32[]{:S(2)}, u32[]{:S(2)}) collective-permute-start(f32[3,3,128,128]{3,2,1,0:T(8,128)S(1)} %select_select_fusion), channel_id=1, source_target_pairs={{1,0},{2,1},{3,2},{4,3},{5,4},{6,5},{7,6},{8,7},{9,8},{10,9},{11,1... | collective-permute-start | bytes 1769480 | tf_op jit(solution)/shard_map/ppermute | solution.py:445
  44.6 0.8 copy-start.2
  44.6 1.0 copy-start.3
  44.7 1.1 copy-start
  44.7 1.3 copy-start.1
  52.2 97.2 %all-to-all-start.1 = ((f32[32,7,64,128]{3,2,1,0:T(8,128)}), f32[32,7,64,128]{3,2,1,0:T(8,128)}, u32[]{:S(2)}, u32[]{:S(2)}) async-start(f32[32,7,64,128]{3,2,1,0:T(8,128)} %get-tuple-element.12), calls=%async_computation.1 | async-start | bytes 14680064 | tf_op jit(solution)/shard_map/all_to_all | solution.py:487
  60.8 23.4 %collective-permute-start.6 = (f32[4,7,64,128]{3,2,1,0:T(8,128)}, f32[4,7,64,128]{3,2,1,0:T(8,128)S(1)}, u32[]{:S(2)}, u32[]{:S(2)}) collective-permute-start(f32[4,7,64,128]{3,2,1,0:T(8,128)} %get-tuple-element.35), channel_id=1, source_target_pairs={{0,96},{32,0},{64,32},{96,64},{1,97},{33,1},{65,33},{97,65},{2,98}... | collective-permute-start | bytes 2752520 | tf_op jit(solution)/shard_map/ppermute | solution.py:493
  60.9 25.1 %collective-permute-start.5 = (f32[4,7,64,128]{3,2,1,0:T(8,128)}, f32[4,7,64,128]{3,2,1,0:T(8,128)}, u32[]{:S(2)}, u32[]{:S(2)}) collective-permute-start(f32[4,7,64,128]{3,2,1,0:T(8,128)} %get-tuple-element.36), channel_id=1, source_target_pairs={{0,64},{32,96},{64,0},{96,32},{1,65},{33,97},{65,1},{97,33},{2,66}... | collective-permute-start | bytes 2752520 | tf_op jit(solution)/shard_map/ppermute | solution.py:493
  61.0 43.7 %collective-permute-start.4 = (f32[4,7,64,128]{3,2,1,0:T(8,128)S(1)}, f32[4,7,64,128]{3,2,1,0:T(8,128)}, u32[]{:S(2)}, u32[]{:S(2)}) collective-permute-start(f32[4,7,64,128]{3,2,1,0:T(8,128)S(1)} %get-tuple-element.37), channel_id=1, source_target_pairs={{0,32},{32,64},{64,96},{96,0},{1,33},{33,65},{65,97},{97,1},{2,34}... | collective-permute-start | bytes 2752520 | tf_op jit(solution)/shard_map/ppermute | solution.py:493
  149.5 97.3 %all-to-all-start = ((f32[32,7,64,128]{3,2,1,0:T(8,128)}), f32[32,7,64,128]{3,2,1,0:T(8,128)}, u32[]{:S(2)}, u32[]{:S(2)}) async-start(f32[32,7,64,128]{3,2,1,0:T(8,128)} %move_rows.2), calls=%async_computation | async-start | bytes 14680064 | tf_op jit(solution)/shard_map/all_to_all | solution.py:487
  159.5 4.8 %copy-start.6 = (s32[16]{0:T(128)S(1)}, s32[16]{0:T(128)}, u32[]{:S(2)}) copy-start(s32[16]{0:T(128)} %get-tuple-element.66.slot_a.source_ref.target_ref) | copy-start | bytes 196
  161.9 23.3 %collective-permute-start.9 = (f32[4,7,64,128]{3,2,1,0:T(8,128)S(1)}, f32[4,7,64,128]{3,2,1,0:T(8,128)S(1)}, u32[]{:S(2)}, u32[]{:S(2)}) collective-permute-start(f32[4,7,64,128]{3,2,1,0:T(8,128)S(1)} %get-tuple-element.31), channel_id=1, source_target_pairs={{0,96},{32,0},{64,32},{96,64},{1,97},{33,1},{65,33},{97,65},{2,98}... | collective-permute-start | bytes 2752520 | tf_op jit(solution)/shard_map/ppermute | solution.py:493
  162.0 24.8 %collective-permute-start.8 = (f32[4,7,64,128]{3,2,1,0:T(8,128)S(1)}, f32[4,7,64,128]{3,2,1,0:T(8,128)S(1)}, u32[]{:S(2)}, u32[]{:S(2)}) collective-permute-start(f32[4,7,64,128]{3,2,1,0:T(8,128)S(1)} %get-tuple-element.32), channel_id=1, source_target_pairs={{0,64},{32,96},{64,0},{96,32},{1,65},{33,97},{65,1},{97,33},{2,66}... | collective-permute-start | bytes 2752520 | tf_op jit(solution)/shard_map/ppermute | solution.py:493
  162.1 43.5 %collective-permute-start.7 = (f32[4,7,64,128]{3,2,1,0:T(8,128)S(1)}, f32[4,7,64,128]{3,2,1,0:T(8,128)S(1)}, u32[]{:S(2)}, u32[]{:S(2)}) collective-permute-start(f32[4,7,64,128]{3,2,1,0:T(8,128)S(1)} %get-tuple-element.33), channel_id=1, source_target_pairs={{0,32},{32,64},{64,96},{96,0},{1,33},{33,65},{65,97},{97,1},{2,34}... | collective-permute-start | bytes 2752520 | tf_op jit(solution)/shard_map/ppermute | solution.py:493

commit v2 on v1

v2 whole, which is shorter than its diff:
```python
import functools

import jax
import jax.numpy as jnp
from jax import lax
from jax.experimental import pallas as pl
from jax.experimental.pallas import tpu as pltpu
from jax.sharding import PartitionSpec as P

B = 128
KP = 2
LANES = 128
CWIN = 7
CB = 16
W = 6
BF = jnp.bfloat16
F32 = jnp.float32
SMEM = pltpu.SMEM
ANYWHERE = pl.BlockSpec(memory_space=pl.ANY)
VMEM = pltpu.VMEM


LEFT, OUT_LEFT, OUT_RIGHT, SLOTS_AT, PLAN = 64, 128, 192, (256, 272), 384
HALF = B // 2


def split(x):
    high = x.astype(BF)
    return high, (x - high.astype(F32)).astype(BF)


def left_operand(x):
    high, low = split(x)
    return jnp.concatenate([high, low, high], axis=1)


def right_operand(x):
    high, low = split(x)
    return jnp.concatenate([high, high, low], axis=0)


def matmul(left, right):
    return jnp.dot(left, right, preferred_element_type=F32)


def spread(total, flag, base, pair, slots):
    first, second = pair
    values = {
        base - 1: jnp.where(flag, first, 0.0),
        base: jnp.where(flag, second, first),
        base + 1: jnp.where(flag, 0.0, second),
    }
    for s, value in values.items():
        if s in slots:
            total[s] = value if total.get(s) is None else total[s] + value


def turn(p_tile, half):
    return p_tile.T[half * HALF : (half + 1) * HALF]


def row_product(p_pair, tiles, half):
    turned = jnp.concatenate([turn(p_pair[0], half), turn(p_pair[1], half)], axis=0)
    return matmul(left_operand(turned), right_operand(jnp.concatenate(tiles, axis=1)))


SLOTS = {0: (0, 1, 2, 3), 1: (1, 2, 3), 2: (1, 2, 3, 4)}


def main_kernel(
    half, plan,
    a_ref, p_ref, before_ref, after_ref, behind_ref,
    out,
    stage, carry, sems,
):
    step = pl.program_id(0)
    steps = pl.num_programs(0) - 1
    buf = lax.rem(step, 2)

    def copy_out(at, which, row):
        c = 2 * at - 1 + row
        return pltpu.make_async_copy(stage.at[which, row], out.at[plan[SLOTS_AT[half] + c]], sems.at[which, row])

    def drain(at):
        which = lax.rem(at, 2)
        for row in range(2):
            @pl.when((2 * at - 1 + row >= 0) & (2 * at - 1 + row < 2 * steps))
            def _():
                copy_out(at, which, row).wait()

    @pl.when(step >= 2)
    def _():
        drain(step - 2)

    @pl.when(step == 0)
    def _():
        carry[...] = jnp.zeros_like(carry)

    stage[buf, 0] = carry[0]
    stage[buf, 1] = carry[1]

    @pl.when(step < steps)
    def _():
        carry[...] = jnp.zeros_like(carry)
        first = step * W
        flags = {q: plan[first + q + 4] > 0 for q in range(-1, W + 1)}

        def p_tile(q, m):
            if q < 0:
                return before_ref[0, m]
            if q >= W:
                return after_ref[0, m]
            return p_ref[q, m]

        lefts = {}
        for r in range(W):
            tiles = {
                0: jnp.where(plan[OUT_LEFT + first + r] > 0, a_ref[r, plan[LEFT + first + r]], 0.0),
                1: a_ref[r, 0],
                2: jnp.where(plan[OUT_RIGHT + first + r] > 0, a_ref[r, 3 - plan[LEFT + first + r]], 0.0),
            }
            for k in range(3):
                lefts[r, r + k - 1] = left_operand(tiles[k])
        total = {r: {} for r in range(W)}
        for q in range(-1, W + 1):
            rows = [r for r in (q - 1, q, q + 1) if 0 <= r < W]
            right = right_operand(jnp.concatenate([p_tile(q, 0), p_tile(q, 1)], axis=1))
            product = matmul(jnp.concatenate([lefts[r, q] for r in rows], axis=0), right)
            for n, r in enumerate(rows):
                pair = (product[n * B : (n + 1) * B, :B], product[n * B : (n + 1) * B, B:])
                spread(total[r], flags[q], q // 3 - r // 3 + 2, pair, SLOTS[r % 3])
        for r in range(W):
            slots = SLOTS[r % 3]
            product = row_product((p_ref[r, 0], p_ref[r, 1]), [total[r][s] for s in slots], half)
            g = r // 3
            for n, s in enumerate(slots):
                one = product[:HALF, n * B : (n + 1) * B]
                two = product[HALF:, n * B : (n + 1) * B]
                for delta, value in (
                    (-1, jnp.where(flags[r], one, 0.0)),
                    (0, jnp.where(flags[r], two, one)),
                    (1, jnp.where(flags[r], 0.0, two)),
                ):
                    place = g + delta + 1
                    if place < 2:
                        stage[buf, place, s + 1 - delta] += value
                    else:
                        carry[place - 2, s + 1 - delta] += value

    for row in range(2):
        @pl.when((2 * step - 1 + row >= 0) & (2 * step - 1 + row < 2 * steps))
        def _():
            copy_out(step, buf, row).start()

    @pl.when(step == steps)
    def _():
        drain(step - 1)
        drain(step)


def main_product(half, plan, a_tiles, p_tiles, places, behind):
    rows = a_tiles.shape[0]
    steps = rows // W
    last = steps - 1

    def spec(shape, index):
        return pl.BlockSpec(shape, index)

    return pl.pallas_call(
        functools.partial(main_kernel, half),
        grid_spec=pltpu.PrefetchScalarGridSpec(
            num_scalar_prefetch=1,
            grid=(steps + 1,),
            in_specs=[
                spec((W, 3, B, B), lambda s, *_: (jnp.minimum(s, last), 0, 0, 0)),
                spec((W, KP, B, B), lambda s, *_: (jnp.minimum(s, last), 0, 0, 0)),
                spec((1, KP, B, B), lambda s, *_: (jnp.maximum(jnp.minimum(s, last) * W - 1, 0), 0, 0, 0)),
                spec((1, KP, B, B), lambda s, *_: (jnp.minimum(s * W + W, rows - 1), 0, 0, 0)),
                ANYWHERE,
            ],
            out_specs=ANYWHERE,
            scratch_shapes=[
                VMEM((2, 2, CWIN, HALF, B), F32),
                VMEM((2, CWIN, HALF, B), F32),
                pltpu.SemaphoreType.DMA((2, 2)),
            ],
        ),
        out_shape=jax.ShapeDtypeStruct((places, CWIN, HALF, B), F32),
        compiler_params=pltpu.CompilerParams(
            dimension_semantics=("arbitrary",), vmem_limit_bytes=56 << 20
        ),
        cost_estimate=pl.CostEstimate(
            flops=12_000_000_000, bytes_accessed=20_000_000, transcendentals=0
        ),
        name="triple_product",
    )(plan, a_tiles, p_tiles, p_tiles, p_tiles, behind)


def edge_kernel(
    half, plan,
    before, after, a_first, a_last, p_first, p_last, in_rows,
    out_rows,
    rows_ref, sems,
):
    coarse = CB
    held = (0, 1, coarse - 2, coarse - 1)

    def copy(n, back):
        there, here = out_rows.at[plan[SLOTS_AT[half] + held[n]]], rows_ref.at[n]
        if back:
            return pltpu.make_async_copy(there, here, sems.at[n])
        return pltpu.make_async_copy(here, there, sems.at[n])

    for n in range(4):
        copy(n, True).start()

    sums = []
    for side in range(2):
        halo = (before, after)[side]
        a_edge = (a_first, a_last)[side]
        own_p = (p_first, p_last)[side]
        own_flag = plan[(4, 3 * coarse + 3)[side]] > 0
        flags, tiles, p_at = {}, {}, {}
        for n in range(4):
            q = n - 1 if side == 0 else n
            flags[q] = plan[(0, 3 * coarse + 4)[side] + n] > 0
            p_at[q] = (halo[9 + 2 * n], halo[10 + 2 * n])
        near = 3 if side == 0 else -1
        flags[near] = own_flag
        p_at[near] = (own_p[0, 0], own_p[0, 1])
        total = {r: {} for r in range(3)}
        total[near] = {}
        for q in range(-1, 4):
            rows = [r for r in (q - 1, q, q + 1) if 0 <= r < 3]
            lefts = [left_operand(halo[3 * r + q - r + 1]) for r in rows]
            if q == (2 if side == 0 else 0):
                rows.append(near)
                lefts.append(left_operand(a_edge[0]))
            right = right_operand(jnp.concatenate(p_at[q], axis=1))
            product = matmul(jnp.concatenate(lefts, axis=0), right)
            for n, r in enumerate(rows):
                pair = (product[n * B : (n + 1) * B, :B], product[n * B : (n + 1) * B, B:])
                base = q // 3 - r // 3 + 2
                slots = SLOTS[r % 3] if r != near else (base - 1, base, base + 1)
                spread(total[r], flags[q], base, pair, slots)
        outer, inner = {}, {}

        def put(target, w, value):
            target[w] = value if w not in target else target[w] + value

        for r in range(3):
            slots = sorted(total[r])
            pick = 1 if side == 0 else 0
            turned = left_operand(turn(p_at[r][pick], half))
            product = matmul(turned, right_operand(jnp.concatenate([total[r][s] for s in slots], axis=1)))
            for n, s in enumerate(slots):
                value = product[:, n * B : (n + 1) * B]
                if side == 0:
                    put(outer, s, jnp.where(flags[r], 0.0, value))
                else:
                    put(outer, s + 2, jnp.where(flags[r], value, 0.0))
        slots = sorted(total[near])
        product = row_product(p_at[near], [total[near][s] for s in slots], half)
        for n, s in enumerate(slots):
            one = product[:HALF, n * B : (n + 1) * B]
            two = product[HALF:, n * B : (n + 1) * B]
            put(outer, s + 1, jnp.where(own_flag, two, one))
            if side == 0:
                put(inner, s, jnp.where(own_flag, 0.0, two))
            else:
                put(inner, s + 2, jnp.where(own_flag, one, 0.0))
        sums.append((outer, inner))

    for n in range(4):
        copy(n, True).wait()
    for n, target in ((0, sums[0][0]), (1, sums[0][1]), (2, sums[1][1]), (3, sums[1][0])):
        for w, value in target.items():
            rows_ref[n, w] += value
    for n in range(4):
        copy(n, False).start()
    for n in range(4):
        copy(n, False).wait()


def edge_product(half, plan, before, after, up, down, p_tiles, out_rows):
    rows = p_tiles.shape[0]

    def whole(x):
        return pl.BlockSpec(x.shape, lambda *_: (0,) * x.ndim)

    return pl.pallas_call(
        functools.partial(edge_kernel, half),
        grid_spec=pltpu.PrefetchScalarGridSpec(
            num_scalar_prefetch=1,
            grid=(1,),
            in_specs=[whole(before), whole(after)]
            + [
                pl.BlockSpec((1, B, B), lambda *_: (0, 0, 0)),
                pl.BlockSpec((1, B, B), lambda *_: (8, 0, 0)),
                pl.BlockSpec((1, KP, B, B), lambda *_: (0, 0, 0, 0)),
                pl.BlockSpec((1, KP, B, B), lambda *_: (rows - 1, 0, 0, 0)),
            ]
            + [ANYWHERE],
            out_specs=ANYWHERE,
            scratch_shapes=[VMEM((4, CWIN, HALF, B), F32), pltpu.SemaphoreType.DMA((4,))],
        ),
        out_shape=jax.ShapeDtypeStruct(out_rows.shape, F32),
        input_output_aliases={7: 0},
        compiler_params=pltpu.CompilerParams(
            dimension_semantics=("arbitrary",), vmem_limit_bytes=32 << 20
        ),
        cost_estimate=pl.CostEstimate(flops=2_000_000_000, bytes_accessed=10_000_000, transcendentals=0),
        name="edge_rows",
    )(plan, before, after, down, up, p_tiles, p_tiles, out_rows)


def plan_kernel(place, cols, length, a_tiles, p_tiles, aggregate, owners, plan, up, down, near, mine_ref, used, sem):
    fine = length.shape[0]
    coarse = fine // 3
    wide = aggregate.shape[0]
    fine_total = wide * LANES
    first = place[0] * fine
    line = jnp.where(first < 4, wide - 1, (first - 4) >> 7)
    begin = jnp.where(first < 4, LANES - 4, (first - 4) & (LANES - 1))
    lines = (line, jnp.where(line == wide - 1, 0, line + 1))
    index_loads = [
        pltpu.make_async_copy(aggregate.at[pl.ds(at, 1)], near.at[pl.ds(n, 1)], sem.at[n]) for n, at in enumerate(lines)
    ]
    own = place[0] * coarse
    index_loads.append(pltpu.make_async_copy(owners.at[pl.ds(own >> 7, 1)], mine_ref, sem.at[2]))
    for load in index_loads:
        load.start()

    def entry(i):
        before = first + i - 1
        before = jnp.where(before < 0, fine_total - 1, before)
        left = jnp.where(cols[1, i] == before, 1, 2)
        return left, length[i] > left, length[i] > 3 - left

    sends = []
    for out, row, p_row in ((up, fine - 3, fine - 4), (down, 0, 0)):
        for r in range(3):
            left, on_left, on_right = entry(row + r)
            for k, slot, on in ((0, left, on_left), (2, 3 - left, on_right)):
                sends.append((a_tiles.at[row + r, slot], out.at[3 * r + k], on))
            sends.append((a_tiles.at[row + r, 0], out.at[3 * r + 1], None))
        for n in range(4):
            for m in range(KP):
                sends.append((p_tiles.at[p_row + n, m], out.at[9 + 2 * n + m], None))
    for k, (here, there, on) in enumerate(sends):
        if on is None:
            pltpu.make_async_copy(here, there, sem.at[3 + k]).start()
        else:

            @pl.when(on)
            def _():
                pltpu.make_async_copy(here, there, sem.at[3 + k]).start()

            @pl.when(jnp.logical_not(on))
            def _():
                there[...] = jnp.zeros(there.shape, F32)

    def flag(k, carry):
        i = first + k - 4
        i = jnp.where(i < 0, i + fine_total, jnp.where(i >= fine_total, i - fine_total, i))
        at = begin + k
        plan[k] = jnp.where(near[at >> 7, at & (LANES - 1)] != lax.div(i, 3), 1, 0)
        return carry

    for load in index_loads:
        load.wait()
    lax.fori_loop(0, fine + 8, flag, 0, unroll=8)

    def group(g, carry):
        for mod in range(3):
            i = 3 * g + mod
            left, on_left, on_right = entry(i)
            plan[LEFT + i] = left
            plan[OUT_LEFT + i] = jnp.where(on_left & (i > 0), 1, 0)
            plan[OUT_RIGHT + i] = jnp.where(on_right & (i < fine - 1), 1, 0)
        return carry

    lax.fori_loop(0, coarse, group, 0, unroll=4)
    for k in range(4):
        used[k] = 0

    def slot(c, carry):
        mine = mine_ref[0, (own + c) & (LANES - 1)]
        shift = ((mine >> 5) - (place[0] >> 5)) & 3
        plan[SLOTS_AT[0] + c] = shift * (coarse // 4) + used[shift]
        plan[SLOTS_AT[1] + c] = mine & 31
        used[shift] = used[shift] + 1
        return carry

    lax.fori_loop(0, coarse, slot, 0)
    for k, (here, there, on) in enumerate(sends):
        if on is None:
            pltpu.make_async_copy(here, there, sem.at[3 + k]).wait()
        else:

            @pl.when(on)
            def _():
                pltpu.make_async_copy(here, there, sem.at[3 + k]).wait()


def make_plan(place, a_cols, a_len, aggregate, owner, a_tiles, p_tiles):
    fine = a_len.shape[0]
    owners = owner.reshape(-1, LANES)

    def whole(shape):
        return pl.BlockSpec(shape, lambda *_: (0,) * len(shape))

    halo = (9 + 4 * KP, B, B)
    return pl.pallas_call(
        plan_kernel,
        grid_spec=pltpu.PrefetchScalarGridSpec(
            num_scalar_prefetch=3,
            grid=(1,),
            in_specs=[ANYWHERE] * 4,
            out_specs=[
                pl.BlockSpec(memory_space=SMEM),
                whole(halo),
                whole(halo),
            ],
            scratch_shapes=[
                SMEM((2, LANES), jnp.int32),
                SMEM((1, LANES), jnp.int32),
                SMEM((4,), jnp.int32),
                pltpu.SemaphoreType.DMA((3 + 2 * halo[0],)),
            ],
        ),
        out_shape=[
            jax.ShapeDtypeStruct((PLAN,), jnp.int32),
            jax.ShapeDtypeStruct(halo, F32),
            jax.ShapeDtypeStruct(halo, F32),
        ],
        compiler_params=pltpu.CompilerParams(vmem_limit_bytes=60 << 20),
        cost_estimate=pl.CostEstimate(flops=0, bytes_accessed=5_000_000, transcendentals=0),
        name="plan",
    )(place, a_cols.T, a_len, a_tiles, p_tiles, aggregate.reshape(-1, LANES), owners)


def relay(pairs, sems_in, sems_out):
    inward = [pltpu.make_async_copy(x, y, sems_in.at[k]) for k, (x, y, z) in enumerate(pairs)]
    outward = [pltpu.make_async_copy(y, z, sems_out.at[k]) for k, (x, y, z) in enumerate(pairs)]
    for copy in inward:
        copy.start()
    for come, go in zip(inward, outward):
        come.wait()
        go.start()
    for copy in outward:
        copy.wait()


def move_kernel(source_ref, target_ref, rows_in, rows_out, stage, sems_in, sems_out):
    relay(
        [(rows_in.at[source_ref[k]], stage.at[k], rows_out.at[target_ref[k]]) for k in range(stage.shape[0])],
        sems_in,
        sems_out,
    )


def move_rows(source, target, rows, places):
    count = source.shape[0]
    return pl.pallas_call(
        move_kernel,
        grid_spec=pltpu.PrefetchScalarGridSpec(
            num_scalar_prefetch=2,
            grid=(1,),
            in_specs=[ANYWHERE],
            out_specs=ANYWHERE,
            scratch_shapes=[
                VMEM((count,) + rows.shape[1:], F32),
                pltpu.SemaphoreType.DMA((count,)),
                pltpu.SemaphoreType.DMA((count,)),
            ],
        ),
        out_shape=jax.ShapeDtypeStruct((places,) + rows.shape[1:], F32),
        compiler_params=pltpu.CompilerParams(vmem_limit_bytes=56 << 20),
        cost_estimate=pl.CostEstimate(flops=0, bytes_accessed=8_000_000, transcendentals=0),
        name="move_rows",
    )(source, target, rows)


def put_kernel(half, source, rows, *refs):
    out, stage, sems_in, sems_out = refs[-4:]
    part = pl.ds(half * HALF, HALF)
    relay(
        [(rows.at[source[k]], stage.at[k], out.at[k, :, part]) for k in range(stage.shape[0])], sems_in, sems_out
    )


def put_rows(half, source, rows, whole=None):
    count = source.shape[0]
    held = [] if whole is None else [whole]
    return pl.pallas_call(
        functools.partial(put_kernel, half),
        grid_spec=pltpu.PrefetchScalarGridSpec(
            num_scalar_prefetch=1,
            grid=(1,),
            in_specs=[ANYWHERE] * (1 + len(held)),
            out_specs=ANYWHERE,
            scratch_shapes=[
                VMEM((count,) + rows.shape[1:], F32),
                pltpu.SemaphoreType.DMA((count,)),
                pltpu.SemaphoreType.DMA((count,)),
            ],
        ),
        out_shape=jax.ShapeDtypeStruct((count, CWIN, B, B), F32),
        input_output_aliases={2: 0} if held else {},
        compiler_params=pltpu.CompilerParams(vmem_limit_bytes=60 << 20),
        cost_estimate=pl.CostEstimate(flops=0, bytes_accessed=8_000_000, transcendentals=0),
        name="put_rows",
    )(source, rows, *held)


AXES = ("gx", "gy")


def shards(a_tiles, a_cols, a_len, p_tiles, aggregate, owner):
    count_x, count_y = lax.axis_size("gx"), lax.axis_size("gy")
    index_x, index_y = lax.axis_index("gx"), lax.axis_index("gy")
    size = count_x * count_y
    device = index_x * count_y + index_y
    coarse = a_tiles.shape[0] // 3
    depth = coarse // count_x
    place = jnp.reshape(device, (1,)).astype(jnp.int32)
    plan, up, down = make_plan(place, a_cols, a_len, aggregate, owner, a_tiles, p_tiles)
    above = [(i, (i + 1) % size) for i in range(size)]
    below = [(j, i) for i, j in above]
    before = lax.ppermute(up, AXES, above)
    behind = lax.ppermute(down, AXES, below)

    def half_rows(half, places, after):
        rows = main_product(half, plan, a_tiles, p_tiles, places, after)
        return edge_product(half, plan, before, behind, up, down, p_tiles, rows)

    rows_b = half_rows(1, count_y, plan)
    rows_a = half_rows(0, coarse, rows_b)

    table = owner.reshape(count_x, count_y, coarse)
    order = jnp.arange(coarse)
    shift = table[0, 0] // count_y
    same = shift[None, :] == shift[:, None]
    rank = jnp.sum((same & (order[None, :] < order[:, None])).astype(jnp.int32), axis=1)
    slot = (shift * depth + rank).astype(jnp.int32)
    from_x = (index_x - shift) % count_x
    column = table[:, index_y] % count_y
    mid_a_target = jnp.sum(
        jnp.where(jnp.arange(count_x)[:, None] == from_x[None, :], column, 0), axis=0
    ).astype(jnp.int32)
    hit = (table[index_x] % count_y) == index_y
    mid_b_source = jnp.sum(jnp.where(hit, jnp.arange(count_y)[:, None], 0), axis=0).astype(jnp.int32)
    found = table.reshape(size, coarse) == device
    sender = jnp.sum(jnp.where(found, jnp.arange(size)[:, None], 0), axis=0)
    ids = sender * coarse + order
    spot = jnp.sum((ids[None, :] < ids[:, None]).astype(jnp.int32), axis=1)
    at = spot[None, :] == order[:, None]
    last_a = jnp.sum(jnp.where(at, (sender % count_y)[None, :], 0), axis=1).astype(jnp.int32)
    last_b = jnp.sum(jnp.where(at, slot[None, :], 0), axis=1).astype(jnp.int32)

    def over_y(x):
        return lax.all_to_all(x, "gy", split_axis=0, concat_axis=0, tiled=True)

    def along_x(x):
        parts = [x[:depth]]
        for k in range(1, count_x):
            pairs = [(i, (i + k) % count_x) for i in range(count_x)]
            parts.append(lax.ppermute(x[k * depth : (k + 1) * depth], "gx", pairs))
        return jnp.concatenate(parts, axis=0)

    got_b = over_y(rows_b)
    got_a = along_x(rows_a)
    end_a = over_y(move_rows(slot, mid_a_target, got_a, count_y))
    end_b = along_x(move_rows(mid_b_source, slot, got_b, coarse))
    return put_rows(0, last_a, end_a, put_rows(1, last_b, end_b))


def solution(mesh):
    in_specs = (
        P(("gx", "gy"), None, None, None),
        P(("gx", "gy"), None),
        P(("gx", "gy")),
        P(("gx", "gy"), None, None, None),
        P(),
        P(),
    )
    out_specs = P(("gx", "gy"), None, None, None)
    return jax.shard_map(shards, mesh=mesh, in_specs=in_specs, out_specs=out_specs, check_vma=False)
```

time: 255 us -> 242 us (0.949)
  waiting for transfers between devices: 157 us -> 124 us
  Pallas kernels: 40.5 us -> 65.5 us
  starting transfers between devices: 29.5 us -> 24.8 us
  other arithmetic: 13.2 us -> 10.1 us
  local copies, waits for them, and re-layouts: 13.2 us -> 16.1 us
    all_to_all x2, waiting for transfers between devices: 75.6 us -> 42 us  [over_y(): return lax.all_to_all(x, 'gy', split_axis=0, concat_axis=0, tiled=True)]
    pallas_call x3 -> x7, Pallas kernels: 31.6 us -> 56.5 us  [the longest x2 31.4 us: main_product(): pl.pallas_call(functools.partial(main_kernel, half), grid_spec=pltpu.Pref...]
    unnamed x18 -> x28, local copies, waits for them, and re-layouts: 1.33 us -> 10.7 us
    ppermute x4 -> x2, starting transfers between devices: 15.5 us -> 8.35 us  [the longest x1 8.27 us: shards(): behind = lax.ppermute(down, AXES, below)]
    slice x4 -> x0, local copies, waits for them, and re-layouts: 3.08 us -> none  [the longest x1 2.29 us: shards(): p_after = lax.ppermute(p_tiles[:4], axes, down)]
  transfers between devices with their start and end apart: 12 -> 10, of which waited for: 8 -> 6; matrix products, arithmetic and copies ran while one was open for 9% -> 6% of each run, Pallas kernels for 11% -> 21%
where the time goes in v2:
time: 242 us; the launch traced here: 241 us
  waiting for transfers between devices  124 us (51%)
  Pallas kernels  65.5 us (27%)
  starting transfers between devices  24.8 us (10%)
  local copies, waits for them, and re-layouts  16.1 us (7%)
  other arithmetic  10.1 us (4%)
    ppermute x6, waiting for transfers between devices, along_x(): parts.append(lax.ppermute(x[k * depth:(k + 1) * depth], 'gx', pairs))  82 us
    all_to_all x2, waiting for transfers between devices, over_y(): return lax.all_to_all(x, 'gy', split_axis=0, concat_axis=0, tiled=True)  42 us
    pallas_call x2, Pallas kernels, main_product(): pl.pallas_call(functools.partial(main_kernel, half), grid_spec=pltpu.Pref...  31.4 us
    pallas_call x2, Pallas kernels, edge_product(): pl.pallas_call(functools.partial(edge_kernel, half), grid_spec=pltpu.Pref...  12 us
    unnamed x28, local copies, waits for them, and re-layouts  10.7 us
    all_to_all x2, starting transfers between devices, over_y(): return lax.all_to_all(x, 'gy', split_axis=0, concat_axis=0, tiled=True)  9.99 us
    pallas_call x2, Pallas kernels, move_rows(): pl.pallas_call(move_kernel, grid_spec=pltpu.PrefetchScalarGridSpec(num_sc...  8.93 us
    pallas_call x2, Pallas kernels, put_rows(): pl.pallas_call(functools.partial(put_kernel, half), grid_spec=pltpu.Prefe...  8.87 us
  transfers between devices with their start and end apart: 10, of which 6 were waited for; matrix products, arithmetic and copies ran while one was open for 6% of the time, Pallas kernels for 21%

profile of v2, /device:TPU:0, one launch (start us, length us, event | category | flops | bytes accessed | tf_op | source)
XLA Modules:
  0.0 240.8 jit_solution(15719586033927593852)
XLA Ops:
  0.0 4.2 %plan.1 = (s32[384]{0:T(512)}, f32[17,128,128]{2,1,0:T(8,128)}, f32[17,128,128]{2,1,0:T(8,128)}) custom-call(s32[1]{0:T(128)} %bitcast.2.place, s32[3,48]{1,0:T(4,128)} %bitcast.21, s32[48]{0:T(128)} %length.1, f32[48,3,128,128]{3,2,1,0:T(8,128)} %a_ref.3, f32[48,2,128,128]{3,2,1,0:T(8,128)} %p_last.3, s32[48,128]{1,0:T(8,128)} %bitcast.19, s32[16,128]{1,0:T(8,128)} %bitcast.18), custom_call_target="tpu_custom_call" | custom-call | bytes 5000000 | tf_op jit(solution)/shard_map/plan/pallas_call | solution.py:414
  4.3 8.3 %collective-permute-start.1 = (f32[17,128,128]{2,1,0:T(8,128)}, f32[17,128,128]{2,1,0:T(8,128)}, u32[]{:S(2)}, u32[]{:S(2)}) collective-permute-start(f32[17,128,128]{2,1,0:T(8,128)} %get-tuple-element.10.a_first), channel_id=1, source_target_pairs={{1,0},{2,1},{3,2},{4,3},{5,4},{6,5},{7,6},{8,7},{9,8},{10,9},{11,1... | collective-permute-start | bytes 3342344 | tf_op jit(solution)/shard_map/ppermute | solution.py:532
  12.6 15.7 %triple_product.2.in_rows = f32[32,7,64,128]{3,2,1,0:T(8,128)} custom-call(s32[384]{0:T(512)} %get-tuple-element.8.plan.behind_ref, f32[48,3,128,128]{3,2,1,0:T(8,128)} %a_ref.3, f32[48,2,128,128]{3,2,1,0:T(8,128)} %p_last.3, f32[48,2,128,128]{3,2,1,0:T(8,128)} %p_last.3, f32[48,2,128,128]{3,2,1,0:T(8,128)} %p_last.3, s32[384]{0:T(512)} %get-tuple-element.8.plan.behind_ref), custom_call_target="tpu_custom_call" | custom-call | flops 12000000000 | bytes 20000000 | tf_op jit(solution)/shard_map/triple_product/pallas_call | solution.py:169
  28.3 3.1 %copy-done = f32[32,7,64,128]{3,2,1,0:T(8,128)S(1)} copy-done((f32[32,7,64,128]{3,2,1,0:T(8,128)S(1)}, f32[32,7,64,128]{3,2,1,0:T(8,128)}, u32[]{:S(2)}) %copy-start) | copy-done | bytes 7340056
  31.4 1.2 copy-done.4
  32.7 6.0 %edge_rows.2.behind_ref = f32[32,7,64,128]{3,2,1,0:T(8,128)S(1)} custom-call(s32[384]{0:T(512)S(1)} %copy-done.6, f32[17,128,128]{2,1,0:T(8,128)} %collective-permute-done.before, f32[17,128,128]{2,1,0:T(8,128)} %collective-permute-done.1.after, f32[17,128,128]{2,1,0:T(8,128)S(1)} %copy-done.4, ...), custom_call_target="tpu_custom_call", output_to_operand_aliasing={{}: (7, {})} | custom-call | flops 2000000000 | bytes 10000000 | tf_op jit(solution)/shard_map/edge_rows/pallas_call | solution.py:291
  38.7 3.0 %copy-done.1 = f32[32,7,64,128]{3,2,1,0:T(8,128)} copy-done((f32[32,7,64,128]{3,2,1,0:T(8,128)}, f32[32,7,64,128]{3,2,1,0:T(8,128)S(1)}, u32[]{:S(2)}) %copy-start.1) | copy-done | bytes 7340056
  41.8 5.1 %all-to-all-start.1 = ((f32[32,7,64,128]{3,2,1,0:T(8,128)}), f32[32,7,64,128]{3,2,1,0:T(8,128)}, u32[]{:S(2)}, u32[]{:S(2)}) async-start(f32[32,7,64,128]{3,2,1,0:T(8,128)} %copy-done.1), calls=%async_computation.1 | async-start | bytes 14680064 | tf_op jit(solution)/shard_map/all_to_all | solution.py:563
  46.8 15.7 %triple_product.3.in_rows = f32[16,7,64,128]{3,2,1,0:T(8,128)} custom-call(s32[384]{0:T(512)} %get-tuple-element.8.plan.behind_ref, f32[48,3,128,128]{3,2,1,0:T(8,128)} %a_ref.3, f32[48,2,128,128]{3,2,1,0:T(8,128)} %p_last.3, f32[48,2,128,128]{3,2,1,0:T(8,128)} %p_last.3, f32[48,2,128,128]{3,2,1,0:T(8,128)} %p_last.3, f32[32,7,64,128]{3,2,1,0:T(8,128)} %copy-done.1), custom_call_target="tpu_custom_call" | custom-call | flops 12000000000 | bytes 20000000 | tf_op jit(solution)/shard_map/triple_product/pallas_call | solution.py:169
  62.6 2.0 copy-done.2
  64.7 1.2 copy-done.5
  65.9 6.0 %edge_rows.3 = f32[16,7,64,128]{3,2,1,0:T(8,128)S(1)} custom-call(s32[384]{0:T(512)S(1)} %copy-done.7, f32[17,128,128]{2,1,0:T(8,128)} %collective-permute-done.before, f32[17,128,128]{2,1,0:T(8,128)} %collective-permute-done.1.after, f32[17,128,128]{2,1,0:T(8,128)S(1)} %copy-done.5, f32[17,128,128]{2,1,0:T(8,128)S(1)} %copy-done.3, ...), custom_call_target="tpu_custom_call", output_to_operand_aliasing={{}: (7, {})} | custom-call | flops 2000000000 | bytes 10000000 | tf_op jit(solution)/shard_map/edge_rows/pallas_call | solution.py:291
  71.9 1.6 fusion.9
  73.5 2.4 collective-permute-start.4
  75.9 0.9 collective-permute-start.2
  78.2 37.7 %collective-permute-done.4 = f32[4,7,64,128]{3,2,1,0:T(8,128)S(1)} collective-permute-done((f32[4,7,64,128]{3,2,1,0:T(8,128)}, f32[4,7,64,128]{3,2,1,0:T(8,128)S(1)}, u32[]{:S(2)}, u32[]{:S(2)}) %collective-permute-start.4) | collective-permute-done | bytes 917536 | tf_op jit(solution)/shard_map/ppermute | solution.py:569
  115.9 3.2 %collective-permute-done.2 = f32[4,7,64,128]{3,2,1,0:T(8,128)} collective-permute-done((f32[4,7,64,128]{3,2,1,0:T(8,128)S(1)}, f32[4,7,64,128]{3,2,1,0:T(8,128)}, u32[]{:S(2)}, u32[]{:S(2)}) %collective-permute-start.2) | collective-permute-done | bytes 917536 | tf_op jit(solution)/shard_map/ppermute | solution.py:569
  119.1 3.6 %pad_maximum_fusion.rows_in = f32[16,7,64,128]{3,2,1,0:T(8,128)} fusion(f32[4,7,64,128]{3,2,1,0:T(8,128)S(1)} %collective-permute-done.4, f32[4,7,64,128]{3,2,1,0:T(8,128)} %collective-permute-done.3, f32[4,7,64,128]{3,2,1,0:T(8,128)} %collective-permute-done.2, f32[4,7,64,128]{3,2,1,0:T(8,128)S(1)} %get-tuple-element.19), kind=kLoop, calls=%fused_computation | loop fusion | flops 2752512 | bytes 7340032 | tf_op jit(solution)/shard_map/concatenate | solution.py:570
  122.7 4.5 %move_rows.2 = f32[32,7,64,128]{3,2,1,0:T(8,128)} custom-call(s32[16]{0:T(128)} %multiply_add_fusion.source_ref.target_ref, s32[16]{0:T(128)} %fusion.5.target_ref, f32[16,7,64,128]{3,2,1,0:T(8,128)} %pad_maximum_fusion.rows_in), custom_call_target="tpu_custom_call" | custom-call | bytes 8000000 | tf_op jit(solution)/shard_map/move_rows/pallas_call | solution.py:465
  127.2 11.9 %all-to-all-done.1.rows_in = f32[32,7,64,128]{3,2,1,0:T(8,128)} async-done(((f32[32,7,64,128]{3,2,1,0:T(8,128)}), f32[32,7,64,128]{3,2,1,0:T(8,128)}, u32[]{:S(2)}, u32[]{:S(2)}) %all-to-all-start.1) | async-done | bytes 7340064 | tf_op jit(solution)/shard_map/all_to_all | solution.py:563
  139.1 4.9 %all-to-all-start = ((f32[32,7,64,128]{3,2,1,0:T(8,128)}), f32[32,7,64,128]{3,2,1,0:T(8,128)}, u32[]{:S(2)}, u32[]{:S(2)}) async-start(f32[32,7,64,128]{3,2,1,0:T(8,128)} %move_rows.2), calls=%async_computation | async-start | bytes 14680064 | tf_op jit(solution)/shard_map/all_to_all | solution.py:563
  144.6 4.4 %move_rows.3 = f32[16,7,64,128]{3,2,1,0:T(8,128)} custom-call(s32[16]{0:T(128)} %select_reduce_fusion.1.source_ref, s32[16]{0:T(128)} %multiply_add_fusion.source_ref.target_ref, f32[32,7,64,128]{3,2,1,0:T(8,128)} %all-to-all-done.1.rows_in), custom_call_target="tpu_custom_call" | custom-call | bytes 8000000 | tf_op jit(solution)/shard_map/move_rows/pallas_call | solution.py:465
  149.1 3.6 %fusion.8 = (f32[4,7,64,128]{3,2,1,0:T(8,128)S(1)}, f32[4,7,64,128]{3,2,1,0:T(8,128)}, f32[4,7,64,128]{3,2,1,0:T(8,128)}, f32[4,7,64,128]{3,2,1,0:T(8,128)S(1)}) fusion(f32[16,7,64,128]{3,2,1,0:T(8,128)} %move_rows.3), kind=kLoop, calls=%fused_computation.40 | loop fusion | bytes 7340032 | tf_op jit(solution)/shard_map/slice | solution.py:566
  152.7 2.4 collective-permute-start.7
  155.1 0.9 collective-permute-start.5
  156.3 0.7 select_reduce_fusion.2
  157.0 38.0 %collective-permute-done.7 = f32[4,7,64,128]{3,2,1,0:T(8,128)S(1)} collective-permute-done((f32[4,7,64,128]{3,2,1,0:T(8,128)}, f32[4,7,64,128]{3,2,1,0:T(8,128)S(1)}, u32[]{:S(2)}, u32[]{:S(2)}) %collective-permute-start.7) | collective-permute-done | bytes 917536 | tf_op jit(solution)/shard_map/ppermute | solution.py:569
  195.0 3.2 %collective-permute-done.5 = f32[4,7,64,128]{3,2,1,0:T(8,128)} collective-permute-done((f32[4,7,64,128]{3,2,1,0:T(8,128)S(1)}, f32[4,7,64,128]{3,2,1,0:T(8,128)}, u32[]{:S(2)}, u32[]{:S(2)}) %collective-permute-start.5) | collective-permute-done | bytes 917536 | tf_op jit(solution)/shard_map/ppermute | solution.py:569
  198.2 3.6 %pad_maximum_fusion.1.rows = f32[16,7,64,128]{3,2,1,0:T(8,128)} fusion(f32[4,7,64,128]{3,2,1,0:T(8,128)S(1)} %collective-permute-done.7, f32[4,7,64,128]{3,2,1,0:T(8,128)} %collective-permute-done.6, f32[4,7,64,128]{3,2,1,0:T(8,128)} %collective-permute-done.5, f32[4,7,64,128]{3,2,1,0:T(8,128)S(1)} %get-tuple-element.15), kind=kLoop, calls=%fused_computation.1 | loop fusion | flops 2752512 | bytes 7340032 | tf_op jit(solution)/shard_map/concatenate | solution.py:570
  201.8 4.4 %put_rows.2.refs_0_ = f32[16,7,128,128]{3,2,1,0:T(8,128)} custom-call(s32[16]{0:T(128)} %get-tuple-element.11.source, f32[16,7,64,128]{3,2,1,0:T(8,128)} %pad_maximum_fusion.1.rows), custom_call_target="tpu_custom_call" | custom-call | bytes 8000000 | tf_op jit(solution)/shard_map/put_rows/pallas_call | solution.py:496
  206.2 30.1 %all-to-all-done.rows = f32[32,7,64,128]{3,2,1,0:T(8,128)} async-done(((f32[32,7,64,128]{3,2,1,0:T(8,128)}), f32[32,7,64,128]{3,2,1,0:T(8,128)}, u32[]{:S(2)}, u32[]{:S(2)}) %all-to-all-start) | async-done | bytes 7340064 | tf_op jit(solution)/shard_map/all_to_all | solution.py:563
  236.4 4.4 %put_rows.3 = f32[16,7,128,128]{3,2,1,0:T(8,128)} custom-call(s32[16]{0:T(128)} %get-tuple-element.12.source, f32[32,7,64,128]{3,2,1,0:T(8,128)} %all-to-all-done.rows, f32[16,7,128,128]{3,2,1,0:T(8,128)} %put_rows.2.refs_0_), custom_call_target="tpu_custom_call", output_to_operand_aliasing={{}: (2, {})} | custom-call | bytes 8000000 | tf_op jit(solution)/shard_map/put_rows/pallas_call | solution.py:496
  (44 shorter events, 2.4 us)
Async XLA Ops:
  4.2 24.0 %collective-permute-start = (f32[17,128,128]{2,1,0:T(8,128)}, f32[17,128,128]{2,1,0:T(8,128)}, u32[]{:S(2)}, u32[]{:S(2)}) collective-permute-start(f32[17,128,128]{2,1,0:T(8,128)} %get-tuple-element.9.a_last), channel_id=1, source_target_pairs={{0,1},{1,2},{2,3},{3,4},{4,5},{5,6},{6,7},{7,8},{8,9},{9,10},{10,1... | collective-permute-start | bytes 3342344 | tf_op jit(solution)/shard_map/ppermute | solution.py:531
  4.3 24.0 %collective-permute-start.1 = (f32[17,128,128]{2,1,0:T(8,128)}, f32[17,128,128]{2,1,0:T(8,128)}, u32[]{:S(2)}, u32[]{:S(2)}) collective-permute-start(f32[17,128,128]{2,1,0:T(8,128)} %get-tuple-element.10.a_first), channel_id=1, source_target_pairs={{1,0},{2,1},{3,2},{4,3},{5,4},{6,5},{7,6},{8,7},{9,8},{10,9},{11,1... | collective-permute-start | bytes 3342344 | tf_op jit(solution)/shard_map/ppermute | solution.py:532
  12.6 15.7 %slice-start = ((s8[6291456]{0:T(1024)(128)(4,1)}), s8[4194304]{0:T(1024)(128)(4,1)S(1)}, s32[]{:S(2)}) async-start(s8[6291456]{0:T(1024)(128)(4,1)} %bitcast.14), calls=%async_computation.2 | async-start | bytes 8388608
  12.6 15.7 %slice-start.1 = ((s8[6291456]{0:T(1024)(128)(4,1)}), s8[2097152]{0:T(1024)(128)(4,1)S(1)}, s32[]{:S(2)}) async-start(s8[6291456]{0:T(1024)(128)(4,1)} %bitcast.14), calls=%async_computation.3 | async-start | bytes 4194304
  12.6 15.7 %copy-start.3 = (f32[17,128,128]{2,1,0:T(8,128)S(1)}, f32[17,128,128]{2,1,0:T(8,128)}, u32[]{:S(2)}) copy-start(f32[17,128,128]{2,1,0:T(8,128)} %get-tuple-element.9.a_last) | copy-start | bytes 3342340
  12.6 15.7 %copy-start.6 = (s32[384]{0:T(512)S(1)}, s32[384]{0:T(512)}, u32[]{:S(2)}) copy-start(s32[384]{0:T(512)} %get-tuple-element.8.plan.behind_ref) | copy-start | bytes 4612
  28.3 3.1 %copy-start = (f32[32,7,64,128]{3,2,1,0:T(8,128)S(1)}, f32[32,7,64,128]{3,2,1,0:T(8,128)}, u32[]{:S(2)}) copy-start(f32[32,7,64,128]{3,2,1,0:T(8,128)} %triple_product.2.in_rows) | copy-start | bytes 22020100
  31.4 1.2 copy-start.4
  38.7 3.1 %copy-start.1 = (f32[32,7,64,128]{3,2,1,0:T(8,128)}, f32[32,7,64,128]{3,2,1,0:T(8,128)S(1)}, u32[]{:S(2)}) copy-start(f32[32,7,64,128]{3,2,1,0:T(8,128)S(1)} %edge_rows.2.behind_ref) | copy-start | bytes 22020100
  41.8 20.8 %slice-start.2 = ((s8[6291456]{0:T(1024)(128)(4,1)}), s8[2097152]{0:T(1024)(128)(4,1)S(1)}, s32[]{:S(2)}) async-start(s8[6291456]{0:T(1024)(128)(4,1)} %bitcast.16), calls=%async_computation.4 | async-start | bytes 4194304
  41.8 97.4 %all-to-all-start.1 = ((f32[32,7,64,128]{3,2,1,0:T(8,128)}), f32[32,7,64,128]{3,2,1,0:T(8,128)}, u32[]{:S(2)}, u32[]{:S(2)}) async-start(f32[32,7,64,128]{3,2,1,0:T(8,128)} %copy-done.1), calls=%async_computation.1 | async-start | bytes 14680064 | tf_op jit(solution)/shard_map/all_to_all | solution.py:563
  46.8 15.8 %slice-start.3 = ((s8[6291456]{0:T(1024)(128)(4,1)}), s8[4194304]{0:T(1024)(128)(4,1)S(1)}, s32[]{:S(2)}) async-start(s8[6291456]{0:T(1024)(128)(4,1)} %bitcast.16), calls=%async_computation.5 | async-start | bytes 8388608
  46.8 15.8 %copy-start.7 = (s32[384]{0:T(512)S(1)}, s32[384]{0:T(512)}, u32[]{:S(2)}) copy-start(s32[384]{0:T(512)} %get-tuple-element.8.plan.behind_ref) | copy-start | bytes 4612
  62.6 2.0 copy-start.2
  64.7 1.2 copy-start.5
  71.9 4.9 %copy-start.8 = (s32[2048]{0:T(1024)S(1)}, s32[2048]{0:T(1024)}, u32[]{:S(2)}) copy-start(s32[2048]{0:T(1024)} %param.11) | copy-start | bytes 24580
  73.5 42.4 %collective-permute-start.4 = (f32[4,7,64,128]{3,2,1,0:T(8,128)}, f32[4,7,64,128]{3,2,1,0:T(8,128)S(1)}, u32[]{:S(2)}, u32[]{:S(2)}) collective-permute-start(f32[4,7,64,128]{3,2,1,0:T(8,128)} %get-tuple-element.20), channel_id=1, source_target_pairs={{0,96},{32,0},{64,32},{96,64},{1,97},{33,1},{65,33},{97,65},{2,98}... | collective-permute-start | bytes 2752520 | tf_op jit(solution)/shard_map/ppermute | solution.py:569
  75.9 40.0 %collective-permute-start.3 = (f32[4,7,64,128]{3,2,1,0:T(8,128)}, f32[4,7,64,128]{3,2,1,0:T(8,128)}, u32[]{:S(2)}, u32[]{:S(2)}) collective-permute-start(f32[4,7,64,128]{3,2,1,0:T(8,128)} %get-tuple-element.21), channel_id=1, source_target_pairs={{0,64},{32,96},{64,0},{96,32},{1,65},{33,97},{65,1},{97,33},{2,66}... | collective-permute-start | bytes 2752520 | tf_op jit(solution)/shard_map/ppermute | solution.py:569
  75.9 43.2 %collective-permute-start.2 = (f32[4,7,64,128]{3,2,1,0:T(8,128)S(1)}, f32[4,7,64,128]{3,2,1,0:T(8,128)}, u32[]{:S(2)}, u32[]{:S(2)}) collective-permute-start(f32[4,7,64,128]{3,2,1,0:T(8,128)S(1)} %get-tuple-element.22), channel_id=1, source_target_pairs={{0,32},{32,64},{64,96},{96,0},{1,33},{33,65},{65,97},{97,1},{2,34}... | collective-permute-start | bytes 2752520 | tf_op jit(solution)/shard_map/ppermute | solution.py:569
  139.1 97.2 %all-to-all-start = ((f32[32,7,64,128]{3,2,1,0:T(8,128)}), f32[32,7,64,128]{3,2,1,0:T(8,128)}, u32[]{:S(2)}, u32[]{:S(2)}) async-start(f32[32,7,64,128]{3,2,1,0:T(8,128)} %move_rows.2), calls=%async_computation | async-start | bytes 14680064 | tf_op jit(solution)/shard_map/all_to_all | solution.py:563
  149.1 7.2 %copy-start.9 = (s32[16]{0:T(128)S(1)}, s32[16]{0:T(128)}, u32[]{:S(2)}) copy-start(s32[16]{0:T(128)} %multiply_add_fusion.source_ref.target_ref) | copy-start | bytes 196
  152.7 42.2 %collective-permute-start.7 = (f32[4,7,64,128]{3,2,1,0:T(8,128)}, f32[4,7,64,128]{3,2,1,0:T(8,128)S(1)}, u32[]{:S(2)}, u32[]{:S(2)}) collective-permute-start(f32[4,7,64,128]{3,2,1,0:T(8,128)} %get-tuple-element.16), channel_id=1, source_target_pairs={{0,96},{32,0},{64,32},{96,64},{1,97},{33,1},{65,33},{97,65},{2,98}... | collective-permute-start | bytes 2752520 | tf_op jit(solution)/shard_map/ppermute | solution.py:569
  155.1 39.9 %collective-permute-start.6 = (f32[4,7,64,128]{3,2,1,0:T(8,128)}, f32[4,7,64,128]{3,2,1,0:T(8,128)}, u32[]{:S(2)}, u32[]{:S(2)}) collective-permute-start(f32[4,7,64,128]{3,2,1,0:T(8,128)} %get-tuple-element.17), channel_id=1, source_target_pairs={{0,64},{32,96},{64,0},{96,32},{1,65},{33,97},{65,1},{97,33},{2,66}... | collective-permute-start | bytes 2752520 | tf_op jit(solution)/shard_map/ppermute | solution.py:569
  155.1 43.0 %collective-permute-start.5 = (f32[4,7,64,128]{3,2,1,0:T(8,128)S(1)}, f32[4,7,64,128]{3,2,1,0:T(8,128)}, u32[]{:S(2)}, u32[]{:S(2)}) collective-permute-start(f32[4,7,64,128]{3,2,1,0:T(8,128)S(1)} %get-tuple-element.18), channel_id=1, source_target_pairs={{0,32},{32,64},{64,96},{96,0},{1,33},{33,65},{65,97},{97,1},{2,34}... | collective-permute-start | bytes 2752520 | tf_op jit(solution)/shard_map/ppermute | solution.py:569

commit v3 on v2

--- a/solution.py
+++ b/solution.py
@@ -12,7 +12,8 @@
 LANES = 128
 CWIN = 7
 CB = 16
-W = 6
+W = 12
+G = W // 3
 BF = jnp.bfloat16
 F32 = jnp.float32
 SMEM = pltpu.SMEM
@@ -78,13 +79,13 @@
     buf = lax.rem(step, 2)
 
     def copy_out(at, which, row):
-        c = 2 * at - 1 + row
+        c = G * at - 1 + row
         return pltpu.make_async_copy(stage.at[which, row], out.at[plan[SLOTS_AT[half] + c]], sems.at[which, row])
 
     def drain(at):
         which = lax.rem(at, 2)
-        for row in range(2):
-            @pl.when((2 * at - 1 + row >= 0) & (2 * at - 1 + row < 2 * steps))
+        for row in range(G):
+            @pl.when((G * at - 1 + row >= 0) & (G * at - 1 + row < G * steps))
             def _():
                 copy_out(at, which, row).wait()
 
@@ -98,6 +99,8 @@
 
     stage[buf, 0] = carry[0]
     stage[buf, 1] = carry[1]
+    for row in range(2, G):
+        stage[buf, row] = jnp.zeros(carry.shape[1:], F32)
 
     @pl.when(step < steps)
     def _():
@@ -112,24 +115,25 @@
                 return after_ref[0, m]
             return p_ref[q, m]
 
-        lefts = {}
-        for r in range(W):
-            tiles = {
-                0: jnp.where(plan[OUT_LEFT + first + r] > 0, a_ref[r, plan[LEFT + first + r]], 0.0),
-                1: a_ref[r, 0],
-                2: jnp.where(plan[OUT_RIGHT + first + r] > 0, a_ref[r, 3 - plan[LEFT + first + r]], 0.0),
-            }
-            for k in range(3):
-                lefts[r, r + k - 1] = left_operand(tiles[k])
+        def a_tile(r, q):
+            if q == r:
+                return a_ref[r, 0]
+            at = first + r
+            if q < r:
+                return jnp.where(plan[OUT_LEFT + at] > 0, a_ref[r, plan[LEFT + at]], 0.0)
+            return jnp.where(plan[OUT_RIGHT + at] > 0, a_ref[r, 3 - plan[LEFT + at]], 0.0)
+
         total = {r: {} for r in range(W)}
         for q in range(-1, W + 1):
             rows = [r for r in (q - 1, q, q + 1) if 0 <= r < W]
             right = right_operand(jnp.concatenate([p_tile(q, 0), p_tile(q, 1)], axis=1))
-            product = matmul(jnp.concatenate([lefts[r, q] for r in rows], axis=0), right)
+            product = matmul(jnp.concatenate([left_operand(a_tile(r, q)) for r in rows], axis=0), right)
             for n, r in enumerate(rows):
                 pair = (product[n * B : (n + 1) * B, :B], product[n * B : (n + 1) * B, B:])
                 spread(total[r], flags[q], q // 3 - r // 3 + 2, pair, SLOTS[r % 3])
-        for r in range(W):
+            r = q - 1
+            if r < 0:
+                continue
             slots = SLOTS[r % 3]
             product = row_product((p_ref[r, 0], p_ref[r, 1]), [total[r][s] for s in slots], half)
             g = r // 3
@@ -142,13 +146,13 @@
                     (1, jnp.where(flags[r], 0.0, two)),
                 ):
                     place = g + delta + 1
-                    if place < 2:
+                    if place < G:
                         stage[buf, place, s + 1 - delta] += value
                     else:
-                        carry[place - 2, s + 1 - delta] += value
-
-    for row in range(2):
-        @pl.when((2 * step - 1 + row >= 0) & (2 * step - 1 + row < 2 * steps))
+                        carry[place - G, s + 1 - delta] += value
+
+    for row in range(G):
+        @pl.when((G * step - 1 + row >= 0) & (G * step - 1 + row < G * steps))
         def _():
             copy_out(step, buf, row).start()
 
@@ -180,9 +184,9 @@
             ],
             out_specs=ANYWHERE,
             scratch_shapes=[
-                VMEM((2, 2, CWIN, HALF, B), F32),
+                VMEM((2, G, CWIN, HALF, B), F32),
                 VMEM((2, CWIN, HALF, B), F32),
-                pltpu.SemaphoreType.DMA((2, 2)),
+                pltpu.SemaphoreType.DMA((2, G)),
             ],
         ),
         out_shape=jax.ShapeDtypeStruct((places, CWIN, HALF, B), F32),
@@ -307,7 +311,7 @@
         out_shape=jax.ShapeDtypeStruct(out_rows.shape, F32),
         input_output_aliases={7: 0},
         compiler_params=pltpu.CompilerParams(
-            dimension_semantics=("arbitrary",), vmem_limit_bytes=32 << 20
+            dimension_semantics=("arbitrary",), vmem_limit_bytes=60 << 20
         ),
         cost_estimate=pl.CostEstimate(flops=2_000_000_000, bytes_accessed=10_000_000, transcendentals=0),
         name="edge_rows",

time: 242 us -> 244 us (level)
  Pallas kernels: 65.5 us -> 81.7 us
  local copies, waits for them, and re-layouts: 16.1 us -> 9.48 us
  waiting for transfers between devices: 124 us -> 119 us
    pallas_call x2, Pallas kernels: 31.4 us -> 48.9 us  [main_product(): pl.pallas_call(functools.partial(main_kernel, half), grid_spec=pltpu.Pref...]
    unnamed x28 -> x8, local copies, waits for them, and re-layouts: 10.7 us -> 1.98 us
    all_to_all x2, waiting for transfers between devices: 42 us -> 37.4 us  [over_y(): return lax.all_to_all(x, 'gy', split_axis=0, concat_axis=0, tiled=True)]
  transfers between devices with their start and end apart: 10 -> 10, of which waited for: 6 -> 8; matrix products, arithmetic and copies ran while one was open for 6% -> 7% of each run, Pallas kernels for 21% -> 28%
where the time goes in v3:
time: 244 us; the launch traced here: 243 us
  waiting for transfers between devices  119 us (49%)
  Pallas kernels  81.7 us (33%)
  starting transfers between devices  22.9 us (9%)
  other arithmetic  10.1 us (4%)
  local copies, waits for them, and re-layouts  9.48 us (4%)
    ppermute x6, waiting for transfers between devices, along_x(): parts.append(lax.ppermute(x[k * depth:(k + 1) * depth], 'gx', pairs))  81.6 us
    pallas_call x2, Pallas kernels, main_product(): pl.pallas_call(functools.partial(main_kernel, half), grid_spec=pltpu.Pref...  48.9 us
    all_to_all x2, waiting for transfers between devices, over_y(): return lax.all_to_all(x, 'gy', split_axis=0, concat_axis=0, tiled=True)  37.4 us
    pallas_call x2, Pallas kernels, edge_product(): pl.pallas_call(functools.partial(edge_kernel, half), grid_spec=pltpu.Pref...  10.7 us
    all_to_all x2, starting transfers between devices, over_y(): return lax.all_to_all(x, 'gy', split_axis=0, concat_axis=0, tiled=True)  10 us
    pallas_call x2, Pallas kernels, move_rows(): pl.pallas_call(move_kernel, grid_spec=pltpu.PrefetchScalarGridSpec(num_sc...  8.89 us
    pallas_call x2, Pallas kernels, put_rows(): pl.pallas_call(functools.partial(put_kernel, half), grid_spec=pltpu.Prefe...  8.87 us
    ppermute x1, starting transfers between devices, shards(): behind = lax.ppermute(down, AXES, below)  8.27 us
  transfers between devices with their start and end apart: 10, of which 8 were waited for; matrix products, arithmetic and copies ran while one was open for 7% of the time, Pallas kernels for 28%

profile of v3, /device:TPU:0, one launch (start us, length us, event | category | flops | bytes accessed | tf_op | source)
XLA Modules:
  0.0 243.5 jit_solution(2147755252304760810)
XLA Ops:
  0.0 4.3 %plan.1 = (s32[384]{0:T(512)}, f32[17,128,128]{2,1,0:T(8,128)}, f32[17,128,128]{2,1,0:T(8,128)}) custom-call(s32[1]{0:T(128)} %bitcast.2.place, s32[3,48]{1,0:T(4,128)} %bitcast.17, s32[48]{0:T(128)} %length.1, f32[48,3,128,128]{3,2,1,0:T(8,128)} %a_ref.3, f32[48,2,128,128]{3,2,1,0:T(8,128)} %p_last.3, s32[48,128]{1,0:T(8,128)} %bitcast.15, s32[16,128]{1,0:T(8,128)} %bitcast.14), custom_call_target="tpu_custom_call" | custom-call | bytes 5000000 | tf_op jit(solution)/shard_map/plan/pallas_call | solution.py:418
  4.3 8.3 %collective-permute-start.1 = (f32[17,128,128]{2,1,0:T(8,128)}, f32[17,128,128]{2,1,0:T(8,128)S(1)}, u32[]{:S(2)}, u32[]{:S(2)}) collective-permute-start(f32[17,128,128]{2,1,0:T(8,128)} %get-tuple-element.10.a_first), channel_id=1, source_target_pairs={{1,0},{2,1},{3,2},{4,3},{5,4},{6,5},{7,6},{8,7},{9,8},{10,9},{11,1... | collective-permute-start | bytes 3342344 | tf_op jit(solution)/shard_map/ppermute | solution.py:536
  12.6 24.4 %triple_product.2.in_rows = f32[32,7,64,128]{3,2,1,0:T(8,128)} custom-call(s32[384]{0:T(512)} %get-tuple-element.8.plan.behind_ref, f32[48,3,128,128]{3,2,1,0:T(8,128)} %a_ref.3, f32[48,2,128,128]{3,2,1,0:T(8,128)} %p_last.3, f32[48,2,128,128]{3,2,1,0:T(8,128)} %p_last.3, f32[48,2,128,128]{3,2,1,0:T(8,128)} %p_last.3, s32[384]{0:T(512)} %get-tuple-element.8.plan.behind_ref), custom_call_target="tpu_custom_call" | custom-call | flops 12000000000 | bytes 20000000 | tf_op jit(solution)/shard_map/triple_product/pallas_call | solution.py:173
  37.1 1.0 copy-done
  38.1 1.0 copy-done.1
  39.1 5.3 %edge_rows.2.behind_ref = f32[32,7,64,128]{3,2,1,0:T(8,128)} custom-call(s32[384]{0:T(512)} %get-tuple-element.8.plan.behind_ref, f32[17,128,128]{2,1,0:T(8,128)} %copy-done, f32[17,128,128]{2,1,0:T(8,128)} %copy-done.1, f32[17,128,128]{2,1,0:T(8,128)} %get-tuple-element.10.a_first, ...), custom_call_target="tpu_custom_call", output_to_operand_aliasing={{}: (7, {})} | custom-call | flops 2000000000 | bytes 10000000 | tf_op jit(solution)/shard_map/edge_rows/pallas_call | solution.py:295
  44.4 5.1 %all-to-all-start.1 = ((f32[32,7,64,128]{3,2,1,0:T(8,128)}), f32[32,7,64,128]{3,2,1,0:T(8,128)}, u32[]{:S(2)}, u32[]{:S(2)}) async-start(f32[32,7,64,128]{3,2,1,0:T(8,128)} %edge_rows.2.behind_ref), calls=%async_computation.1 | async-start | bytes 14680064 | tf_op jit(solution)/shard_map/all_to_all | solution.py:567
  49.5 24.5 %triple_product.3.in_rows = f32[16,7,64,128]{3,2,1,0:T(8,128)} custom-call(s32[384]{0:T(512)} %get-tuple-element.8.plan.behind_ref, f32[48,3,128,128]{3,2,1,0:T(8,128)} %a_ref.3, f32[48,2,128,128]{3,2,1,0:T(8,128)} %p_last.3, f32[48,2,128,128]{3,2,1,0:T(8,128)} %p_last.3, f32[48,2,128,128]{3,2,1,0:T(8,128)} %p_last.3, f32[32,7,64,128]{3,2,1,0:T(8,128)} %edge_rows.2.behind_ref), custom_call_target="tpu_custom_call" | custom-call | flops 12000000000 | bytes 20000000 | tf_op jit(solution)/shard_map/triple_product/pallas_call | solution.py:173
  74.0 5.4 %edge_rows.3 = f32[16,7,64,128]{3,2,1,0:T(8,128)} custom-call(s32[384]{0:T(512)} %get-tuple-element.8.plan.behind_ref, f32[17,128,128]{2,1,0:T(8,128)} %copy-done, f32[17,128,128]{2,1,0:T(8,128)} %copy-done.1, f32[17,128,128]{2,1,0:T(8,128)} %get-tuple-element.10.a_first, f32[17,128,128]{2,1,0:T(8,128)} %get-tuple-element.9.a_last, ...), custom_call_target="tpu_custom_call", output_to_operand_aliasing={{}: (7, {})} | custom-call | flops 2000000000 | bytes 10000000 | tf_op jit(solution)/shard_map/edge_rows/pallas_call | solution.py:295
  79.4 3.6 %fusion.9 = (f32[4,7,64,128]{3,2,1,0:T(8,128)S(1)}, f32[4,7,64,128]{3,2,1,0:T(8,128)}, f32[4,7,64,128]{3,2,1,0:T(8,128)}, f32[4,7,64,128]{3,2,1,0:T(8,128)S(1)}) fusion(f32[16,7,64,128]{3,2,1,0:T(8,128)} %edge_rows.3), kind=kLoop, calls=%fused_computation.41 | loop fusion | bytes 7340032 | tf_op jit(solution)/shard_map/slice | solution.py:570
  83.1 0.8 collective-permute-start.4
  84.4 0.9 collective-permute-start.2
  85.5 0.6 fusion.5.target_ref
  86.8 19.7 %collective-permute-done.4 = f32[4,7,64,128]{3,2,1,0:T(8,128)S(1)} collective-permute-done((f32[4,7,64,128]{3,2,1,0:T(8,128)}, f32[4,7,64,128]{3,2,1,0:T(8,128)S(1)}, u32[]{:S(2)}, u32[]{:S(2)}) %collective-permute-start.4) | collective-permute-done | bytes 917536 | tf_op jit(solution)/shard_map/ppermute | solution.py:573
  106.5 2.5 %collective-permute-done.3 = f32[4,7,64,128]{3,2,1,0:T(8,128)} collective-permute-done((f32[4,7,64,128]{3,2,1,0:T(8,128)}, f32[4,7,64,128]{3,2,1,0:T(8,128)}, u32[]{:S(2)}, u32[]{:S(2)}) %collective-permute-start.3) | collective-permute-done | bytes 917536 | tf_op jit(solution)/shard_map/ppermute | solution.py:573
  109.0 18.3 %collective-permute-done.2 = f32[4,7,64,128]{3,2,1,0:T(8,128)} collective-permute-done((f32[4,7,64,128]{3,2,1,0:T(8,128)S(1)}, f32[4,7,64,128]{3,2,1,0:T(8,128)}, u32[]{:S(2)}, u32[]{:S(2)}) %collective-permute-start.2) | collective-permute-done | bytes 917536 | tf_op jit(solution)/shard_map/ppermute | solution.py:573
  127.3 3.6 %pad_maximum_fusion.rows_in = f32[16,7,64,128]{3,2,1,0:T(8,128)} fusion(f32[4,7,64,128]{3,2,1,0:T(8,128)S(1)} %collective-permute-done.4, f32[4,7,64,128]{3,2,1,0:T(8,128)} %collective-permute-done.3, f32[4,7,64,128]{3,2,1,0:T(8,128)} %collective-permute-done.2, f32[4,7,64,128]{3,2,1,0:T(8,128)S(1)} %get-tuple-element.19), kind=kLoop, calls=%fused_computation | loop fusion | flops 2752512 | bytes 7340032 | tf_op jit(solution)/shard_map/concatenate | solution.py:574
  130.9 4.4 %move_rows.2 = f32[32,7,64,128]{3,2,1,0:T(8,128)} custom-call(s32[16]{0:T(128)} %multiply_add_fusion.source_ref.target_ref, s32[16]{0:T(128)} %fusion.5.target_ref, f32[16,7,64,128]{3,2,1,0:T(8,128)} %pad_maximum_fusion.rows_in), custom_call_target="tpu_custom_call" | custom-call | bytes 8000000 | tf_op jit(solution)/shard_map/move_rows/pallas_call | solution.py:469
  135.4 6.2 %all-to-all-done.1.rows_in = f32[32,7,64,128]{3,2,1,0:T(8,128)} async-done(((f32[32,7,64,128]{3,2,1,0:T(8,128)}), f32[32,7,64,128]{3,2,1,0:T(8,128)}, u32[]{:S(2)}, u32[]{:S(2)}) %all-to-all-start.1) | async-done | bytes 7340064 | tf_op jit(solution)/shard_map/all_to_all | solution.py:567
  141.6 4.9 %all-to-all-start = ((f32[32,7,64,128]{3,2,1,0:T(8,128)}), f32[32,7,64,128]{3,2,1,0:T(8,128)}, u32[]{:S(2)}, u32[]{:S(2)}) async-start(f32[32,7,64,128]{3,2,1,0:T(8,128)} %move_rows.2), calls=%async_computation | async-start | bytes 14680064 | tf_op jit(solution)/shard_map/all_to_all | solution.py:567
  147.1 4.4 %move_rows.3 = f32[16,7,64,128]{3,2,1,0:T(8,128)} custom-call(s32[16]{0:T(128)} %select_reduce_fusion.1.source_ref, s32[16]{0:T(128)} %multiply_add_fusion.source_ref.target_ref, f32[32,7,64,128]{3,2,1,0:T(8,128)} %all-to-all-done.1.rows_in), custom_call_target="tpu_custom_call" | custom-call | bytes 8000000 | tf_op jit(solution)/shard_map/move_rows/pallas_call | solution.py:469
  151.6 3.7 %fusion.8 = (f32[4,7,64,128]{3,2,1,0:T(8,128)S(1)}, f32[4,7,64,128]{3,2,1,0:T(8,128)}, f32[4,7,64,128]{3,2,1,0:T(8,128)}, f32[4,7,64,128]{3,2,1,0:T(8,128)S(1)}) fusion(f32[16,7,64,128]{3,2,1,0:T(8,128)} %move_rows.3), kind=kLoop, calls=%fused_computation.40 | loop fusion | bytes 7340032 | tf_op jit(solution)/shard_map/slice | solution.py:570
  155.2 0.8 collective-permute-start.7
  156.6 0.9 collective-permute-start.5
  157.8 0.7 select_reduce_fusion.2
  158.5 20.1 %collective-permute-done.7 = f32[4,7,64,128]{3,2,1,0:T(8,128)S(1)} collective-permute-done((f32[4,7,64,128]{3,2,1,0:T(8,128)}, f32[4,7,64,128]{3,2,1,0:T(8,128)S(1)}, u32[]{:S(2)}, u32[]{:S(2)}) %collective-permute-start.7) | collective-permute-done | bytes 917536 | tf_op jit(solution)/shard_map/ppermute | solution.py:573
  178.7 2.5 %collective-permute-done.6 = f32[4,7,64,128]{3,2,1,0:T(8,128)} collective-permute-done((f32[4,7,64,128]{3,2,1,0:T(8,128)}, f32[4,7,64,128]{3,2,1,0:T(8,128)}, u32[]{:S(2)}, u32[]{:S(2)}) %collective-permute-start.6) | collective-permute-done | bytes 917536 | tf_op jit(solution)/shard_map/ppermute | solution.py:573
  181.2 18.4 %collective-permute-done.5 = f32[4,7,64,128]{3,2,1,0:T(8,128)} collective-permute-done((f32[4,7,64,128]{3,2,1,0:T(8,128)S(1)}, f32[4,7,64,128]{3,2,1,0:T(8,128)}, u32[]{:S(2)}, u32[]{:S(2)}) %collective-permute-start.5) | collective-permute-done | bytes 917536 | tf_op jit(solution)/shard_map/ppermute | solution.py:573
  199.6 3.6 %pad_maximum_fusion.1.rows = f32[16,7,64,128]{3,2,1,0:T(8,128)} fusion(f32[4,7,64,128]{3,2,1,0:T(8,128)S(1)} %collective-permute-done.7, f32[4,7,64,128]{3,2,1,0:T(8,128)} %collective-permute-done.6, f32[4,7,64,128]{3,2,1,0:T(8,128)} %collective-permute-done.5, f32[4,7,64,128]{3,2,1,0:T(8,128)S(1)} %get-tuple-element.15), kind=kLoop, calls=%fused_computation.1 | loop fusion | flops 2752512 | bytes 7340032 | tf_op jit(solution)/shard_map/concatenate | solution.py:574
  203.2 4.4 %put_rows.2.refs_0_ = f32[16,7,128,128]{3,2,1,0:T(8,128)} custom-call(s32[16]{0:T(128)} %get-tuple-element.11.source, f32[16,7,64,128]{3,2,1,0:T(8,128)} %pad_maximum_fusion.1.rows), custom_call_target="tpu_custom_call" | custom-call | bytes 8000000 | tf_op jit(solution)/shard_map/put_rows/pallas_call | solution.py:500
  207.7 31.2 %all-to-all-done.rows = f32[32,7,64,128]{3,2,1,0:T(8,128)} async-done(((f32[32,7,64,128]{3,2,1,0:T(8,128)}), f32[32,7,64,128]{3,2,1,0:T(8,128)}, u32[]{:S(2)}, u32[]{:S(2)}) %all-to-all-start) | async-done | bytes 7340064 | tf_op jit(solution)/shard_map/all_to_all | solution.py:567
  238.9 4.4 %put_rows.3 = f32[16,7,128,128]{3,2,1,0:T(8,128)} custom-call(s32[16]{0:T(128)} %get-tuple-element.12.source, f32[32,7,64,128]{3,2,1,0:T(8,128)} %all-to-all-done.rows, f32[16,7,128,128]{3,2,1,0:T(8,128)} %put_rows.2.refs_0_), custom_call_target="tpu_custom_call", output_to_operand_aliasing={{}: (2, {})} | custom-call | bytes 8000000 | tf_op jit(solution)/shard_map/put_rows/pallas_call | solution.py:500
  (22 shorter events, 2.9 us)
Async XLA Ops:
  4.3 32.8 %collective-permute-start = (f32[17,128,128]{2,1,0:T(8,128)}, f32[17,128,128]{2,1,0:T(8,128)S(1)}, u32[]{:S(2)}, u32[]{:S(2)}) collective-permute-start(f32[17,128,128]{2,1,0:T(8,128)} %get-tuple-element.9.a_last), channel_id=1, source_target_pairs={{0,1},{1,2},{2,3},{3,4},{4,5},{5,6},{6,7},{7,8},{8,9},{9,10},{10,1... | collective-permute-start | bytes 3342344 | tf_op jit(solution)/shard_map/ppermute | solution.py:535
  4.3 32.7 %collective-permute-start.1 = (f32[17,128,128]{2,1,0:T(8,128)}, f32[17,128,128]{2,1,0:T(8,128)S(1)}, u32[]{:S(2)}, u32[]{:S(2)}) collective-permute-start(f32[17,128,128]{2,1,0:T(8,128)} %get-tuple-element.10.a_first), channel_id=1, source_target_pairs={{1,0},{2,1},{3,2},{4,3},{5,4},{6,5},{7,6},{8,7},{9,8},{10,9},{11,1... | collective-permute-start | bytes 3342344 | tf_op jit(solution)/shard_map/ppermute | solution.py:536
  37.1 1.0 copy-start
  38.1 1.0 copy-start.1
  44.4 97.2 %all-to-all-start.1 = ((f32[32,7,64,128]{3,2,1,0:T(8,128)}), f32[32,7,64,128]{3,2,1,0:T(8,128)}, u32[]{:S(2)}, u32[]{:S(2)}) async-start(f32[32,7,64,128]{3,2,1,0:T(8,128)} %edge_rows.2.behind_ref), calls=%async_computation.1 | async-start | bytes 14680064 | tf_op jit(solution)/shard_map/all_to_all | solution.py:567
  79.4 5.9 %copy-start.2 = (s32[2048]{0:T(1024)S(1)}, s32[2048]{0:T(1024)}, u32[]{:S(2)}) copy-start(s32[2048]{0:T(1024)} %param.11) | copy-start | bytes 24580
  83.1 23.4 %collective-permute-start.4 = (f32[4,7,64,128]{3,2,1,0:T(8,128)}, f32[4,7,64,128]{3,2,1,0:T(8,128)S(1)}, u32[]{:S(2)}, u32[]{:S(2)}) collective-permute-start(f32[4,7,64,128]{3,2,1,0:T(8,128)} %get-tuple-element.20), channel_id=1, source_target_pairs={{0,96},{32,0},{64,32},{96,64},{1,97},{33,1},{65,33},{97,65},{2,98}... | collective-permute-start | bytes 2752520 | tf_op jit(solution)/shard_map/ppermute | solution.py:573
  83.9 25.1 %collective-permute-start.3 = (f32[4,7,64,128]{3,2,1,0:T(8,128)}, f32[4,7,64,128]{3,2,1,0:T(8,128)}, u32[]{:S(2)}, u32[]{:S(2)}) collective-permute-start(f32[4,7,64,128]{3,2,1,0:T(8,128)} %get-tuple-element.21), channel_id=1, source_target_pairs={{0,64},{32,96},{64,0},{96,32},{1,65},{33,97},{65,1},{97,33},{2,66}... | collective-permute-start | bytes 2752520 | tf_op jit(solution)/shard_map/ppermute | solution.py:573
  84.4 42.9 %collective-permute-start.2 = (f32[4,7,64,128]{3,2,1,0:T(8,128)S(1)}, f32[4,7,64,128]{3,2,1,0:T(8,128)}, u32[]{:S(2)}, u32[]{:S(2)}) collective-permute-start(f32[4,7,64,128]{3,2,1,0:T(8,128)S(1)} %get-tuple-element.22), channel_id=1, source_target_pairs={{0,32},{32,64},{64,96},{96,0},{1,33},{33,65},{65,97},{97,1},{2,34}... | collective-permute-start | bytes 2752520 | tf_op jit(solution)/shard_map/ppermute | solution.py:573
  141.6 97.2 %all-to-all-start = ((f32[32,7,64,128]{3,2,1,0:T(8,128)}), f32[32,7,64,128]{3,2,1,0:T(8,128)}, u32[]{:S(2)}, u32[]{:S(2)}) async-start(f32[32,7,64,128]{3,2,1,0:T(8,128)} %move_rows.2), calls=%async_computation | async-start | bytes 14680064 | tf_op jit(solution)/shard_map/all_to_all | solution.py:567
  151.6 6.2 %copy-start.3 = (s32[16]{0:T(128)S(1)}, s32[16]{0:T(128)}, u32[]{:S(2)}) copy-start(s32[16]{0:T(128)} %multiply_add_fusion.source_ref.target_ref) | copy-start | bytes 196
  155.2 23.4 %collective-permute-start.7 = (f32[4,7,64,128]{3,2,1,0:T(8,128)}, f32[4,7,64,128]{3,2,1,0:T(8,128)S(1)}, u32[]{:S(2)}, u32[]{:S(2)}) collective-permute-start(f32[4,7,64,128]{3,2,1,0:T(8,128)} %get-tuple-element.16), channel_id=1, source_target_pairs={{0,96},{32,0},{64,32},{96,64},{1,97},{33,1},{65,33},{97,65},{2,98}... | collective-permute-start | bytes 2752520 | tf_op jit(solution)/shard_map/ppermute | solution.py:573
  156.1 25.1 %collective-permute-start.6 = (f32[4,7,64,128]{3,2,1,0:T(8,128)}, f32[4,7,64,128]{3,2,1,0:T(8,128)}, u32[]{:S(2)}, u32[]{:S(2)}) collective-permute-start(f32[4,7,64,128]{3,2,1,0:T(8,128)} %get-tuple-element.17), channel_id=1, source_target_pairs={{0,64},{32,96},{64,0},{96,32},{1,65},{33,97},{65,1},{97,33},{2,66}... | collective-permute-start | bytes 2752520 | tf_op jit(solution)/shard_map/ppermute | solution.py:573
  156.6 43.0 %collective-permute-start.5 = (f32[4,7,64,128]{3,2,1,0:T(8,128)S(1)}, f32[4,7,64,128]{3,2,1,0:T(8,128)}, u32[]{:S(2)}, u32[]{:S(2)}) collective-permute-start(f32[4,7,64,128]{3,2,1,0:T(8,128)S(1)} %get-tuple-element.18), channel_id=1, source_target_pairs={{0,32},{32,64},{64,96},{96,0},{1,33},{33,65},{65,97},{97,1},{2,34}... | collective-permute-start | bytes 2752520 | tf_op jit(solution)/shard_map/ppermute | solution.py:573

commit v4 on v2

--- a/solution.py
+++ b/solution.py
@@ -96,12 +96,13 @@
     def _():
         carry[...] = jnp.zeros_like(carry)
 
-    stage[buf, 0] = carry[0]
-    stage[buf, 1] = carry[1]
+    @pl.when(step == steps)
+    def _():
+        stage[buf, 0] = carry[0]
 
     @pl.when(step < steps)
     def _():
-        carry[...] = jnp.zeros_like(carry)
+        sums = {(place, w): carry[place, w] for place in range(2) for w in range(CWIN)}
         first = step * W
         flags = {q: plan[first + q + 4] > 0 for q in range(-1, W + 1)}
 
@@ -141,11 +142,17 @@
                     (0, jnp.where(flags[r], two, one)),
                     (1, jnp.where(flags[r], 0.0, two)),
                 ):
-                    place = g + delta + 1
-                    if place < 2:
-                        stage[buf, place, s + 1 - delta] += value
-                    else:
-                        carry[place - 2, s + 1 - delta] += value
+                    key = (g + delta + 1, s + 1 - delta)
+                    sums[key] = value if key not in sums else sums[key] + value
+        for place in range(4):
+            for w in range(CWIN):
+                value = sums.get((place, w))
+                if value is None:
+                    value = jnp.zeros((HALF, B), F32)
+                if place < 2:
+                    stage[buf, place, w] = value
+                else:
+                    carry[place - 2, w] = value
 
     for row in range(2):
         @pl.when((2 * step - 1 + row >= 0) & (2 * step - 1 + row < 2 * steps))
@@ -307,7 +314,7 @@
         out_shape=jax.ShapeDtypeStruct(out_rows.shape, F32),
         input_output_aliases={7: 0},
         compiler_params=pltpu.CompilerParams(
-            dimension_semantics=("arbitrary",), vmem_limit_bytes=32 << 20
+            dimension_semantics=("arbitrary",), vmem_limit_bytes=60 << 20
         ),
         cost_estimate=pl.CostEstimate(flops=2_000_000_000, bytes_accessed=10_000_000, transcendentals=0),
         name="edge_rows",

time: 242 us -> 235 us (0.971)
  local copies, waits for them, and re-layouts: 16.1 us -> 9.48 us
  waiting for transfers between devices: 124 us -> 128 us
    unnamed x28 -> x8, local copies, waits for them, and re-layouts: 10.7 us -> 1.98 us
    all_to_all x2, waiting for transfers between devices: 42 us -> 46 us  [over_y(): return lax.all_to_all(x, 'gy', split_axis=0, concat_axis=0, tiled=True)]
  transfers between devices with their start and end apart: 10 -> 10, of which waited for: 6 -> 8; matrix products, arithmetic and copies ran while one was open for 6% -> 8% of each run, Pallas kernels for 21% -> 21%
where the time goes in v4:
time: 235 us; the launch traced here: 234 us
  waiting for transfers between devices  128 us (54%)
  Pallas kernels  63.7 us (27%)
  starting transfers between devices  22.9 us (10%)
  other arithmetic  10.1 us (4%)
  local copies, waits for them, and re-layouts  9.48 us (4%)
    ppermute x6, waiting for transfers between devices, along_x(): parts.append(lax.ppermute(x[k * depth:(k + 1) * depth], 'gx', pairs))  82 us
    all_to_all x2, waiting for transfers between devices, over_y(): return lax.all_to_all(x, 'gy', split_axis=0, concat_axis=0, tiled=True)  46 us
    pallas_call x2, Pallas kernels, main_product(): pl.pallas_call(functools.partial(main_kernel, half), grid_spec=pltpu.Pref...  31 us
    pallas_call x2, Pallas kernels, edge_product(): pl.pallas_call(functools.partial(edge_kernel, half), grid_spec=pltpu.Pref...  10.7 us
    all_to_all x2, starting transfers between devices, over_y(): return lax.all_to_all(x, 'gy', split_axis=0, concat_axis=0, tiled=True)  9.87 us
    pallas_call x2, Pallas kernels, move_rows(): pl.pallas_call(move_kernel, grid_spec=pltpu.PrefetchScalarGridSpec(num_sc...  8.93 us
    pallas_call x2, Pallas kernels, put_rows(): pl.pallas_call(functools.partial(put_kernel, half), grid_spec=pltpu.Prefe...  8.87 us
    ppermute x1, starting transfers between devices, shards(): behind = lax.ppermute(down, AXES, below)  8.27 us
  transfers between devices with their start and end apart: 10, of which 8 were waited for; matrix products, arithmetic and copies ran while one was open for 8% of the time, Pallas kernels for 21%

profile of v4, /device:TPU:0, one launch (start us, length us, event | category | flops | bytes accessed | tf_op | source)
XLA Modules:
  0.0 234.4 jit_solution(8348856682048538349)
XLA Ops:
  0.0 4.3 %plan.1 = (s32[384]{0:T(512)}, f32[17,128,128]{2,1,0:T(8,128)}, f32[17,128,128]{2,1,0:T(8,128)}) custom-call(s32[1]{0:T(128)} %bitcast.2.place, s32[3,48]{1,0:T(4,128)} %bitcast.17, s32[48]{0:T(128)} %length.1, f32[48,3,128,128]{3,2,1,0:T(8,128)} %a_ref.3, f32[48,2,128,128]{3,2,1,0:T(8,128)} %p_last.3, s32[48,128]{1,0:T(8,128)} %bitcast.15, s32[16,128]{1,0:T(8,128)} %bitcast.14), custom_call_target="tpu_custom_call" | custom-call | bytes 5000000 | tf_op jit(solution)/shard_map/plan/pallas_call | solution.py:421
  4.4 8.3 %collective-permute-start.1 = (f32[17,128,128]{2,1,0:T(8,128)}, f32[17,128,128]{2,1,0:T(8,128)S(1)}, u32[]{:S(2)}, u32[]{:S(2)}) collective-permute-start(f32[17,128,128]{2,1,0:T(8,128)} %get-tuple-element.10.a_first), channel_id=1, source_target_pairs={{1,0},{2,1},{3,2},{4,3},{5,4},{6,5},{7,6},{8,7},{9,8},{10,9},{11,1... | collective-permute-start | bytes 3342344 | tf_op jit(solution)/shard_map/ppermute | solution.py:539
  12.6 15.5 %triple_product.2.in_rows = f32[32,7,64,128]{3,2,1,0:T(8,128)} custom-call(s32[384]{0:T(512)} %get-tuple-element.8.plan.behind_ref, f32[48,3,128,128]{3,2,1,0:T(8,128)} %a_ref.3, f32[48,2,128,128]{3,2,1,0:T(8,128)} %p_last.3, f32[48,2,128,128]{3,2,1,0:T(8,128)} %p_last.3, f32[48,2,128,128]{3,2,1,0:T(8,128)} %p_last.3, s32[384]{0:T(512)} %get-tuple-element.8.plan.behind_ref), custom_call_target="tpu_custom_call" | custom-call | flops 12000000000 | bytes 20000000 | tf_op jit(solution)/shard_map/triple_product/pallas_call | solution.py:176
  28.2 1.0 copy-done
  29.2 1.0 copy-done.1
  30.1 5.3 %edge_rows.2.behind_ref = f32[32,7,64,128]{3,2,1,0:T(8,128)} custom-call(s32[384]{0:T(512)} %get-tuple-element.8.plan.behind_ref, f32[17,128,128]{2,1,0:T(8,128)} %copy-done, f32[17,128,128]{2,1,0:T(8,128)} %copy-done.1, f32[17,128,128]{2,1,0:T(8,128)} %get-tuple-element.10.a_first, ...), custom_call_target="tpu_custom_call", output_to_operand_aliasing={{}: (7, {})} | custom-call | flops 2000000000 | bytes 10000000 | tf_op jit(solution)/shard_map/edge_rows/pallas_call | solution.py:298
  35.4 4.9 %all-to-all-start.1 = ((f32[32,7,64,128]{3,2,1,0:T(8,128)}), f32[32,7,64,128]{3,2,1,0:T(8,128)}, u32[]{:S(2)}, u32[]{:S(2)}) async-start(f32[32,7,64,128]{3,2,1,0:T(8,128)} %edge_rows.2.behind_ref), calls=%async_computation.1 | async-start | bytes 14680064 | tf_op jit(solution)/shard_map/all_to_all | solution.py:570
  40.4 15.4 %triple_product.3.in_rows = f32[16,7,64,128]{3,2,1,0:T(8,128)} custom-call(s32[384]{0:T(512)} %get-tuple-element.8.plan.behind_ref, f32[48,3,128,128]{3,2,1,0:T(8,128)} %a_ref.3, f32[48,2,128,128]{3,2,1,0:T(8,128)} %p_last.3, f32[48,2,128,128]{3,2,1,0:T(8,128)} %p_last.3, f32[48,2,128,128]{3,2,1,0:T(8,128)} %p_last.3, f32[32,7,64,128]{3,2,1,0:T(8,128)} %edge_rows.2.behind_ref), custom_call_target="tpu_custom_call" | custom-call | flops 12000000000 | bytes 20000000 | tf_op jit(solution)/shard_map/triple_product/pallas_call | solution.py:176
  55.8 5.5 %edge_rows.3 = f32[16,7,64,128]{3,2,1,0:T(8,128)} custom-call(s32[384]{0:T(512)} %get-tuple-element.8.plan.behind_ref, f32[17,128,128]{2,1,0:T(8,128)} %copy-done, f32[17,128,128]{2,1,0:T(8,128)} %copy-done.1, f32[17,128,128]{2,1,0:T(8,128)} %get-tuple-element.10.a_first, f32[17,128,128]{2,1,0:T(8,128)} %get-tuple-element.9.a_last, ...), custom_call_target="tpu_custom_call", output_to_operand_aliasing={{}: (7, {})} | custom-call | flops 2000000000 | bytes 10000000 | tf_op jit(solution)/shard_map/edge_rows/pallas_call | solution.py:298
  61.3 3.6 %fusion.9 = (f32[4,7,64,128]{3,2,1,0:T(8,128)S(1)}, f32[4,7,64,128]{3,2,1,0:T(8,128)}, f32[4,7,64,128]{3,2,1,0:T(8,128)}, f32[4,7,64,128]{3,2,1,0:T(8,128)S(1)}) fusion(f32[16,7,64,128]{3,2,1,0:T(8,128)} %edge_rows.3), kind=kLoop, calls=%fused_computation.41 | loop fusion | bytes 7340032 | tf_op jit(solution)/shard_map/slice | solution.py:573
  64.9 1.5 collective-permute-start.4
  66.4 0.9 collective-permute-start.2
  67.4 0.6 fusion.5.target_ref
  68.8 19.6 %collective-permute-done.4 = f32[4,7,64,128]{3,2,1,0:T(8,128)S(1)} collective-permute-done((f32[4,7,64,128]{3,2,1,0:T(8,128)}, f32[4,7,64,128]{3,2,1,0:T(8,128)S(1)}, u32[]{:S(2)}, u32[]{:S(2)}) %collective-permute-start.4) | collective-permute-done | bytes 917536 | tf_op jit(solution)/shard_map/ppermute | solution.py:576
  88.4 3.1 %collective-permute-done.3 = f32[4,7,64,128]{3,2,1,0:T(8,128)} collective-permute-done((f32[4,7,64,128]{3,2,1,0:T(8,128)}, f32[4,7,64,128]{3,2,1,0:T(8,128)}, u32[]{:S(2)}, u32[]{:S(2)}) %collective-permute-start.3) | collective-permute-done | bytes 917536 | tf_op jit(solution)/shard_map/ppermute | solution.py:576
  91.5 18.1 %collective-permute-done.2 = f32[4,7,64,128]{3,2,1,0:T(8,128)} collective-permute-done((f32[4,7,64,128]{3,2,1,0:T(8,128)S(1)}, f32[4,7,64,128]{3,2,1,0:T(8,128)}, u32[]{:S(2)}, u32[]{:S(2)}) %collective-permute-start.2) | collective-permute-done | bytes 917536 | tf_op jit(solution)/shard_map/ppermute | solution.py:576
  109.6 3.6 %pad_maximum_fusion.rows_in = f32[16,7,64,128]{3,2,1,0:T(8,128)} fusion(f32[4,7,64,128]{3,2,1,0:T(8,128)S(1)} %collective-permute-done.4, f32[4,7,64,128]{3,2,1,0:T(8,128)} %collective-permute-done.3, f32[4,7,64,128]{3,2,1,0:T(8,128)} %collective-permute-done.2, f32[4,7,64,128]{3,2,1,0:T(8,128)S(1)} %get-tuple-element.19), kind=kLoop, calls=%fused_computation | loop fusion | flops 2752512 | bytes 7340032 | tf_op jit(solution)/shard_map/concatenate | solution.py:577
  113.2 4.5 %move_rows.2 = f32[32,7,64,128]{3,2,1,0:T(8,128)} custom-call(s32[16]{0:T(128)} %multiply_add_fusion.source_ref.target_ref, s32[16]{0:T(128)} %fusion.5.target_ref, f32[16,7,64,128]{3,2,1,0:T(8,128)} %pad_maximum_fusion.rows_in), custom_call_target="tpu_custom_call" | custom-call | bytes 8000000 | tf_op jit(solution)/shard_map/move_rows/pallas_call | solution.py:472
  117.7 14.9 %all-to-all-done.1.rows_in = f32[32,7,64,128]{3,2,1,0:T(8,128)} async-done(((f32[32,7,64,128]{3,2,1,0:T(8,128)}), f32[32,7,64,128]{3,2,1,0:T(8,128)}, u32[]{:S(2)}, u32[]{:S(2)}) %all-to-all-start.1) | async-done | bytes 7340064 | tf_op jit(solution)/shard_map/all_to_all | solution.py:570
  132.7 4.9 %all-to-all-start = ((f32[32,7,64,128]{3,2,1,0:T(8,128)}), f32[32,7,64,128]{3,2,1,0:T(8,128)}, u32[]{:S(2)}, u32[]{:S(2)}) async-start(f32[32,7,64,128]{3,2,1,0:T(8,128)} %move_rows.2), calls=%async_computation | async-start | bytes 14680064 | tf_op jit(solution)/shard_map/all_to_all | solution.py:570
  138.2 4.4 %move_rows.3 = f32[16,7,64,128]{3,2,1,0:T(8,128)} custom-call(s32[16]{0:T(128)} %select_reduce_fusion.1.source_ref, s32[16]{0:T(128)} %multiply_add_fusion.source_ref.target_ref, f32[32,7,64,128]{3,2,1,0:T(8,128)} %all-to-all-done.1.rows_in), custom_call_target="tpu_custom_call" | custom-call | bytes 8000000 | tf_op jit(solution)/shard_map/move_rows/pallas_call | solution.py:472
  142.6 3.7 %fusion.8 = (f32[4,7,64,128]{3,2,1,0:T(8,128)S(1)}, f32[4,7,64,128]{3,2,1,0:T(8,128)}, f32[4,7,64,128]{3,2,1,0:T(8,128)}, f32[4,7,64,128]{3,2,1,0:T(8,128)S(1)}) fusion(f32[16,7,64,128]{3,2,1,0:T(8,128)} %move_rows.3), kind=kLoop, calls=%fused_computation.40 | loop fusion | bytes 7340032 | tf_op jit(solution)/shard_map/slice | solution.py:573
  146.3 1.5 collective-permute-start.7
  147.8 0.9 collective-permute-start.5
  149.0 0.7 select_reduce_fusion.2
  149.7 20.0 %collective-permute-done.7 = f32[4,7,64,128]{3,2,1,0:T(8,128)S(1)} collective-permute-done((f32[4,7,64,128]{3,2,1,0:T(8,128)}, f32[4,7,64,128]{3,2,1,0:T(8,128)S(1)}, u32[]{:S(2)}, u32[]{:S(2)}) %collective-permute-start.7) | collective-permute-done | bytes 917536 | tf_op jit(solution)/shard_map/ppermute | solution.py:576
  169.7 3.1 %collective-permute-done.6 = f32[4,7,64,128]{3,2,1,0:T(8,128)} collective-permute-done((f32[4,7,64,128]{3,2,1,0:T(8,128)}, f32[4,7,64,128]{3,2,1,0:T(8,128)}, u32[]{:S(2)}, u32[]{:S(2)}) %collective-permute-start.6) | collective-permute-done | bytes 917536 | tf_op jit(solution)/shard_map/ppermute | solution.py:576
  172.9 18.0 %collective-permute-done.5 = f32[4,7,64,128]{3,2,1,0:T(8,128)} collective-permute-done((f32[4,7,64,128]{3,2,1,0:T(8,128)S(1)}, f32[4,7,64,128]{3,2,1,0:T(8,128)}, u32[]{:S(2)}, u32[]{:S(2)}) %collective-permute-start.5) | collective-permute-done | bytes 917536 | tf_op jit(solution)/shard_map/ppermute | solution.py:576
  190.9 3.6 %pad_maximum_fusion.1.rows = f32[16,7,64,128]{3,2,1,0:T(8,128)} fusion(f32[4,7,64,128]{3,2,1,0:T(8,128)S(1)} %collective-permute-done.7, f32[4,7,64,128]{3,2,1,0:T(8,128)} %collective-permute-done.6, f32[4,7,64,128]{3,2,1,0:T(8,128)} %collective-permute-done.5, f32[4,7,64,128]{3,2,1,0:T(8,128)S(1)} %get-tuple-element.15), kind=kLoop, calls=%fused_computation.1 | loop fusion | flops 2752512 | bytes 7340032 | tf_op jit(solution)/shard_map/concatenate | solution.py:577
  194.5 4.4 %put_rows.2.refs_0_ = f32[16,7,128,128]{3,2,1,0:T(8,128)} custom-call(s32[16]{0:T(128)} %get-tuple-element.11.source, f32[16,7,64,128]{3,2,1,0:T(8,128)} %pad_maximum_fusion.1.rows), custom_call_target="tpu_custom_call" | custom-call | bytes 8000000 | tf_op jit(solution)/shard_map/put_rows/pallas_call | solution.py:503
  198.9 31.0 %all-to-all-done.rows = f32[32,7,64,128]{3,2,1,0:T(8,128)} async-done(((f32[32,7,64,128]{3,2,1,0:T(8,128)}), f32[32,7,64,128]{3,2,1,0:T(8,128)}, u32[]{:S(2)}, u32[]{:S(2)}) %all-to-all-start) | async-done | bytes 7340064 | tf_op jit(solution)/shard_map/all_to_all | solution.py:570
  229.9 4.4 %put_rows.3 = f32[16,7,128,128]{3,2,1,0:T(8,128)} custom-call(s32[16]{0:T(128)} %get-tuple-element.12.source, f32[32,7,64,128]{3,2,1,0:T(8,128)} %all-to-all-done.rows, f32[16,7,128,128]{3,2,1,0:T(8,128)} %put_rows.2.refs_0_), custom_call_target="tpu_custom_call", output_to_operand_aliasing={{}: (2, {})} | custom-call | bytes 8000000 | tf_op jit(solution)/shard_map/put_rows/pallas_call | solution.py:503
  (22 shorter events, 1.9 us)
Async XLA Ops:
  4.3 23.9 %collective-permute-start = (f32[17,128,128]{2,1,0:T(8,128)}, f32[17,128,128]{2,1,0:T(8,128)S(1)}, u32[]{:S(2)}, u32[]{:S(2)}) collective-permute-start(f32[17,128,128]{2,1,0:T(8,128)} %get-tuple-element.9.a_last), channel_id=1, source_target_pairs={{0,1},{1,2},{2,3},{3,4},{4,5},{5,6},{6,7},{7,8},{8,9},{9,10},{10,1... | collective-permute-start | bytes 3342344 | tf_op jit(solution)/shard_map/ppermute | solution.py:538
  4.4 23.8 %collective-permute-start.1 = (f32[17,128,128]{2,1,0:T(8,128)}, f32[17,128,128]{2,1,0:T(8,128)S(1)}, u32[]{:S(2)}, u32[]{:S(2)}) collective-permute-start(f32[17,128,128]{2,1,0:T(8,128)} %get-tuple-element.10.a_first), channel_id=1, source_target_pairs={{1,0},{2,1},{3,2},{4,3},{5,4},{6,5},{7,6},{8,7},{9,8},{10,9},{11,1... | collective-permute-start | bytes 3342344 | tf_op jit(solution)/shard_map/ppermute | solution.py:539
  28.2 1.0 copy-start
  29.2 1.0 copy-start.1
  35.4 97.2 %all-to-all-start.1 = ((f32[32,7,64,128]{3,2,1,0:T(8,128)}), f32[32,7,64,128]{3,2,1,0:T(8,128)}, u32[]{:S(2)}, u32[]{:S(2)}) async-start(f32[32,7,64,128]{3,2,1,0:T(8,128)} %edge_rows.2.behind_ref), calls=%async_computation.1 | async-start | bytes 14680064 | tf_op jit(solution)/shard_map/all_to_all | solution.py:570
  61.3 6.0 %copy-start.2 = (s32[2048]{0:T(1024)S(1)}, s32[2048]{0:T(1024)}, u32[]{:S(2)}) copy-start(s32[2048]{0:T(1024)} %param.11) | copy-start | bytes 24580
  64.9 23.4 %collective-permute-start.4 = (f32[4,7,64,128]{3,2,1,0:T(8,128)}, f32[4,7,64,128]{3,2,1,0:T(8,128)S(1)}, u32[]{:S(2)}, u32[]{:S(2)}) collective-permute-start(f32[4,7,64,128]{3,2,1,0:T(8,128)} %get-tuple-element.20), channel_id=1, source_target_pairs={{0,96},{32,0},{64,32},{96,64},{1,97},{33,1},{65,33},{97,65},{2,98}... | collective-permute-start | bytes 2752520 | tf_op jit(solution)/shard_map/ppermute | solution.py:576
  66.4 25.0 %collective-permute-start.3 = (f32[4,7,64,128]{3,2,1,0:T(8,128)}, f32[4,7,64,128]{3,2,1,0:T(8,128)}, u32[]{:S(2)}, u32[]{:S(2)}) collective-permute-start(f32[4,7,64,128]{3,2,1,0:T(8,128)} %get-tuple-element.21), channel_id=1, source_target_pairs={{0,64},{32,96},{64,0},{96,32},{1,65},{33,97},{65,1},{97,33},{2,66}... | collective-permute-start | bytes 2752520 | tf_op jit(solution)/shard_map/ppermute | solution.py:576
  66.4 43.2 %collective-permute-start.2 = (f32[4,7,64,128]{3,2,1,0:T(8,128)S(1)}, f32[4,7,64,128]{3,2,1,0:T(8,128)}, u32[]{:S(2)}, u32[]{:S(2)}) collective-permute-start(f32[4,7,64,128]{3,2,1,0:T(8,128)S(1)} %get-tuple-element.22), channel_id=1, source_target_pairs={{0,32},{32,64},{64,96},{96,0},{1,33},{33,65},{65,97},{97,1},{2,34}... | collective-permute-start | bytes 2752520 | tf_op jit(solution)/shard_map/ppermute | solution.py:576
  132.7 97.2 %all-to-all-start = ((f32[32,7,64,128]{3,2,1,0:T(8,128)}), f32[32,7,64,128]{3,2,1,0:T(8,128)}, u32[]{:S(2)}, u32[]{:S(2)}) async-start(f32[32,7,64,128]{3,2,1,0:T(8,128)} %move_rows.2), calls=%async_computation | async-start | bytes 14680064 | tf_op jit(solution)/shard_map/all_to_all | solution.py:570
  142.6 6.4 %copy-start.3 = (s32[16]{0:T(128)S(1)}, s32[16]{0:T(128)}, u32[]{:S(2)}) copy-start(s32[16]{0:T(128)} %multiply_add_fusion.source_ref.target_ref) | copy-start | bytes 196
  146.3 23.4 %collective-permute-start.7 = (f32[4,7,64,128]{3,2,1,0:T(8,128)}, f32[4,7,64,128]{3,2,1,0:T(8,128)S(1)}, u32[]{:S(2)}, u32[]{:S(2)}) collective-permute-start(f32[4,7,64,128]{3,2,1,0:T(8,128)} %get-tuple-element.16), channel_id=1, source_target_pairs={{0,96},{32,0},{64,32},{96,64},{1,97},{33,1},{65,33},{97,65},{2,98}... | collective-permute-start | bytes 2752520 | tf_op jit(solution)/shard_map/ppermute | solution.py:576
  147.8 25.1 %collective-permute-start.6 = (f32[4,7,64,128]{3,2,1,0:T(8,128)}, f32[4,7,64,128]{3,2,1,0:T(8,128)}, u32[]{:S(2)}, u32[]{:S(2)}) collective-permute-start(f32[4,7,64,128]{3,2,1,0:T(8,128)} %get-tuple-element.17), channel_id=1, source_target_pairs={{0,64},{32,96},{64,0},{96,32},{1,65},{33,97},{65,1},{97,33},{2,66}... | collective-permute-start | bytes 2752520 | tf_op jit(solution)/shard_map/ppermute | solution.py:576
  147.8 43.0 %collective-permute-start.5 = (f32[4,7,64,128]{3,2,1,0:T(8,128)S(1)}, f32[4,7,64,128]{3,2,1,0:T(8,128)}, u32[]{:S(2)}, u32[]{:S(2)}) collective-permute-start(f32[4,7,64,128]{3,2,1,0:T(8,128)S(1)} %get-tuple-element.18), channel_id=1, source_target_pairs={{0,32},{32,64},{64,96},{96,0},{1,33},{33,65},{65,97},{97,1},{2,34}... | collective-permute-start | bytes 2752520 | tf_op jit(solution)/shard_map/ppermute | solution.py:576

commit v5 on v4

--- a/solution.py
+++ b/solution.py
@@ -12,7 +12,8 @@
 LANES = 128
 CWIN = 7
 CB = 16
-W = 6
+W = 12
+G = W // 3
 BF = jnp.bfloat16
 F32 = jnp.float32
 SMEM = pltpu.SMEM
@@ -78,13 +79,13 @@
     buf = lax.rem(step, 2)
 
     def copy_out(at, which, row):
-        c = 2 * at - 1 + row
+        c = G * at - 1 + row
         return pltpu.make_async_copy(stage.at[which, row], out.at[plan[SLOTS_AT[half] + c]], sems.at[which, row])
 
     def drain(at):
         which = lax.rem(at, 2)
-        for row in range(2):
-            @pl.when((2 * at - 1 + row >= 0) & (2 * at - 1 + row < 2 * steps))
+        for row in range(G):
+            @pl.when((G * at - 1 + row >= 0) & (G * at - 1 + row < G * steps))
             def _():
                 copy_out(at, which, row).wait()
 
@@ -144,18 +145,18 @@
                 ):
                     key = (g + delta + 1, s + 1 - delta)
                     sums[key] = value if key not in sums else sums[key] + value
-        for place in range(4):
+        for place in range(G + 2):
             for w in range(CWIN):
                 value = sums.get((place, w))
                 if value is None:
                     value = jnp.zeros((HALF, B), F32)
-                if place < 2:
+                if place < G:
                     stage[buf, place, w] = value
                 else:
-                    carry[place - 2, w] = value
-
-    for row in range(2):
-        @pl.when((2 * step - 1 + row >= 0) & (2 * step - 1 + row < 2 * steps))
+                    carry[place - G, w] = value
+
+    for row in range(G):
+        @pl.when((G * step - 1 + row >= 0) & (G * step - 1 + row < G * steps))
         def _():
             copy_out(step, buf, row).start()
 
@@ -187,9 +188,9 @@
             ],
             out_specs=ANYWHERE,
             scratch_shapes=[
-                VMEM((2, 2, CWIN, HALF, B), F32),
+                VMEM((2, G, CWIN, HALF, B), F32),
                 VMEM((2, CWIN, HALF, B), F32),
-                pltpu.SemaphoreType.DMA((2, 2)),
+                pltpu.SemaphoreType.DMA((2, G)),
             ],
         ),
         out_shape=jax.ShapeDtypeStruct((places, CWIN, HALF, B), F32),
@@ -399,7 +400,7 @@
         used[shift] = used[shift] + 1
         return carry
 
-    lax.fori_loop(0, coarse, slot, 0)
+    lax.fori_loop(0, coarse, slot, 0, unroll=4)
     for k, (here, there, on) in enumerate(sends):
         if on is None:
             pltpu.make_async_copy(here, there, sem.at[3 + k]).wait()

time: 235 us -> 235 us (level)
  transfers between devices with their start and end apart: 10 -> 10, of which waited for: 8 -> 6; matrix products, arithmetic and copies ran while one was open for 8% -> 8% of each run, Pallas kernels for 21% -> 21%
where the time goes in v5:
time: 235 us; the launch traced here: 234 us
  waiting for transfers between devices  127 us (54%)
  Pallas kernels  62.8 us (27%)
  starting transfers between devices  24 us (10%)
  other arithmetic  10.1 us (4%)
  local copies, waits for them, and re-layouts  9.48 us (4%)
    ppermute x6, waiting for transfers between devices, along_x(): parts.append(lax.ppermute(x[k * depth:(k + 1) * depth], 'gx', pairs))  82 us
    all_to_all x2, waiting for transfers between devices, over_y(): return lax.all_to_all(x, 'gy', split_axis=0, concat_axis=0, tiled=True)  45.5 us
    pallas_call x2, Pallas kernels, main_product(): pl.pallas_call(functools.partial(main_kernel, half), grid_spec=pltpu.Pref...  30.1 us
    pallas_call x2, Pallas kernels, edge_product(): pl.pallas_call(functools.partial(edge_kernel, half), grid_spec=pltpu.Pref...  10.7 us
    all_to_all x2, starting transfers between devices, over_y(): return lax.all_to_all(x, 'gy', split_axis=0, concat_axis=0, tiled=True)  10 us
    pallas_call x2, Pallas kernels, move_rows(): pl.pallas_call(move_kernel, grid_spec=pltpu.PrefetchScalarGridSpec(num_sc...  8.88 us
    pallas_call x2, Pallas kernels, put_rows(): pl.pallas_call(functools.partial(put_kernel, half), grid_spec=pltpu.Prefe...  8.87 us
    ppermute x1, starting transfers between devices, shards(): behind = lax.ppermute(down, AXES, below)  8.27 us
  transfers between devices with their start and end apart: 10, of which 6 were waited for; matrix products, arithmetic and copies ran while one was open for 8% of the time, Pallas kernels for 21%

profile of v5, /device:TPU:0, one launch (start us, length us, event | category | flops | bytes accessed | tf_op | source)
XLA Modules:
  0.0 234.2 jit_solution(360291935602329905)
XLA Ops:
  0.0 4.2 %plan.1 = (s32[384]{0:T(512)}, f32[17,128,128]{2,1,0:T(8,128)}, f32[17,128,128]{2,1,0:T(8,128)}) custom-call(s32[1]{0:T(128)} %bitcast.2.place, s32[3,48]{1,0:T(4,128)} %bitcast.17, s32[48]{0:T(128)} %length.1, f32[48,3,128,128]{3,2,1,0:T(8,128)} %a_ref.3, f32[48,2,128,128]{3,2,1,0:T(8,128)} %p_last.3, s32[48,128]{1,0:T(8,128)} %bitcast.15, s32[16,128]{1,0:T(8,128)} %bitcast.14), custom_call_target="tpu_custom_call" | custom-call | bytes 5000000 | tf_op jit(solution)/shard_map/plan/pallas_call | solution.py:422
  4.3 8.3 %collective-permute-start.1 = (f32[17,128,128]{2,1,0:T(8,128)}, f32[17,128,128]{2,1,0:T(8,128)S(1)}, u32[]{:S(2)}, u32[]{:S(2)}) collective-permute-start(f32[17,128,128]{2,1,0:T(8,128)} %get-tuple-element.10.a_first), channel_id=1, source_target_pairs={{1,0},{2,1},{3,2},{4,3},{5,4},{6,5},{7,6},{8,7},{9,8},{10,9},{11,1... | collective-permute-start | bytes 3342344 | tf_op jit(solution)/shard_map/ppermute | solution.py:540
  12.6 15.0 %triple_product.2.in_rows = f32[32,7,64,128]{3,2,1,0:T(8,128)} custom-call(s32[384]{0:T(512)} %get-tuple-element.8.plan.behind_ref, f32[48,3,128,128]{3,2,1,0:T(8,128)} %a_ref.3, f32[48,2,128,128]{3,2,1,0:T(8,128)} %p_last.3, f32[48,2,128,128]{3,2,1,0:T(8,128)} %p_last.3, f32[48,2,128,128]{3,2,1,0:T(8,128)} %p_last.3, s32[384]{0:T(512)} %get-tuple-element.8.plan.behind_ref), custom_call_target="tpu_custom_call" | custom-call | flops 12000000000 | bytes 20000000 | tf_op jit(solution)/shard_map/triple_product/pallas_call | solution.py:177
  27.6 1.0 copy-done
  28.6 1.0 copy-done.1
  29.6 5.3 %edge_rows.2.behind_ref = f32[32,7,64,128]{3,2,1,0:T(8,128)} custom-call(s32[384]{0:T(512)} %get-tuple-element.8.plan.behind_ref, f32[17,128,128]{2,1,0:T(8,128)} %copy-done, f32[17,128,128]{2,1,0:T(8,128)} %copy-done.1, f32[17,128,128]{2,1,0:T(8,128)} %get-tuple-element.10.a_first, ...), custom_call_target="tpu_custom_call", output_to_operand_aliasing={{}: (7, {})} | custom-call | flops 2000000000 | bytes 10000000 | tf_op jit(solution)/shard_map/edge_rows/pallas_call | solution.py:299
  34.9 4.9 %all-to-all-start.1 = ((f32[32,7,64,128]{3,2,1,0:T(8,128)}), f32[32,7,64,128]{3,2,1,0:T(8,128)}, u32[]{:S(2)}, u32[]{:S(2)}) async-start(f32[32,7,64,128]{3,2,1,0:T(8,128)} %edge_rows.2.behind_ref), calls=%async_computation.1 | async-start | bytes 14680064 | tf_op jit(solution)/shard_map/all_to_all | solution.py:571
  39.9 15.1 %triple_product.3.in_rows = f32[16,7,64,128]{3,2,1,0:T(8,128)} custom-call(s32[384]{0:T(512)} %get-tuple-element.8.plan.behind_ref, f32[48,3,128,128]{3,2,1,0:T(8,128)} %a_ref.3, f32[48,2,128,128]{3,2,1,0:T(8,128)} %p_last.3, f32[48,2,128,128]{3,2,1,0:T(8,128)} %p_last.3, f32[48,2,128,128]{3,2,1,0:T(8,128)} %p_last.3, f32[32,7,64,128]{3,2,1,0:T(8,128)} %edge_rows.2.behind_ref), custom_call_target="tpu_custom_call" | custom-call | flops 12000000000 | bytes 20000000 | tf_op jit(solution)/shard_map/triple_product/pallas_call | solution.py:177
  55.0 5.4 %edge_rows.3 = f32[16,7,64,128]{3,2,1,0:T(8,128)} custom-call(s32[384]{0:T(512)} %get-tuple-element.8.plan.behind_ref, f32[17,128,128]{2,1,0:T(8,128)} %copy-done, f32[17,128,128]{2,1,0:T(8,128)} %copy-done.1, f32[17,128,128]{2,1,0:T(8,128)} %get-tuple-element.10.a_first, f32[17,128,128]{2,1,0:T(8,128)} %get-tuple-element.9.a_last, ...), custom_call_target="tpu_custom_call", output_to_operand_aliasing={{}: (7, {})} | custom-call | flops 2000000000 | bytes 10000000 | tf_op jit(solution)/shard_map/edge_rows/pallas_call | solution.py:299
  60.4 3.6 %fusion.9 = (f32[4,7,64,128]{3,2,1,0:T(8,128)S(1)}, f32[4,7,64,128]{3,2,1,0:T(8,128)}, f32[4,7,64,128]{3,2,1,0:T(8,128)}, f32[4,7,64,128]{3,2,1,0:T(8,128)S(1)}) fusion(f32[16,7,64,128]{3,2,1,0:T(8,128)} %edge_rows.3), kind=kLoop, calls=%fused_computation.41 | loop fusion | bytes 7340032 | tf_op jit(solution)/shard_map/slice | solution.py:574
  64.0 1.9 collective-permute-start.4
  66.0 0.9 collective-permute-start.2
  67.0 0.6 fusion.5.target_ref
  67.7 0.6 multiply_add_fusion.source_ref.target_ref
  68.3 37.6 %collective-permute-done.4 = f32[4,7,64,128]{3,2,1,0:T(8,128)S(1)} collective-permute-done((f32[4,7,64,128]{3,2,1,0:T(8,128)}, f32[4,7,64,128]{3,2,1,0:T(8,128)S(1)}, u32[]{:S(2)}, u32[]{:S(2)}) %collective-permute-start.4) | collective-permute-done | bytes 917536 | tf_op jit(solution)/shard_map/ppermute | solution.py:577
  106.0 3.2 %collective-permute-done.2 = f32[4,7,64,128]{3,2,1,0:T(8,128)} collective-permute-done((f32[4,7,64,128]{3,2,1,0:T(8,128)S(1)}, f32[4,7,64,128]{3,2,1,0:T(8,128)}, u32[]{:S(2)}, u32[]{:S(2)}) %collective-permute-start.2) | collective-permute-done | bytes 917536 | tf_op jit(solution)/shard_map/ppermute | solution.py:577
  109.1 3.6 %pad_maximum_fusion.rows_in = f32[16,7,64,128]{3,2,1,0:T(8,128)} fusion(f32[4,7,64,128]{3,2,1,0:T(8,128)S(1)} %collective-permute-done.4, f32[4,7,64,128]{3,2,1,0:T(8,128)} %collective-permute-done.3, f32[4,7,64,128]{3,2,1,0:T(8,128)} %collective-permute-done.2, f32[4,7,64,128]{3,2,1,0:T(8,128)S(1)} %get-tuple-element.19), kind=kLoop, calls=%fused_computation | loop fusion | flops 2752512 | bytes 7340032 | tf_op jit(solution)/shard_map/concatenate | solution.py:578
  112.8 4.4 %move_rows.2 = f32[32,7,64,128]{3,2,1,0:T(8,128)} custom-call(s32[16]{0:T(128)} %multiply_add_fusion.source_ref.target_ref, s32[16]{0:T(128)} %fusion.5.target_ref, f32[16,7,64,128]{3,2,1,0:T(8,128)} %pad_maximum_fusion.rows_in), custom_call_target="tpu_custom_call" | custom-call | bytes 8000000 | tf_op jit(solution)/shard_map/move_rows/pallas_call | solution.py:473
  117.2 15.0 %all-to-all-done.1.rows_in = f32[32,7,64,128]{3,2,1,0:T(8,128)} async-done(((f32[32,7,64,128]{3,2,1,0:T(8,128)}), f32[32,7,64,128]{3,2,1,0:T(8,128)}, u32[]{:S(2)}, u32[]{:S(2)}) %all-to-all-start.1) | async-done | bytes 7340064 | tf_op jit(solution)/shard_map/all_to_all | solution.py:571
  132.2 5.1 %all-to-all-start = ((f32[32,7,64,128]{3,2,1,0:T(8,128)}), f32[32,7,64,128]{3,2,1,0:T(8,128)}, u32[]{:S(2)}, u32[]{:S(2)}) async-start(f32[32,7,64,128]{3,2,1,0:T(8,128)} %move_rows.2), calls=%async_computation | async-start | bytes 14680064 | tf_op jit(solution)/shard_map/all_to_all | solution.py:571
  137.3 0.6 select_reduce_fusion.1.source_ref
  137.8 4.4 %move_rows.3 = f32[16,7,64,128]{3,2,1,0:T(8,128)} custom-call(s32[16]{0:T(128)} %select_reduce_fusion.1.source_ref, s32[16]{0:T(128)} %multiply_add_fusion.source_ref.target_ref, f32[32,7,64,128]{3,2,1,0:T(8,128)} %all-to-all-done.1.rows_in), custom_call_target="tpu_custom_call" | custom-call | bytes 8000000 | tf_op jit(solution)/shard_map/move_rows/pallas_call | solution.py:473
  142.3 3.7 %fusion.8 = (f32[4,7,64,128]{3,2,1,0:T(8,128)S(1)}, f32[4,7,64,128]{3,2,1,0:T(8,128)}, f32[4,7,64,128]{3,2,1,0:T(8,128)}, f32[4,7,64,128]{3,2,1,0:T(8,128)S(1)}) fusion(f32[16,7,64,128]{3,2,1,0:T(8,128)} %move_rows.3), kind=kLoop, calls=%fused_computation.40 | loop fusion | bytes 7340032 | tf_op jit(solution)/shard_map/slice | solution.py:574
  146.0 1.9 collective-permute-start.7
  147.9 0.9 collective-permute-start.5
  149.1 0.7 select_reduce_fusion.2
  149.8 38.0 %collective-permute-done.7 = f32[4,7,64,128]{3,2,1,0:T(8,128)S(1)} collective-permute-done((f32[4,7,64,128]{3,2,1,0:T(8,128)}, f32[4,7,64,128]{3,2,1,0:T(8,128)S(1)}, u32[]{:S(2)}, u32[]{:S(2)}) %collective-permute-start.7) | collective-permute-done | bytes 917536 | tf_op jit(solution)/shard_map/ppermute | solution.py:577
  187.8 3.2 %collective-permute-done.5 = f32[4,7,64,128]{3,2,1,0:T(8,128)} collective-permute-done((f32[4,7,64,128]{3,2,1,0:T(8,128)S(1)}, f32[4,7,64,128]{3,2,1,0:T(8,128)}, u32[]{:S(2)}, u32[]{:S(2)}) %collective-permute-start.5) | collective-permute-done | bytes 917536 | tf_op jit(solution)/shard_map/ppermute | solution.py:577
  190.9 3.6 %pad_maximum_fusion.1.rows = f32[16,7,64,128]{3,2,1,0:T(8,128)} fusion(f32[4,7,64,128]{3,2,1,0:T(8,128)S(1)} %collective-permute-done.7, f32[4,7,64,128]{3,2,1,0:T(8,128)} %collective-permute-done.6, f32[4,7,64,128]{3,2,1,0:T(8,128)} %collective-permute-done.5, f32[4,7,64,128]{3,2,1,0:T(8,128)S(1)} %get-tuple-element.15), kind=kLoop, calls=%fused_computation.1 | loop fusion | flops 2752512 | bytes 7340032 | tf_op jit(solution)/shard_map/concatenate | solution.py:578
  194.6 4.4 %put_rows.2.refs_0_ = f32[16,7,128,128]{3,2,1,0:T(8,128)} custom-call(s32[16]{0:T(128)} %get-tuple-element.11.source, f32[16,7,64,128]{3,2,1,0:T(8,128)} %pad_maximum_fusion.1.rows), custom_call_target="tpu_custom_call" | custom-call | bytes 8000000 | tf_op jit(solution)/shard_map/put_rows/pallas_call | solution.py:504
  199.0 30.6 %all-to-all-done.rows = f32[32,7,64,128]{3,2,1,0:T(8,128)} async-done(((f32[32,7,64,128]{3,2,1,0:T(8,128)}), f32[32,7,64,128]{3,2,1,0:T(8,128)}, u32[]{:S(2)}, u32[]{:S(2)}) %all-to-all-start) | async-done | bytes 7340064 | tf_op jit(solution)/shard_map/all_to_all | solution.py:571
  229.6 4.4 %put_rows.3 = f32[16,7,128,128]{3,2,1,0:T(8,128)} custom-call(s32[16]{0:T(128)} %get-tuple-element.12.source, f32[32,7,64,128]{3,2,1,0:T(8,128)} %all-to-all-done.rows, f32[16,7,128,128]{3,2,1,0:T(8,128)} %put_rows.2.refs_0_), custom_call_target="tpu_custom_call", output_to_operand_aliasing={{}: (2, {})} | custom-call | bytes 8000000 | tf_op jit(solution)/shard_map/put_rows/pallas_call | solution.py:504
  (22 shorter events, 0.7 us)
Async XLA Ops:
  4.2 23.4 %collective-permute-start = (f32[17,128,128]{2,1,0:T(8,128)}, f32[17,128,128]{2,1,0:T(8,128)S(1)}, u32[]{:S(2)}, u32[]{:S(2)}) collective-permute-start(f32[17,128,128]{2,1,0:T(8,128)} %get-tuple-element.9.a_last), channel_id=1, source_target_pairs={{0,1},{1,2},{2,3},{3,4},{4,5},{5,6},{6,7},{7,8},{8,9},{9,10},{10,1... | collective-permute-start | bytes 3342344 | tf_op jit(solution)/shard_map/ppermute | solution.py:539
  4.3 23.3 %collective-permute-start.1 = (f32[17,128,128]{2,1,0:T(8,128)}, f32[17,128,128]{2,1,0:T(8,128)S(1)}, u32[]{:S(2)}, u32[]{:S(2)}) collective-permute-start(f32[17,128,128]{2,1,0:T(8,128)} %get-tuple-element.10.a_first), channel_id=1, source_target_pairs={{1,0},{2,1},{3,2},{4,3},{5,4},{6,5},{7,6},{8,7},{9,8},{10,9},{11,1... | collective-permute-start | bytes 3342344 | tf_op jit(solution)/shard_map/ppermute | solution.py:540
  27.6 1.0 copy-start
  28.6 1.0 copy-start.1
  34.9 97.2 %all-to-all-start.1 = ((f32[32,7,64,128]{3,2,1,0:T(8,128)}), f32[32,7,64,128]{3,2,1,0:T(8,128)}, u32[]{:S(2)}, u32[]{:S(2)}) async-start(f32[32,7,64,128]{3,2,1,0:T(8,128)} %edge_rows.2.behind_ref), calls=%async_computation.1 | async-start | bytes 14680064 | tf_op jit(solution)/shard_map/all_to_all | solution.py:571
  60.4 6.4 %copy-start.2 = (s32[2048]{0:T(1024)S(1)}, s32[2048]{0:T(1024)}, u32[]{:S(2)}) copy-start(s32[2048]{0:T(1024)} %param.11) | copy-start | bytes 24580
  64.0 41.9 %collective-permute-start.4 = (f32[4,7,64,128]{3,2,1,0:T(8,128)}, f32[4,7,64,128]{3,2,1,0:T(8,128)S(1)}, u32[]{:S(2)}, u32[]{:S(2)}) collective-permute-start(f32[4,7,64,128]{3,2,1,0:T(8,128)} %get-tuple-element.20), channel_id=1, source_target_pairs={{0,96},{32,0},{64,32},{96,64},{1,97},{33,1},{65,33},{97,65},{2,98}... | collective-permute-start | bytes 2752520 | tf_op jit(solution)/shard_map/ppermute | solution.py:577
  66.0 40.0 %collective-permute-start.3 = (f32[4,7,64,128]{3,2,1,0:T(8,128)}, f32[4,7,64,128]{3,2,1,0:T(8,128)}, u32[]{:S(2)}, u32[]{:S(2)}) collective-permute-start(f32[4,7,64,128]{3,2,1,0:T(8,128)} %get-tuple-element.21), channel_id=1, source_target_pairs={{0,64},{32,96},{64,0},{96,32},{1,65},{33,97},{65,1},{97,33},{2,66}... | collective-permute-start | bytes 2752520 | tf_op jit(solution)/shard_map/ppermute | solution.py:577
  66.0 43.2 %collective-permute-start.2 = (f32[4,7,64,128]{3,2,1,0:T(8,128)S(1)}, f32[4,7,64,128]{3,2,1,0:T(8,128)}, u32[]{:S(2)}, u32[]{:S(2)}) collective-permute-start(f32[4,7,64,128]{3,2,1,0:T(8,128)S(1)} %get-tuple-element.22), channel_id=1, source_target_pairs={{0,32},{32,64},{64,96},{96,0},{1,33},{33,65},{65,97},{97,1},{2,34}... | collective-permute-start | bytes 2752520 | tf_op jit(solution)/shard_map/ppermute | solution.py:577
  132.2 97.4 %all-to-all-start = ((f32[32,7,64,128]{3,2,1,0:T(8,128)}), f32[32,7,64,128]{3,2,1,0:T(8,128)}, u32[]{:S(2)}, u32[]{:S(2)}) async-start(f32[32,7,64,128]{3,2,1,0:T(8,128)} %move_rows.2), calls=%async_computation | async-start | bytes 14680064 | tf_op jit(solution)/shard_map/all_to_all | solution.py:571
  142.3 6.8 %copy-start.3 = (s32[16]{0:T(128)S(1)}, s32[16]{0:T(128)}, u32[]{:S(2)}) copy-start(s32[16]{0:T(128)} %multiply_add_fusion.source_ref.target_ref) | copy-start | bytes 196
  146.0 41.8 %collective-permute-start.7 = (f32[4,7,64,128]{3,2,1,0:T(8,128)}, f32[4,7,64,128]{3,2,1,0:T(8,128)S(1)}, u32[]{:S(2)}, u32[]{:S(2)}) collective-permute-start(f32[4,7,64,128]{3,2,1,0:T(8,128)} %get-tuple-element.16), channel_id=1, source_target_pairs={{0,96},{32,0},{64,32},{96,64},{1,97},{33,1},{65,33},{97,65},{2,98}... | collective-permute-start | bytes 2752520 | tf_op jit(solution)/shard_map/ppermute | solution.py:577
  147.9 39.9 %collective-permute-start.6 = (f32[4,7,64,128]{3,2,1,0:T(8,128)}, f32[4,7,64,128]{3,2,1,0:T(8,128)}, u32[]{:S(2)}, u32[]{:S(2)}) collective-permute-start(f32[4,7,64,128]{3,2,1,0:T(8,128)} %get-tuple-element.17), channel_id=1, source_target_pairs={{0,64},{32,96},{64,0},{96,32},{1,65},{33,97},{65,1},{97,33},{2,66}... | collective-permute-start | bytes 2752520 | tf_op jit(solution)/shard_map/ppermute | solution.py:577
  147.9 43.0 %collective-permute-start.5 = (f32[4,7,64,128]{3,2,1,0:T(8,128)S(1)}, f32[4,7,64,128]{3,2,1,0:T(8,128)}, u32[]{:S(2)}, u32[]{:S(2)}) collective-permute-start(f32[4,7,64,128]{3,2,1,0:T(8,128)S(1)} %get-tuple-element.18), channel_id=1, source_target_pairs={{0,32},{32,64},{64,96},{96,0},{1,33},{33,65},{65,97},{97,1},{2,34}... | collective-permute-start | bytes 2752520 | tf_op jit(solution)/shard_map/ppermute | solution.py:577

commit v6 on v5

--- a/solution.py
+++ b/solution.py
@@ -68,6 +68,16 @@
 SLOTS = {0: (0, 1, 2, 3), 1: (1, 2, 3), 2: (1, 2, 3, 4)}
 
 
+def staggered(items, produce, consume):
+    held = None
+    for item in items:
+        made = produce(item)
+        if held is not None:
+            consume(*held)
+        held = item, made
+    consume(*held)
+
+
 def main_kernel(
     half, plan,
     a_ref, p_ref, before_ref, after_ref, behind_ref,
@@ -124,18 +134,26 @@
             for k in range(3):
                 lefts[r, r + k - 1] = left_operand(tiles[k])
         total = {r: {} for r in range(W)}
-        for q in range(-1, W + 1):
-            rows = [r for r in (q - 1, q, q + 1) if 0 <= r < W]
+
+        def rows_of(q):
+            return [r for r in (q - 1, q, q + 1) if 0 <= r < W]
+
+        def column(q):
             right = right_operand(jnp.concatenate([p_tile(q, 0), p_tile(q, 1)], axis=1))
-            product = matmul(jnp.concatenate([lefts[r, q] for r in rows], axis=0), right)
-            for n, r in enumerate(rows):
+            return matmul(jnp.concatenate([lefts[r, q] for r in rows_of(q)], axis=0), right)
+
+        def add_column(q, product):
+            for n, r in enumerate(rows_of(q)):
                 pair = (product[n * B : (n + 1) * B, :B], product[n * B : (n + 1) * B, B:])
                 spread(total[r], flags[q], q // 3 - r // 3 + 2, pair, SLOTS[r % 3])
-        for r in range(W):
-            slots = SLOTS[r % 3]
-            product = row_product((p_ref[r, 0], p_ref[r, 1]), [total[r][s] for s in slots], half)
-            g = r // 3
-            for n, s in enumerate(slots):
+
+        staggered(range(-1, W + 1), column, add_column)
+
+        def row(r):
+            return row_product((p_ref[r, 0], p_ref[r, 1]), [total[r][s] for s in SLOTS[r % 3]], half)
+
+        def add_row(r, product):
+            for n, s in enumerate(SLOTS[r % 3]):
                 one = product[:HALF, n * B : (n + 1) * B]
                 two = product[HALF:, n * B : (n + 1) * B]
                 for delta, value in (
@@ -143,8 +161,10 @@
                     (0, jnp.where(flags[r], two, one)),
                     (1, jnp.where(flags[r], 0.0, two)),
                 ):
-                    key = (g + delta + 1, s + 1 - delta)
+                    key = (r // 3 + delta + 1, s + 1 - delta)
                     sums[key] = value if key not in sums else sums[key] + value
+
+        staggered(range(W), row, add_row)
         for place in range(G + 2):
             for w in range(CWIN):
                 value = sums.get((place, w))
@@ -222,7 +242,7 @@
     for n in range(4):
         copy(n, True).start()
 
-    sums = []
+    sums, sides = [], []
     for side in range(2):
         halo = (before, after)[side]
         a_edge = (a_first, a_last)[side]
@@ -251,6 +271,8 @@
                 base = q // 3 - r // 3 + 2
                 slots = SLOTS[r % 3] if r != near else (base - 1, base, base + 1)
                 spread(total[r], flags[q], base, pair, slots)
+        sides.append((total, flags, p_at, near, own_flag))
+    for side, (total, flags, p_at, near, own_flag) in enumerate(sides):
         outer, inner = {}, {}
 
         def put(target, w, value):

time: 235 us -> 235 us (level)
  no operation moved by 1% of the time
where the time goes in v6:
time: 235 us; the launch traced here: 234 us
  waiting for transfers between devices  128 us (54%)
  Pallas kernels  62.5 us (27%)
  starting transfers between devices  24 us (10%)
  other arithmetic  10.1 us (4%)
  local copies, waits for them, and re-layouts  9.48 us (4%)
    ppermute x6, waiting for transfers between devices, along_x(): parts.append(lax.ppermute(x[k * depth:(k + 1) * depth], 'gx', pairs))  82 us
    all_to_all x2, waiting for transfers between devices, over_y(): return lax.all_to_all(x, 'gy', split_axis=0, concat_axis=0, tiled=True)  45.6 us
    pallas_call x2, Pallas kernels, main_product(): pl.pallas_call(functools.partial(main_kernel, half), grid_spec=pltpu.Pref...  30.1 us
    pallas_call x2, Pallas kernels, edge_product(): pl.pallas_call(functools.partial(edge_kernel, half), grid_spec=pltpu.Pref...  10.4 us
    all_to_all x2, starting transfers between devices, over_y(): return lax.all_to_all(x, 'gy', split_axis=0, concat_axis=0, tiled=True)  10 us
    pallas_call x2, Pallas kernels, move_rows(): pl.pallas_call(move_kernel, grid_spec=pltpu.PrefetchScalarGridSpec(num_sc...  8.91 us
    pallas_call x2, Pallas kernels, put_rows(): pl.pallas_call(functools.partial(put_kernel, half), grid_spec=pltpu.Prefe...  8.87 us
    ppermute x1, starting transfers between devices, shards(): behind = lax.ppermute(down, AXES, below)  8.27 us
  transfers between devices with their start and end apart: 10, of which 6 were waited for; matrix products, arithmetic and copies ran while one was open for 8% of the time, Pallas kernels for 21%

profile of v6, /device:TPU:0, one launch (start us, length us, event | category | flops | bytes accessed | tf_op | source)
XLA Modules:
  0.0 234.1 jit_solution(2067609313986156528)
XLA Ops:
  0.0 4.2 %plan.1 = (s32[384]{0:T(512)}, f32[17,128,128]{2,1,0:T(8,128)}, f32[17,128,128]{2,1,0:T(8,128)}) custom-call(s32[1]{0:T(128)} %bitcast.2.place, s32[3,48]{1,0:T(4,128)} %bitcast.17, s32[48]{0:T(128)} %length.1, f32[48,3,128,128]{3,2,1,0:T(8,128)} %a_ref.3, f32[48,2,128,128]{3,2,1,0:T(8,128)} %p_last.3, s32[48,128]{1,0:T(8,128)} %bitcast.15, s32[16,128]{1,0:T(8,128)} %bitcast.14), custom_call_target="tpu_custom_call" | custom-call | bytes 5000000 | tf_op jit(solution)/shard_map/plan/pallas_call | solution.py:444
  4.3 8.3 %collective-permute-start.1 = (f32[17,128,128]{2,1,0:T(8,128)}, f32[17,128,128]{2,1,0:T(8,128)S(1)}, u32[]{:S(2)}, u32[]{:S(2)}) collective-permute-start(f32[17,128,128]{2,1,0:T(8,128)} %get-tuple-element.10.a_first), channel_id=1, source_target_pairs={{1,0},{2,1},{3,2},{4,3},{5,4},{6,5},{7,6},{8,7},{9,8},{10,9},{11,1... | collective-permute-start | bytes 3342344 | tf_op jit(solution)/shard_map/ppermute | solution.py:562
  12.6 15.0 %triple_product.2.in_rows = f32[32,7,64,128]{3,2,1,0:T(8,128)} custom-call(s32[384]{0:T(512)} %get-tuple-element.8.plan.behind_ref, f32[48,3,128,128]{3,2,1,0:T(8,128)} %a_ref.3, f32[48,2,128,128]{3,2,1,0:T(8,128)} %p_last.3, f32[48,2,128,128]{3,2,1,0:T(8,128)} %p_last.3, f32[48,2,128,128]{3,2,1,0:T(8,128)} %p_last.3, s32[384]{0:T(512)} %get-tuple-element.8.plan.behind_ref), custom_call_target="tpu_custom_call" | custom-call | flops 12000000000 | bytes 20000000 | tf_op jit(solution)/shard_map/triple_product/pallas_call | solution.py:197
  27.6 1.0 copy-done
  28.6 1.0 copy-done.1
  29.6 5.2 %edge_rows.2.behind_ref = f32[32,7,64,128]{3,2,1,0:T(8,128)} custom-call(s32[384]{0:T(512)} %get-tuple-element.8.plan.behind_ref, f32[17,128,128]{2,1,0:T(8,128)} %copy-done, f32[17,128,128]{2,1,0:T(8,128)} %copy-done.1, f32[17,128,128]{2,1,0:T(8,128)} %get-tuple-element.10.a_first, ...), custom_call_target="tpu_custom_call", output_to_operand_aliasing={{}: (7, {})} | custom-call | flops 2000000000 | bytes 10000000 | tf_op jit(solution)/shard_map/edge_rows/pallas_call | solution.py:321
  34.8 4.9 %all-to-all-start.1 = ((f32[32,7,64,128]{3,2,1,0:T(8,128)}), f32[32,7,64,128]{3,2,1,0:T(8,128)}, u32[]{:S(2)}, u32[]{:S(2)}) async-start(f32[32,7,64,128]{3,2,1,0:T(8,128)} %edge_rows.2.behind_ref), calls=%async_computation.1 | async-start | bytes 14680064 | tf_op jit(solution)/shard_map/all_to_all | solution.py:593
  39.7 15.1 %triple_product.3.in_rows = f32[16,7,64,128]{3,2,1,0:T(8,128)} custom-call(s32[384]{0:T(512)} %get-tuple-element.8.plan.behind_ref, f32[48,3,128,128]{3,2,1,0:T(8,128)} %a_ref.3, f32[48,2,128,128]{3,2,1,0:T(8,128)} %p_last.3, f32[48,2,128,128]{3,2,1,0:T(8,128)} %p_last.3, f32[48,2,128,128]{3,2,1,0:T(8,128)} %p_last.3, f32[32,7,64,128]{3,2,1,0:T(8,128)} %edge_rows.2.behind_ref), custom_call_target="tpu_custom_call" | custom-call | flops 12000000000 | bytes 20000000 | tf_op jit(solution)/shard_map/triple_product/pallas_call | solution.py:197
  54.8 5.2 %edge_rows.3 = f32[16,7,64,128]{3,2,1,0:T(8,128)} custom-call(s32[384]{0:T(512)} %get-tuple-element.8.plan.behind_ref, f32[17,128,128]{2,1,0:T(8,128)} %copy-done, f32[17,128,128]{2,1,0:T(8,128)} %copy-done.1, f32[17,128,128]{2,1,0:T(8,128)} %get-tuple-element.10.a_first, f32[17,128,128]{2,1,0:T(8,128)} %get-tuple-element.9.a_last, ...), custom_call_target="tpu_custom_call", output_to_operand_aliasing={{}: (7, {})} | custom-call | flops 2000000000 | bytes 10000000 | tf_op jit(solution)/shard_map/edge_rows/pallas_call | solution.py:321
  60.1 3.6 %fusion.9 = (f32[4,7,64,128]{3,2,1,0:T(8,128)S(1)}, f32[4,7,64,128]{3,2,1,0:T(8,128)}, f32[4,7,64,128]{3,2,1,0:T(8,128)}, f32[4,7,64,128]{3,2,1,0:T(8,128)S(1)}) fusion(f32[16,7,64,128]{3,2,1,0:T(8,128)} %edge_rows.3), kind=kLoop, calls=%fused_computation.41 | loop fusion | bytes 7340032 | tf_op jit(solution)/shard_map/slice | solution.py:596
  63.7 2.0 collective-permute-start.4
  65.7 0.9 collective-permute-start.2
  66.7 0.6 fusion.5.target_ref
  67.5 0.6 multiply_add_fusion.source_ref.target_ref
  68.0 37.6 %collective-permute-done.4 = f32[4,7,64,128]{3,2,1,0:T(8,128)S(1)} collective-permute-done((f32[4,7,64,128]{3,2,1,0:T(8,128)}, f32[4,7,64,128]{3,2,1,0:T(8,128)S(1)}, u32[]{:S(2)}, u32[]{:S(2)}) %collective-permute-start.4) | collective-permute-done | bytes 917536 | tf_op jit(solution)/shard_map/ppermute | solution.py:599
  105.7 3.2 %collective-permute-done.2 = f32[4,7,64,128]{3,2,1,0:T(8,128)} collective-permute-done((f32[4,7,64,128]{3,2,1,0:T(8,128)S(1)}, f32[4,7,64,128]{3,2,1,0:T(8,128)}, u32[]{:S(2)}, u32[]{:S(2)}) %collective-permute-start.2) | collective-permute-done | bytes 917536 | tf_op jit(solution)/shard_map/ppermute | solution.py:599
  108.9 3.6 %pad_maximum_fusion.rows_in = f32[16,7,64,128]{3,2,1,0:T(8,128)} fusion(f32[4,7,64,128]{3,2,1,0:T(8,128)S(1)} %collective-permute-done.4, f32[4,7,64,128]{3,2,1,0:T(8,128)} %collective-permute-done.3, f32[4,7,64,128]{3,2,1,0:T(8,128)} %collective-permute-done.2, f32[4,7,64,128]{3,2,1,0:T(8,128)S(1)} %get-tuple-element.19), kind=kLoop, calls=%fused_computation | loop fusion | flops 2752512 | bytes 7340032 | tf_op jit(solution)/shard_map/concatenate | solution.py:600
  112.5 4.5 %move_rows.2 = f32[32,7,64,128]{3,2,1,0:T(8,128)} custom-call(s32[16]{0:T(128)} %multiply_add_fusion.source_ref.target_ref, s32[16]{0:T(128)} %fusion.5.target_ref, f32[16,7,64,128]{3,2,1,0:T(8,128)} %pad_maximum_fusion.rows_in), custom_call_target="tpu_custom_call" | custom-call | bytes 8000000 | tf_op jit(solution)/shard_map/move_rows/pallas_call | solution.py:495
  116.9 15.1 %all-to-all-done.1.rows_in = f32[32,7,64,128]{3,2,1,0:T(8,128)} async-done(((f32[32,7,64,128]{3,2,1,0:T(8,128)}), f32[32,7,64,128]{3,2,1,0:T(8,128)}, u32[]{:S(2)}, u32[]{:S(2)}) %all-to-all-start.1) | async-done | bytes 7340064 | tf_op jit(solution)/shard_map/all_to_all | solution.py:593
  132.0 5.1 %all-to-all-start = ((f32[32,7,64,128]{3,2,1,0:T(8,128)}), f32[32,7,64,128]{3,2,1,0:T(8,128)}, u32[]{:S(2)}, u32[]{:S(2)}) async-start(f32[32,7,64,128]{3,2,1,0:T(8,128)} %move_rows.2), calls=%async_computation | async-start | bytes 14680064 | tf_op jit(solution)/shard_map/all_to_all | solution.py:593
  137.2 0.6 select_reduce_fusion.1.source_ref
  137.7 4.4 %move_rows.3 = f32[16,7,64,128]{3,2,1,0:T(8,128)} custom-call(s32[16]{0:T(128)} %select_reduce_fusion.1.source_ref, s32[16]{0:T(128)} %multiply_add_fusion.source_ref.target_ref, f32[32,7,64,128]{3,2,1,0:T(8,128)} %all-to-all-done.1.rows_in), custom_call_target="tpu_custom_call" | custom-call | bytes 8000000 | tf_op jit(solution)/shard_map/move_rows/pallas_call | solution.py:495
  142.2 3.7 %fusion.8 = (f32[4,7,64,128]{3,2,1,0:T(8,128)S(1)}, f32[4,7,64,128]{3,2,1,0:T(8,128)}, f32[4,7,64,128]{3,2,1,0:T(8,128)}, f32[4,7,64,128]{3,2,1,0:T(8,128)S(1)}) fusion(f32[16,7,64,128]{3,2,1,0:T(8,128)} %move_rows.3), kind=kLoop, calls=%fused_computation.40 | loop fusion | bytes 7340032 | tf_op jit(solution)/shard_map/slice | solution.py:596
  145.9 1.9 collective-permute-start.7
  147.8 0.9 collective-permute-start.5
  149.0 0.7 select_reduce_fusion.2
  149.7 38.0 %collective-permute-done.7 = f32[4,7,64,128]{3,2,1,0:T(8,128)S(1)} collective-permute-done((f32[4,7,64,128]{3,2,1,0:T(8,128)}, f32[4,7,64,128]{3,2,1,0:T(8,128)S(1)}, u32[]{:S(2)}, u32[]{:S(2)}) %collective-permute-start.7) | collective-permute-done | bytes 917536 | tf_op jit(solution)/shard_map/ppermute | solution.py:599
  187.7 3.2 %collective-permute-done.5 = f32[4,7,64,128]{3,2,1,0:T(8,128)} collective-permute-done((f32[4,7,64,128]{3,2,1,0:T(8,128)S(1)}, f32[4,7,64,128]{3,2,1,0:T(8,128)}, u32[]{:S(2)}, u32[]{:S(2)}) %collective-permute-start.5) | collective-permute-done | bytes 917536 | tf_op jit(solution)/shard_map/ppermute | solution.py:599
  190.9 3.6 %pad_maximum_fusion.1.rows = f32[16,7,64,128]{3,2,1,0:T(8,128)} fusion(f32[4,7,64,128]{3,2,1,0:T(8,128)S(1)} %collective-permute-done.7, f32[4,7,64,128]{3,2,1,0:T(8,128)} %collective-permute-done.6, f32[4,7,64,128]{3,2,1,0:T(8,128)} %collective-permute-done.5, f32[4,7,64,128]{3,2,1,0:T(8,128)S(1)} %get-tuple-element.15), kind=kLoop, calls=%fused_computation.1 | loop fusion | flops 2752512 | bytes 7340032 | tf_op jit(solution)/shard_map/concatenate | solution.py:600
  194.5 4.4 %put_rows.2.refs_0_ = f32[16,7,128,128]{3,2,1,0:T(8,128)} custom-call(s32[16]{0:T(128)} %get-tuple-element.11.source, f32[16,7,64,128]{3,2,1,0:T(8,128)} %pad_maximum_fusion.1.rows), custom_call_target="tpu_custom_call" | custom-call | bytes 8000000 | tf_op jit(solution)/shard_map/put_rows/pallas_call | solution.py:526
  198.9 30.6 %all-to-all-done.rows = f32[32,7,64,128]{3,2,1,0:T(8,128)} async-done(((f32[32,7,64,128]{3,2,1,0:T(8,128)}), f32[32,7,64,128]{3,2,1,0:T(8,128)}, u32[]{:S(2)}, u32[]{:S(2)}) %all-to-all-start) | async-done | bytes 7340064 | tf_op jit(solution)/shard_map/all_to_all | solution.py:593
  229.5 4.4 %put_rows.3 = f32[16,7,128,128]{3,2,1,0:T(8,128)} custom-call(s32[16]{0:T(128)} %get-tuple-element.12.source, f32[32,7,64,128]{3,2,1,0:T(8,128)} %all-to-all-done.rows, f32[16,7,128,128]{3,2,1,0:T(8,128)} %put_rows.2.refs_0_), custom_call_target="tpu_custom_call", output_to_operand_aliasing={{}: (2, {})} | custom-call | bytes 8000000 | tf_op jit(solution)/shard_map/put_rows/pallas_call | solution.py:526
  (22 shorter events, 0.7 us)
Async XLA Ops:
  4.2 23.4 %collective-permute-start = (f32[17,128,128]{2,1,0:T(8,128)}, f32[17,128,128]{2,1,0:T(8,128)S(1)}, u32[]{:S(2)}, u32[]{:S(2)}) collective-permute-start(f32[17,128,128]{2,1,0:T(8,128)} %get-tuple-element.9.a_last), channel_id=1, source_target_pairs={{0,1},{1,2},{2,3},{3,4},{4,5},{5,6},{6,7},{7,8},{8,9},{9,10},{10,1... | collective-permute-start | bytes 3342344 | tf_op jit(solution)/shard_map/ppermute | solution.py:561
  4.3 23.3 %collective-permute-start.1 = (f32[17,128,128]{2,1,0:T(8,128)}, f32[17,128,128]{2,1,0:T(8,128)S(1)}, u32[]{:S(2)}, u32[]{:S(2)}) collective-permute-start(f32[17,128,128]{2,1,0:T(8,128)} %get-tuple-element.10.a_first), channel_id=1, source_target_pairs={{1,0},{2,1},{3,2},{4,3},{5,4},{6,5},{7,6},{8,7},{9,8},{10,9},{11,1... | collective-permute-start | bytes 3342344 | tf_op jit(solution)/shard_map/ppermute | solution.py:562
  27.6 1.0 copy-start
  28.6 1.0 copy-start.1
  34.8 97.2 %all-to-all-start.1 = ((f32[32,7,64,128]{3,2,1,0:T(8,128)}), f32[32,7,64,128]{3,2,1,0:T(8,128)}, u32[]{:S(2)}, u32[]{:S(2)}) async-start(f32[32,7,64,128]{3,2,1,0:T(8,128)} %edge_rows.2.behind_ref), calls=%async_computation.1 | async-start | bytes 14680064 | tf_op jit(solution)/shard_map/all_to_all | solution.py:593
  60.1 6.5 %copy-start.2 = (s32[2048]{0:T(1024)S(1)}, s32[2048]{0:T(1024)}, u32[]{:S(2)}) copy-start(s32[2048]{0:T(1024)} %param.11) | copy-start | bytes 24580
  63.7 41.9 %collective-permute-start.4 = (f32[4,7,64,128]{3,2,1,0:T(8,128)}, f32[4,7,64,128]{3,2,1,0:T(8,128)S(1)}, u32[]{:S(2)}, u32[]{:S(2)}) collective-permute-start(f32[4,7,64,128]{3,2,1,0:T(8,128)} %get-tuple-element.20), channel_id=1, source_target_pairs={{0,96},{32,0},{64,32},{96,64},{1,97},{33,1},{65,33},{97,65},{2,98}... | collective-permute-start | bytes 2752520 | tf_op jit(solution)/shard_map/ppermute | solution.py:599
  65.7 40.0 %collective-permute-start.3 = (f32[4,7,64,128]{3,2,1,0:T(8,128)}, f32[4,7,64,128]{3,2,1,0:T(8,128)}, u32[]{:S(2)}, u32[]{:S(2)}) collective-permute-start(f32[4,7,64,128]{3,2,1,0:T(8,128)} %get-tuple-element.21), channel_id=1, source_target_pairs={{0,64},{32,96},{64,0},{96,32},{1,65},{33,97},{65,1},{97,33},{2,66}... | collective-permute-start | bytes 2752520 | tf_op jit(solution)/shard_map/ppermute | solution.py:599
  65.7 43.2 %collective-permute-start.2 = (f32[4,7,64,128]{3,2,1,0:T(8,128)S(1)}, f32[4,7,64,128]{3,2,1,0:T(8,128)}, u32[]{:S(2)}, u32[]{:S(2)}) collective-permute-start(f32[4,7,64,128]{3,2,1,0:T(8,128)S(1)} %get-tuple-element.22), channel_id=1, source_target_pairs={{0,32},{32,64},{64,96},{96,0},{1,33},{33,65},{65,97},{97,1},{2,34}... | collective-permute-start | bytes 2752520 | tf_op jit(solution)/shard_map/ppermute | solution.py:599
  132.0 97.4 %all-to-all-start = ((f32[32,7,64,128]{3,2,1,0:T(8,128)}), f32[32,7,64,128]{3,2,1,0:T(8,128)}, u32[]{:S(2)}, u32[]{:S(2)}) async-start(f32[32,7,64,128]{3,2,1,0:T(8,128)} %move_rows.2), calls=%async_computation | async-start | bytes 14680064 | tf_op jit(solution)/shard_map/all_to_all | solution.py:593
  142.2 6.8 %copy-start.3 = (s32[16]{0:T(128)S(1)}, s32[16]{0:T(128)}, u32[]{:S(2)}) copy-start(s32[16]{0:T(128)} %multiply_add_fusion.source_ref.target_ref) | copy-start | bytes 196
  145.9 41.8 %collective-permute-start.7 = (f32[4,7,64,128]{3,2,1,0:T(8,128)}, f32[4,7,64,128]{3,2,1,0:T(8,128)S(1)}, u32[]{:S(2)}, u32[]{:S(2)}) collective-permute-start(f32[4,7,64,128]{3,2,1,0:T(8,128)} %get-tuple-element.16), channel_id=1, source_target_pairs={{0,96},{32,0},{64,32},{96,64},{1,97},{33,1},{65,33},{97,65},{2,98}... | collective-permute-start | bytes 2752520 | tf_op jit(solution)/shard_map/ppermute | solution.py:599
  147.8 39.9 %collective-permute-start.6 = (f32[4,7,64,128]{3,2,1,0:T(8,128)}, f32[4,7,64,128]{3,2,1,0:T(8,128)}, u32[]{:S(2)}, u32[]{:S(2)}) collective-permute-start(f32[4,7,64,128]{3,2,1,0:T(8,128)} %get-tuple-element.17), channel_id=1, source_target_pairs={{0,64},{32,96},{64,0},{96,32},{1,65},{33,97},{65,1},{97,33},{2,66}... | collective-permute-start | bytes 2752520 | tf_op jit(solution)/shard_map/ppermute | solution.py:599
  147.8 43.0 %collective-permute-start.5 = (f32[4,7,64,128]{3,2,1,0:T(8,128)S(1)}, f32[4,7,64,128]{3,2,1,0:T(8,128)}, u32[]{:S(2)}, u32[]{:S(2)}) collective-permute-start(f32[4,7,64,128]{3,2,1,0:T(8,128)S(1)} %get-tuple-element.18), channel_id=1, source_target_pairs={{0,32},{32,64},{64,96},{96,0},{1,33},{33,65},{65,97},{97,1},{2,34}... | collective-permute-start | bytes 2752520 | tf_op jit(solution)/shard_map/ppermute | solution.py:599

commit v7 on v5

--- a/solution.py
+++ b/solution.py
@@ -315,7 +315,7 @@
         out_shape=jax.ShapeDtypeStruct(out_rows.shape, F32),
         input_output_aliases={7: 0},
         compiler_params=pltpu.CompilerParams(
-            dimension_semantics=("arbitrary",), vmem_limit_bytes=60 << 20
+            dimension_semantics=("arbitrary",), vmem_limit_bytes=50 << 20
         ),
         cost_estimate=pl.CostEstimate(flops=2_000_000_000, bytes_accessed=10_000_000, transcendentals=0),
         name="edge_rows",

time: 235 us -> 232 us (0.987)
  no operation moved by 1% of the time
where the time goes in v7:
time: 232 us
  waiting for transfers between devices  127 us (55%)
  Pallas kernels  61.4 us (26%)
  starting transfers between devices  25.7 us (11%)
  other arithmetic  10.1 us (4%)
  local copies, waits for them, and re-layouts  7.51 us (3%)
    ppermute x6, waiting for transfers between devices, along_x(): parts.append(lax.ppermute(x[k * depth:(k + 1) * depth], 'gx', pairs))  82.1 us
    all_to_all x2, waiting for transfers between devices, over_y(): return lax.all_to_all(x, 'gy', split_axis=0, concat_axis=0, tiled=True)  44.5 us
    pallas_call x2, Pallas kernels, main_product(): pl.pallas_call(functools.partial(main_kernel, half), grid_spec=pltpu.Pref...  30.3 us
    all_to_all x2, starting transfers between devices, over_y(): return lax.all_to_all(x, 'gy', split_axis=0, concat_axis=0, tiled=True)  10 us
    pallas_call x2, Pallas kernels, edge_product(): pl.pallas_call(functools.partial(edge_kernel, half), grid_spec=pltpu.Pref...  9.19 us
    pallas_call x2, Pallas kernels, move_rows(): pl.pallas_call(move_kernel, grid_spec=pltpu.PrefetchScalarGridSpec(num_sc...  8.89 us
    pallas_call x2, Pallas kernels, put_rows(): pl.pallas_call(functools.partial(put_kernel, half), grid_spec=pltpu.Prefe...  8.87 us
    ppermute x1, starting transfers between devices, shards(): behind = lax.ppermute(down, AXES, below)  8.27 us
  transfers between devices with their start and end apart: 10, of which 6 were waited for; matrix products, arithmetic and copies ran while one was open for 8% of the time, Pallas kernels for 21%

profile of v7, /device:TPU:0, one launch (start us, length us, event | category | flops | bytes accessed | tf_op | source)
XLA Modules:
  0.0 231.6 jit_solution(6388614257902350591)
XLA Ops:
  0.0 4.2 %plan.1 = (s32[384]{0:T(512)}, f32[17,128,128]{2,1,0:T(8,128)}, f32[17,128,128]{2,1,0:T(8,128)}) custom-call(s32[1]{0:T(128)} %bitcast.2.place, s32[3,48]{1,0:T(4,128)} %bitcast.17, s32[48]{0:T(128)} %length.1, f32[48,3,128,128]{3,2,1,0:T(8,128)} %a_ref.3, f32[48,2,128,128]{3,2,1,0:T(8,128)} %p_last.3, s32[48,128]{1,0:T(8,128)} %bitcast.15, s32[16,128]{1,0:T(8,128)} %bitcast.14), custom_call_target="tpu_custom_call" | custom-call | bytes 5000000 | tf_op jit(solution)/shard_map/plan/pallas_call | solution.py:422
  4.3 8.3 %collective-permute-start.1 = (f32[17,128,128]{2,1,0:T(8,128)}, f32[17,128,128]{2,1,0:T(8,128)S(1)}, u32[]{:S(2)}, u32[]{:S(2)}) collective-permute-start(f32[17,128,128]{2,1,0:T(8,128)} %get-tuple-element.10.a_first), channel_id=1, source_target_pairs={{1,0},{2,1},{3,2},{4,3},{5,4},{6,5},{7,6},{8,7},{9,8},{10,9},{11,1... | collective-permute-start | bytes 3342344 | tf_op jit(solution)/shard_map/ppermute | solution.py:540
  12.5 15.1 %triple_product.2.in_rows = f32[32,7,64,128]{3,2,1,0:T(8,128)} custom-call(s32[384]{0:T(512)} %get-tuple-element.8.plan.behind_ref, f32[48,3,128,128]{3,2,1,0:T(8,128)} %a_ref.3, f32[48,2,128,128]{3,2,1,0:T(8,128)} %p_last.3, f32[48,2,128,128]{3,2,1,0:T(8,128)} %p_last.3, f32[48,2,128,128]{3,2,1,0:T(8,128)} %p_last.3, s32[384]{0:T(512)} %get-tuple-element.8.plan.behind_ref), custom_call_target="tpu_custom_call" | custom-call | flops 12000000000 | bytes 20000000 | tf_op jit(solution)/shard_map/triple_product/pallas_call | solution.py:177
  27.7 4.6 %edge_rows.2.behind_ref = f32[32,7,64,128]{3,2,1,0:T(8,128)} custom-call(s32[384]{0:T(512)S(1)} %copy-done.1, f32[17,128,128]{2,1,0:T(8,128)S(1)} %collective-permute-done.before, f32[17,128,128]{2,1,0:T(8,128)S(1)} %collective-permute-done.1.after, f32[17,128,128]{2,1,0:T(8,128)S(1)} %copy-done, ...), custom_call_target="tpu_custom_call", output_to_operand_aliasing={{}: (7, {})} | custom-call | flops 2000000000 | bytes 10000000 | tf_op jit(solution)/shard_map/edge_rows/pallas_call | solution.py:299
  32.3 4.9 %all-to-all-start.1 = ((f32[32,7,64,128]{3,2,1,0:T(8,128)}), f32[32,7,64,128]{3,2,1,0:T(8,128)}, u32[]{:S(2)}, u32[]{:S(2)}) async-start(f32[32,7,64,128]{3,2,1,0:T(8,128)} %edge_rows.2.behind_ref), calls=%async_computation.1 | async-start | bytes 14680064 | tf_op jit(solution)/shard_map/all_to_all | solution.py:571
  37.3 15.2 %triple_product.3.in_rows = f32[16,7,64,128]{3,2,1,0:T(8,128)} custom-call(s32[384]{0:T(512)} %get-tuple-element.8.plan.behind_ref, f32[48,3,128,128]{3,2,1,0:T(8,128)} %a_ref.3, f32[48,2,128,128]{3,2,1,0:T(8,128)} %p_last.3, f32[48,2,128,128]{3,2,1,0:T(8,128)} %p_last.3, f32[48,2,128,128]{3,2,1,0:T(8,128)} %p_last.3, f32[32,7,64,128]{3,2,1,0:T(8,128)} %edge_rows.2.behind_ref), custom_call_target="tpu_custom_call" | custom-call | flops 12000000000 | bytes 20000000 | tf_op jit(solution)/shard_map/triple_product/pallas_call | solution.py:177
  52.4 4.6 %edge_rows.3 = f32[16,7,64,128]{3,2,1,0:T(8,128)} custom-call(s32[384]{0:T(512)S(1)} %copy-done.2, f32[17,128,128]{2,1,0:T(8,128)S(1)} %collective-permute-done.before, f32[17,128,128]{2,1,0:T(8,128)S(1)} %collective-permute-done.1.after, f32[17,128,128]{2,1,0:T(8,128)S(1)} %copy-done, ...), custom_call_target="tpu_custom_call", output_to_operand_aliasing={{}: (7, {})} | custom-call | flops 2000000000 | bytes 10000000 | tf_op jit(solution)/shard_map/edge_rows/pallas_call | solution.py:299
  57.1 3.6 %fusion.9 = (f32[4,7,64,128]{3,2,1,0:T(8,128)S(1)}, f32[4,7,64,128]{3,2,1,0:T(8,128)}, f32[4,7,64,128]{3,2,1,0:T(8,128)}, f32[4,7,64,128]{3,2,1,0:T(8,128)S(1)}) fusion(f32[16,7,64,128]{3,2,1,0:T(8,128)} %edge_rows.3), kind=kLoop, calls=%fused_computation.41 | loop fusion | bytes 7340032 | tf_op jit(solution)/shard_map/slice | solution.py:574
  60.7 2.8 %collective-permute-start.4 = (f32[4,7,64,128]{3,2,1,0:T(8,128)}, f32[4,7,64,128]{3,2,1,0:T(8,128)S(1)}, u32[]{:S(2)}, u32[]{:S(2)}) collective-permute-start(f32[4,7,64,128]{3,2,1,0:T(8,128)} %get-tuple-element.20), channel_id=1, source_target_pairs={{0,96},{32,0},{64,32},{96,64},{1,97},{33,1},{65,33},{97,65},{2,98}... | collective-permute-start | bytes 2752520 | tf_op jit(solution)/shard_map/ppermute | solution.py:577
  63.5 0.9 collective-permute-start.2
  64.5 0.6 fusion.5.target_ref
  65.1 0.2 convert_reduce_fusion
  65.2 0.5 multiply_add_fusion.source_ref.target_ref
  65.8 37.7 %collective-permute-done.4 = f32[4,7,64,128]{3,2,1,0:T(8,128)S(1)} collective-permute-done((f32[4,7,64,128]{3,2,1,0:T(8,128)}, f32[4,7,64,128]{3,2,1,0:T(8,128)S(1)}, u32[]{:S(2)}, u32[]{:S(2)}) %collective-permute-start.4) | collective-permute-done | bytes 917536 | tf_op jit(solution)/shard_map/ppermute | solution.py:577
  103.5 3.2 %collective-permute-done.2 = f32[4,7,64,128]{3,2,1,0:T(8,128)} collective-permute-done((f32[4,7,64,128]{3,2,1,0:T(8,128)S(1)}, f32[4,7,64,128]{3,2,1,0:T(8,128)}, u32[]{:S(2)}, u32[]{:S(2)}) %collective-permute-start.2) | collective-permute-done | bytes 917536 | tf_op jit(solution)/shard_map/ppermute | solution.py:577
  106.7 3.6 %pad_maximum_fusion.rows_in = f32[16,7,64,128]{3,2,1,0:T(8,128)} fusion(f32[4,7,64,128]{3,2,1,0:T(8,128)S(1)} %collective-permute-done.4, f32[4,7,64,128]{3,2,1,0:T(8,128)} %collective-permute-done.3, f32[4,7,64,128]{3,2,1,0:T(8,128)} %collective-permute-done.2, f32[4,7,64,128]{3,2,1,0:T(8,128)S(1)} %get-tuple-element.19), kind=kLoop, calls=%fused_computation | loop fusion | flops 2752512 | bytes 7340032 | tf_op jit(solution)/shard_map/concatenate | solution.py:578
  110.3 4.4 %move_rows.2 = f32[32,7,64,128]{3,2,1,0:T(8,128)} custom-call(s32[16]{0:T(128)} %multiply_add_fusion.source_ref.target_ref, s32[16]{0:T(128)} %fusion.5.target_ref, f32[16,7,64,128]{3,2,1,0:T(8,128)} %pad_maximum_fusion.rows_in), custom_call_target="tpu_custom_call" | custom-call | bytes 8000000 | tf_op jit(solution)/shard_map/move_rows/pallas_call | solution.py:473
  114.8 14.8 %all-to-all-done.1.rows_in = f32[32,7,64,128]{3,2,1,0:T(8,128)} async-done(((f32[32,7,64,128]{3,2,1,0:T(8,128)}), f32[32,7,64,128]{3,2,1,0:T(8,128)}, u32[]{:S(2)}, u32[]{:S(2)}) %all-to-all-start.1) | async-done | bytes 7340064 | tf_op jit(solution)/shard_map/all_to_all | solution.py:571
  129.5 5.1 %all-to-all-start = ((f32[32,7,64,128]{3,2,1,0:T(8,128)}), f32[32,7,64,128]{3,2,1,0:T(8,128)}, u32[]{:S(2)}, u32[]{:S(2)}) async-start(f32[32,7,64,128]{3,2,1,0:T(8,128)} %move_rows.2), calls=%async_computation | async-start | bytes 14680064 | tf_op jit(solution)/shard_map/all_to_all | solution.py:571
  134.7 0.6 select_reduce_fusion.1.source_ref
  135.2 4.4 %move_rows.3 = f32[16,7,64,128]{3,2,1,0:T(8,128)} custom-call(s32[16]{0:T(128)} %select_reduce_fusion.1.source_ref, s32[16]{0:T(128)} %multiply_add_fusion.source_ref.target_ref, f32[32,7,64,128]{3,2,1,0:T(8,128)} %all-to-all-done.1.rows_in), custom_call_target="tpu_custom_call" | custom-call | bytes 8000000 | tf_op jit(solution)/shard_map/move_rows/pallas_call | solution.py:473
  139.7 3.7 %fusion.8 = (f32[4,7,64,128]{3,2,1,0:T(8,128)S(1)}, f32[4,7,64,128]{3,2,1,0:T(8,128)}, f32[4,7,64,128]{3,2,1,0:T(8,128)}, f32[4,7,64,128]{3,2,1,0:T(8,128)S(1)}) fusion(f32[16,7,64,128]{3,2,1,0:T(8,128)} %move_rows.3), kind=kLoop, calls=%fused_computation.40 | loop fusion | bytes 7340032 | tf_op jit(solution)/shard_map/slice | solution.py:574
  143.4 2.8 %collective-permute-start.7 = (f32[4,7,64,128]{3,2,1,0:T(8,128)}, f32[4,7,64,128]{3,2,1,0:T(8,128)S(1)}, u32[]{:S(2)}, u32[]{:S(2)}) collective-permute-start(f32[4,7,64,128]{3,2,1,0:T(8,128)} %get-tuple-element.16), channel_id=1, source_target_pairs={{0,96},{32,0},{64,32},{96,64},{1,97},{33,1},{65,33},{97,65},{2,98}... | collective-permute-start | bytes 2752520 | tf_op jit(solution)/shard_map/ppermute | solution.py:577
  146.2 0.9 collective-permute-start.5
  147.2 0.2 convert_reduce_fusion.1
  147.3 0.7 select_reduce_fusion.2
  148.1 38.0 %collective-permute-done.7 = f32[4,7,64,128]{3,2,1,0:T(8,128)S(1)} collective-permute-done((f32[4,7,64,128]{3,2,1,0:T(8,128)}, f32[4,7,64,128]{3,2,1,0:T(8,128)S(1)}, u32[]{:S(2)}, u32[]{:S(2)}) %collective-permute-start.7) | collective-permute-done | bytes 917536 | tf_op jit(solution)/shard_map/ppermute | solution.py:577
  186.0 3.2 %collective-permute-done.5 = f32[4,7,64,128]{3,2,1,0:T(8,128)} collective-permute-done((f32[4,7,64,128]{3,2,1,0:T(8,128)S(1)}, f32[4,7,64,128]{3,2,1,0:T(8,128)}, u32[]{:S(2)}, u32[]{:S(2)}) %collective-permute-start.5) | collective-permute-done | bytes 917536 | tf_op jit(solution)/shard_map/ppermute | solution.py:577
  189.2 3.6 %pad_maximum_fusion.1.rows = f32[16,7,64,128]{3,2,1,0:T(8,128)} fusion(f32[4,7,64,128]{3,2,1,0:T(8,128)S(1)} %collective-permute-done.7, f32[4,7,64,128]{3,2,1,0:T(8,128)} %collective-permute-done.6, f32[4,7,64,128]{3,2,1,0:T(8,128)} %collective-permute-done.5, f32[4,7,64,128]{3,2,1,0:T(8,128)S(1)} %get-tuple-element.15), kind=kLoop, calls=%fused_computation.1 | loop fusion | flops 2752512 | bytes 7340032 | tf_op jit(solution)/shard_map/concatenate | solution.py:578
  192.8 4.4 %put_rows.2.refs_0_ = f32[16,7,128,128]{3,2,1,0:T(8,128)} custom-call(s32[16]{0:T(128)} %get-tuple-element.11.source, f32[16,7,64,128]{3,2,1,0:T(8,128)} %pad_maximum_fusion.1.rows), custom_call_target="tpu_custom_call" | custom-call | bytes 8000000 | tf_op jit(solution)/shard_map/put_rows/pallas_call | solution.py:504
  197.3 29.7 %all-to-all-done.rows = f32[32,7,64,128]{3,2,1,0:T(8,128)} async-done(((f32[32,7,64,128]{3,2,1,0:T(8,128)}), f32[32,7,64,128]{3,2,1,0:T(8,128)}, u32[]{:S(2)}, u32[]{:S(2)}) %all-to-all-start) | async-done | bytes 7340064 | tf_op jit(solution)/shard_map/all_to_all | solution.py:571
  227.0 4.4 %put_rows.3 = f32[16,7,128,128]{3,2,1,0:T(8,128)} custom-call(s32[16]{0:T(128)} %get-tuple-element.12.source, f32[32,7,64,128]{3,2,1,0:T(8,128)} %all-to-all-done.rows, f32[16,7,128,128]{3,2,1,0:T(8,128)} %put_rows.2.refs_0_), custom_call_target="tpu_custom_call", output_to_operand_aliasing={{}: (2, {})} | custom-call | bytes 8000000 | tf_op jit(solution)/shard_map/put_rows/pallas_call | solution.py:504
  (24 shorter events, 0.4 us)
Async XLA Ops:
  4.2 23.5 %collective-permute-start = (f32[17,128,128]{2,1,0:T(8,128)}, f32[17,128,128]{2,1,0:T(8,128)S(1)}, u32[]{:S(2)}, u32[]{:S(2)}) collective-permute-start(f32[17,128,128]{2,1,0:T(8,128)} %get-tuple-element.9.a_last), channel_id=1, source_target_pairs={{0,1},{1,2},{2,3},{3,4},{4,5},{5,6},{6,7},{7,8},{8,9},{9,10},{10,1... | collective-permute-start | bytes 3342344 | tf_op jit(solution)/shard_map/ppermute | solution.py:539
  4.3 23.4 %collective-permute-start.1 = (f32[17,128,128]{2,1,0:T(8,128)}, f32[17,128,128]{2,1,0:T(8,128)S(1)}, u32[]{:S(2)}, u32[]{:S(2)}) collective-permute-start(f32[17,128,128]{2,1,0:T(8,128)} %get-tuple-element.10.a_first), channel_id=1, source_target_pairs={{1,0},{2,1},{3,2},{4,3},{5,4},{6,5},{7,6},{8,7},{9,8},{10,9},{11,1... | collective-permute-start | bytes 3342344 | tf_op jit(solution)/shard_map/ppermute | solution.py:540
  12.5 15.2 %copy-start = (f32[17,128,128]{2,1,0:T(8,128)S(1)}, f32[17,128,128]{2,1,0:T(8,128)}, u32[]{:S(2)}) copy-start(f32[17,128,128]{2,1,0:T(8,128)} %get-tuple-element.10.a_first) | copy-start | bytes 3342340
  12.5 15.2 %copy-start.1 = (s32[384]{0:T(512)S(1)}, s32[384]{0:T(512)}, u32[]{:S(2)}) copy-start(s32[384]{0:T(512)} %get-tuple-element.8.plan.behind_ref) | copy-start | bytes 4612
  32.3 97.2 %all-to-all-start.1 = ((f32[32,7,64,128]{3,2,1,0:T(8,128)}), f32[32,7,64,128]{3,2,1,0:T(8,128)}, u32[]{:S(2)}, u32[]{:S(2)}) async-start(f32[32,7,64,128]{3,2,1,0:T(8,128)} %edge_rows.2.behind_ref), calls=%async_computation.1 | async-start | bytes 14680064 | tf_op jit(solution)/shard_map/all_to_all | solution.py:571
  37.2 15.2 %copy-start.2 = (s32[384]{0:T(512)S(1)}, s32[384]{0:T(512)}, u32[]{:S(2)}) copy-start(s32[384]{0:T(512)} %get-tuple-element.8.plan.behind_ref) | copy-start | bytes 4612
  57.1 7.3 %copy-start.3 = (s32[2048]{0:T(1024)S(1)}, s32[2048]{0:T(1024)}, u32[]{:S(2)}) copy-start(s32[2048]{0:T(1024)} %param.11) | copy-start | bytes 24580
  60.7 42.8 %collective-permute-start.4 = (f32[4,7,64,128]{3,2,1,0:T(8,128)}, f32[4,7,64,128]{3,2,1,0:T(8,128)S(1)}, u32[]{:S(2)}, u32[]{:S(2)}) collective-permute-start(f32[4,7,64,128]{3,2,1,0:T(8,128)} %get-tuple-element.20), channel_id=1, source_target_pairs={{0,96},{32,0},{64,32},{96,64},{1,97},{33,1},{65,33},{97,65},{2,98}... | collective-permute-start | bytes 2752520 | tf_op jit(solution)/shard_map/ppermute | solution.py:577
  63.5 40.0 %collective-permute-start.3 = (f32[4,7,64,128]{3,2,1,0:T(8,128)}, f32[4,7,64,128]{3,2,1,0:T(8,128)}, u32[]{:S(2)}, u32[]{:S(2)}) collective-permute-start(f32[4,7,64,128]{3,2,1,0:T(8,128)} %get-tuple-element.21), channel_id=1, source_target_pairs={{0,64},{32,96},{64,0},{96,32},{1,65},{33,97},{65,1},{97,33},{2,66}... | collective-permute-start | bytes 2752520 | tf_op jit(solution)/shard_map/ppermute | solution.py:577
  63.5 43.2 %collective-permute-start.2 = (f32[4,7,64,128]{3,2,1,0:T(8,128)S(1)}, f32[4,7,64,128]{3,2,1,0:T(8,128)}, u32[]{:S(2)}, u32[]{:S(2)}) collective-permute-start(f32[4,7,64,128]{3,2,1,0:T(8,128)S(1)} %get-tuple-element.22), channel_id=1, source_target_pairs={{0,32},{32,64},{64,96},{96,0},{1,33},{33,65},{65,97},{97,1},{2,34}... | collective-permute-start | bytes 2752520 | tf_op jit(solution)/shard_map/ppermute | solution.py:577
  129.5 97.4 %all-to-all-start = ((f32[32,7,64,128]{3,2,1,0:T(8,128)}), f32[32,7,64,128]{3,2,1,0:T(8,128)}, u32[]{:S(2)}, u32[]{:S(2)}) async-start(f32[32,7,64,128]{3,2,1,0:T(8,128)} %move_rows.2), calls=%async_computation | async-start | bytes 14680064 | tf_op jit(solution)/shard_map/all_to_all | solution.py:571
  139.7 7.7 %copy-start.4 = (s32[16]{0:T(128)S(1)}, s32[16]{0:T(128)}, u32[]{:S(2)}) copy-start(s32[16]{0:T(128)} %multiply_add_fusion.source_ref.target_ref) | copy-start | bytes 196
  143.4 42.7 %collective-permute-start.7 = (f32[4,7,64,128]{3,2,1,0:T(8,128)}, f32[4,7,64,128]{3,2,1,0:T(8,128)S(1)}, u32[]{:S(2)}, u32[]{:S(2)}) collective-permute-start(f32[4,7,64,128]{3,2,1,0:T(8,128)} %get-tuple-element.16), channel_id=1, source_target_pairs={{0,96},{32,0},{64,32},{96,64},{1,97},{33,1},{65,33},{97,65},{2,98}... | collective-permute-start | bytes 2752520 | tf_op jit(solution)/shard_map/ppermute | solution.py:577
  146.1 39.9 %collective-permute-start.6 = (f32[4,7,64,128]{3,2,1,0:T(8,128)}, f32[4,7,64,128]{3,2,1,0:T(8,128)}, u32[]{:S(2)}, u32[]{:S(2)}) collective-permute-start(f32[4,7,64,128]{3,2,1,0:T(8,128)} %get-tuple-element.17), channel_id=1, source_target_pairs={{0,64},{32,96},{64,0},{96,32},{1,65},{33,97},{65,1},{97,33},{2,66}... | collective-permute-start | bytes 2752520 | tf_op jit(solution)/shard_map/ppermute | solution.py:577
  146.2 43.0 %collective-permute-start.5 = (f32[4,7,64,128]{3,2,1,0:T(8,128)S(1)}, f32[4,7,64,128]{3,2,1,0:T(8,128)}, u32[]{:S(2)}, u32[]{:S(2)}) collective-permute-start(f32[4,7,64,128]{3,2,1,0:T(8,128)S(1)} %get-tuple-element.18), channel_id=1, source_target_pairs={{0,32},{32,64},{64,96},{96,0},{1,33},{33,65},{65,97},{97,1},{2,34}... | collective-permute-start | bytes 2752520 | tf_op jit(solution)/shard_map/ppermute | solution.py:577

commit v8 on v7

--- a/solution.py
+++ b/solution.py
@@ -61,7 +61,8 @@
 
 
 def row_product(p_pair, tiles, half):
-    turned = jnp.concatenate([turn(p_pair[0], half), turn(p_pair[1], half)], axis=0)
+    part = slice(half * HALF, (half + 1) * HALF)
+    turned = jnp.concatenate([p_pair[0][:, part], p_pair[1][:, part]], axis=1).T
     return matmul(left_operand(turned), right_operand(jnp.concatenate(tiles, axis=1)))
 
 

time: 232 us -> 232 us (level)
  no operation moved by 1% of the time
where the time goes in v8:
time: 232 us
  waiting for transfers between devices  126 us (54%)
  Pallas kernels  61.8 us (27%)
  starting transfers between devices  25.6 us (11%)
  other arithmetic  10.1 us (4%)
  local copies, waits for them, and re-layouts  7.51 us (3%)
    ppermute x6, waiting for transfers between devices, along_x(): parts.append(lax.ppermute(x[k * depth:(k + 1) * depth], 'gx', pairs))  82.1 us
    all_to_all x2, waiting for transfers between devices, over_y(): return lax.all_to_all(x, 'gy', split_axis=0, concat_axis=0, tiled=True)  44.3 us
    pallas_call x2, Pallas kernels, main_product(): pl.pallas_call(functools.partial(main_kernel, half), grid_spec=pltpu.Pref...  30.4 us
    all_to_all x2, starting transfers between devices, over_y(): return lax.all_to_all(x, 'gy', split_axis=0, concat_axis=0, tiled=True)  10 us
    pallas_call x2, Pallas kernels, edge_product(): pl.pallas_call(functools.partial(edge_kernel, half), grid_spec=pltpu.Pref...  9.45 us
    pallas_call x2, Pallas kernels, move_rows(): pl.pallas_call(move_kernel, grid_spec=pltpu.PrefetchScalarGridSpec(num_sc...  8.89 us
    pallas_call x2, Pallas kernels, put_rows(): pl.pallas_call(functools.partial(put_kernel, half), grid_spec=pltpu.Prefe...  8.87 us
    ppermute x1, starting transfers between devices, shards(): behind = lax.ppermute(down, AXES, below)  8.27 us
  transfers between devices with their start and end apart: 10, of which 6 were waited for; matrix products, arithmetic and copies ran while one was open for 8% of the time, Pallas kernels for 21%

profile of v8, /device:TPU:0, one launch (start us, length us, event | category | flops | bytes accessed | tf_op | source)
XLA Modules:
  0.0 231.6 jit_solution(13274459755259011158)
XLA Ops:
  0.0 4.2 %plan.1 = (s32[384]{0:T(512)}, f32[17,128,128]{2,1,0:T(8,128)}, f32[17,128,128]{2,1,0:T(8,128)}) custom-call(s32[1]{0:T(128)} %bitcast.2.place, s32[3,48]{1,0:T(4,128)} %bitcast.17, s32[48]{0:T(128)} %length.1, f32[48,3,128,128]{3,2,1,0:T(8,128)} %a_ref.3, f32[48,2,128,128]{3,2,1,0:T(8,128)} %p_last.3, s32[48,128]{1,0:T(8,128)} %bitcast.15, s32[16,128]{1,0:T(8,128)} %bitcast.14), custom_call_target="tpu_custom_call" | custom-call | bytes 5000000 | tf_op jit(solution)/shard_map/plan/pallas_call | solution.py:423
  4.3 8.3 %collective-permute-start.1 = (f32[17,128,128]{2,1,0:T(8,128)}, f32[17,128,128]{2,1,0:T(8,128)S(1)}, u32[]{:S(2)}, u32[]{:S(2)}) collective-permute-start(f32[17,128,128]{2,1,0:T(8,128)} %get-tuple-element.10.a_first), channel_id=1, source_target_pairs={{1,0},{2,1},{3,2},{4,3},{5,4},{6,5},{7,6},{8,7},{9,8},{10,9},{11,1... | collective-permute-start | bytes 3342344 | tf_op jit(solution)/shard_map/ppermute | solution.py:541
  12.5 15.2 %triple_product.2.in_rows = f32[32,7,64,128]{3,2,1,0:T(8,128)} custom-call(s32[384]{0:T(512)} %get-tuple-element.8.plan.behind_ref, f32[48,3,128,128]{3,2,1,0:T(8,128)} %a_ref.3, f32[48,2,128,128]{3,2,1,0:T(8,128)} %p_last.3, f32[48,2,128,128]{3,2,1,0:T(8,128)} %p_last.3, f32[48,2,128,128]{3,2,1,0:T(8,128)} %p_last.3, s32[384]{0:T(512)} %get-tuple-element.8.plan.behind_ref), custom_call_target="tpu_custom_call" | custom-call | flops 12000000000 | bytes 20000000 | tf_op jit(solution)/shard_map/triple_product/pallas_call | solution.py:178
  27.8 4.6 %edge_rows.2.behind_ref = f32[32,7,64,128]{3,2,1,0:T(8,128)} custom-call(s32[384]{0:T(512)S(1)} %copy-done.1, f32[17,128,128]{2,1,0:T(8,128)S(1)} %collective-permute-done.before, f32[17,128,128]{2,1,0:T(8,128)S(1)} %collective-permute-done.1.after, f32[17,128,128]{2,1,0:T(8,128)S(1)} %copy-done, ...), custom_call_target="tpu_custom_call", output_to_operand_aliasing={{}: (7, {})} | custom-call | flops 2000000000 | bytes 10000000 | tf_op jit(solution)/shard_map/edge_rows/pallas_call | solution.py:300
  32.4 4.9 %all-to-all-start.1 = ((f32[32,7,64,128]{3,2,1,0:T(8,128)}), f32[32,7,64,128]{3,2,1,0:T(8,128)}, u32[]{:S(2)}, u32[]{:S(2)}) async-start(f32[32,7,64,128]{3,2,1,0:T(8,128)} %edge_rows.2.behind_ref), calls=%async_computation.1 | async-start | bytes 14680064 | tf_op jit(solution)/shard_map/all_to_all | solution.py:572
  37.3 15.2 %triple_product.3.in_rows = f32[16,7,64,128]{3,2,1,0:T(8,128)} custom-call(s32[384]{0:T(512)} %get-tuple-element.8.plan.behind_ref, f32[48,3,128,128]{3,2,1,0:T(8,128)} %a_ref.3, f32[48,2,128,128]{3,2,1,0:T(8,128)} %p_last.3, f32[48,2,128,128]{3,2,1,0:T(8,128)} %p_last.3, f32[48,2,128,128]{3,2,1,0:T(8,128)} %p_last.3, f32[32,7,64,128]{3,2,1,0:T(8,128)} %edge_rows.2.behind_ref), custom_call_target="tpu_custom_call" | custom-call | flops 12000000000 | bytes 20000000 | tf_op jit(solution)/shard_map/triple_product/pallas_call | solution.py:178
  52.5 4.9 %edge_rows.3 = f32[16,7,64,128]{3,2,1,0:T(8,128)} custom-call(s32[384]{0:T(512)S(1)} %copy-done.2, f32[17,128,128]{2,1,0:T(8,128)S(1)} %collective-permute-done.before, f32[17,128,128]{2,1,0:T(8,128)S(1)} %collective-permute-done.1.after, f32[17,128,128]{2,1,0:T(8,128)S(1)} %copy-done, ...), custom_call_target="tpu_custom_call", output_to_operand_aliasing={{}: (7, {})} | custom-call | flops 2000000000 | bytes 10000000 | tf_op jit(solution)/shard_map/edge_rows/pallas_call | solution.py:300
  57.4 3.6 %fusion.9 = (f32[4,7,64,128]{3,2,1,0:T(8,128)S(1)}, f32[4,7,64,128]{3,2,1,0:T(8,128)}, f32[4,7,64,128]{3,2,1,0:T(8,128)}, f32[4,7,64,128]{3,2,1,0:T(8,128)S(1)}) fusion(f32[16,7,64,128]{3,2,1,0:T(8,128)} %edge_rows.3), kind=kLoop, calls=%fused_computation.41 | loop fusion | bytes 7340032 | tf_op jit(solution)/shard_map/slice | solution.py:575
  61.1 2.7 %collective-permute-start.4 = (f32[4,7,64,128]{3,2,1,0:T(8,128)}, f32[4,7,64,128]{3,2,1,0:T(8,128)S(1)}, u32[]{:S(2)}, u32[]{:S(2)}) collective-permute-start(f32[4,7,64,128]{3,2,1,0:T(8,128)} %get-tuple-element.20), channel_id=1, source_target_pairs={{0,96},{32,0},{64,32},{96,64},{1,97},{33,1},{65,33},{97,65},{2,98}... | collective-permute-start | bytes 2752520 | tf_op jit(solution)/shard_map/ppermute | solution.py:578
  63.8 0.9 collective-permute-start.2
  64.8 0.6 fusion.5.target_ref
  65.3 0.2 convert_reduce_fusion
  65.5 0.5 multiply_add_fusion.source_ref.target_ref
  66.0 37.7 %collective-permute-done.4 = f32[4,7,64,128]{3,2,1,0:T(8,128)S(1)} collective-permute-done((f32[4,7,64,128]{3,2,1,0:T(8,128)}, f32[4,7,64,128]{3,2,1,0:T(8,128)S(1)}, u32[]{:S(2)}, u32[]{:S(2)}) %collective-permute-start.4) | collective-permute-done | bytes 917536 | tf_op jit(solution)/shard_map/ppermute | solution.py:578
  103.8 3.2 %collective-permute-done.2 = f32[4,7,64,128]{3,2,1,0:T(8,128)} collective-permute-done((f32[4,7,64,128]{3,2,1,0:T(8,128)S(1)}, f32[4,7,64,128]{3,2,1,0:T(8,128)}, u32[]{:S(2)}, u32[]{:S(2)}) %collective-permute-start.2) | collective-permute-done | bytes 917536 | tf_op jit(solution)/shard_map/ppermute | solution.py:578
  107.0 3.6 %pad_maximum_fusion.rows_in = f32[16,7,64,128]{3,2,1,0:T(8,128)} fusion(f32[4,7,64,128]{3,2,1,0:T(8,128)S(1)} %collective-permute-done.4, f32[4,7,64,128]{3,2,1,0:T(8,128)} %collective-permute-done.3, f32[4,7,64,128]{3,2,1,0:T(8,128)} %collective-permute-done.2, f32[4,7,64,128]{3,2,1,0:T(8,128)S(1)} %get-tuple-element.19), kind=kLoop, calls=%fused_computation | loop fusion | flops 2752512 | bytes 7340032 | tf_op jit(solution)/shard_map/concatenate | solution.py:579
  110.6 4.4 %move_rows.2 = f32[32,7,64,128]{3,2,1,0:T(8,128)} custom-call(s32[16]{0:T(128)} %multiply_add_fusion.source_ref.target_ref, s32[16]{0:T(128)} %fusion.5.target_ref, f32[16,7,64,128]{3,2,1,0:T(8,128)} %pad_maximum_fusion.rows_in), custom_call_target="tpu_custom_call" | custom-call | bytes 8000000 | tf_op jit(solution)/shard_map/move_rows/pallas_call | solution.py:474
  115.1 14.5 %all-to-all-done.1.rows_in = f32[32,7,64,128]{3,2,1,0:T(8,128)} async-done(((f32[32,7,64,128]{3,2,1,0:T(8,128)}), f32[32,7,64,128]{3,2,1,0:T(8,128)}, u32[]{:S(2)}, u32[]{:S(2)}) %all-to-all-start.1) | async-done | bytes 7340064 | tf_op jit(solution)/shard_map/all_to_all | solution.py:572
  129.6 5.1 %all-to-all-start = ((f32[32,7,64,128]{3,2,1,0:T(8,128)}), f32[32,7,64,128]{3,2,1,0:T(8,128)}, u32[]{:S(2)}, u32[]{:S(2)}) async-start(f32[32,7,64,128]{3,2,1,0:T(8,128)} %move_rows.2), calls=%async_computation | async-start | bytes 14680064 | tf_op jit(solution)/shard_map/all_to_all | solution.py:572
  134.7 0.6 select_reduce_fusion.1.source_ref
  135.3 4.4 %move_rows.3 = f32[16,7,64,128]{3,2,1,0:T(8,128)} custom-call(s32[16]{0:T(128)} %select_reduce_fusion.1.source_ref, s32[16]{0:T(128)} %multiply_add_fusion.source_ref.target_ref, f32[32,7,64,128]{3,2,1,0:T(8,128)} %all-to-all-done.1.rows_in), custom_call_target="tpu_custom_call" | custom-call | bytes 8000000 | tf_op jit(solution)/shard_map/move_rows/pallas_call | solution.py:474
  139.8 3.7 %fusion.8 = (f32[4,7,64,128]{3,2,1,0:T(8,128)S(1)}, f32[4,7,64,128]{3,2,1,0:T(8,128)}, f32[4,7,64,128]{3,2,1,0:T(8,128)}, f32[4,7,64,128]{3,2,1,0:T(8,128)S(1)}) fusion(f32[16,7,64,128]{3,2,1,0:T(8,128)} %move_rows.3), kind=kLoop, calls=%fused_computation.40 | loop fusion | bytes 7340032 | tf_op jit(solution)/shard_map/slice | solution.py:575
  143.4 2.7 %collective-permute-start.7 = (f32[4,7,64,128]{3,2,1,0:T(8,128)}, f32[4,7,64,128]{3,2,1,0:T(8,128)S(1)}, u32[]{:S(2)}, u32[]{:S(2)}) collective-permute-start(f32[4,7,64,128]{3,2,1,0:T(8,128)} %get-tuple-element.16), channel_id=1, source_target_pairs={{0,96},{32,0},{64,32},{96,64},{1,97},{33,1},{65,33},{97,65},{2,98}... | collective-permute-start | bytes 2752520 | tf_op jit(solution)/shard_map/ppermute | solution.py:578
  146.2 0.9 collective-permute-start.5
  147.2 0.2 convert_reduce_fusion.1
  147.4 0.7 select_reduce_fusion.2
  148.1 38.0 %collective-permute-done.7 = f32[4,7,64,128]{3,2,1,0:T(8,128)S(1)} collective-permute-done((f32[4,7,64,128]{3,2,1,0:T(8,128)}, f32[4,7,64,128]{3,2,1,0:T(8,128)S(1)}, u32[]{:S(2)}, u32[]{:S(2)}) %collective-permute-start.7) | collective-permute-done | bytes 917536 | tf_op jit(solution)/shard_map/ppermute | solution.py:578
  186.0 3.2 %collective-permute-done.5 = f32[4,7,64,128]{3,2,1,0:T(8,128)} collective-permute-done((f32[4,7,64,128]{3,2,1,0:T(8,128)S(1)}, f32[4,7,64,128]{3,2,1,0:T(8,128)}, u32[]{:S(2)}, u32[]{:S(2)}) %collective-permute-start.5) | collective-permute-done | bytes 917536 | tf_op jit(solution)/shard_map/ppermute | solution.py:578
  189.2 3.6 %pad_maximum_fusion.1.rows = f32[16,7,64,128]{3,2,1,0:T(8,128)} fusion(f32[4,7,64,128]{3,2,1,0:T(8,128)S(1)} %collective-permute-done.7, f32[4,7,64,128]{3,2,1,0:T(8,128)} %collective-permute-done.6, f32[4,7,64,128]{3,2,1,0:T(8,128)} %collective-permute-done.5, f32[4,7,64,128]{3,2,1,0:T(8,128)S(1)} %get-tuple-element.15), kind=kLoop, calls=%fused_computation.1 | loop fusion | flops 2752512 | bytes 7340032 | tf_op jit(solution)/shard_map/concatenate | solution.py:579
  192.8 4.4 %put_rows.2.refs_0_ = f32[16,7,128,128]{3,2,1,0:T(8,128)} custom-call(s32[16]{0:T(128)} %get-tuple-element.11.source, f32[16,7,64,128]{3,2,1,0:T(8,128)} %pad_maximum_fusion.1.rows), custom_call_target="tpu_custom_call" | custom-call | bytes 8000000 | tf_op jit(solution)/shard_map/put_rows/pallas_call | solution.py:505
  197.3 29.8 %all-to-all-done.rows = f32[32,7,64,128]{3,2,1,0:T(8,128)} async-done(((f32[32,7,64,128]{3,2,1,0:T(8,128)}), f32[32,7,64,128]{3,2,1,0:T(8,128)}, u32[]{:S(2)}, u32[]{:S(2)}) %all-to-all-start) | async-done | bytes 7340064 | tf_op jit(solution)/shard_map/all_to_all | solution.py:572
  227.0 4.4 %put_rows.3 = f32[16,7,128,128]{3,2,1,0:T(8,128)} custom-call(s32[16]{0:T(128)} %get-tuple-element.12.source, f32[32,7,64,128]{3,2,1,0:T(8,128)} %all-to-all-done.rows, f32[16,7,128,128]{3,2,1,0:T(8,128)} %put_rows.2.refs_0_), custom_call_target="tpu_custom_call", output_to_operand_aliasing={{}: (2, {})} | custom-call | bytes 8000000 | tf_op jit(solution)/shard_map/put_rows/pallas_call | solution.py:505
  (24 shorter events, 0.4 us)
Async XLA Ops:
  4.2 23.6 %collective-permute-start = (f32[17,128,128]{2,1,0:T(8,128)}, f32[17,128,128]{2,1,0:T(8,128)S(1)}, u32[]{:S(2)}, u32[]{:S(2)}) collective-permute-start(f32[17,128,128]{2,1,0:T(8,128)} %get-tuple-element.9.a_last), channel_id=1, source_target_pairs={{0,1},{1,2},{2,3},{3,4},{4,5},{5,6},{6,7},{7,8},{8,9},{9,10},{10,1... | collective-permute-start | bytes 3342344 | tf_op jit(solution)/shard_map/ppermute | solution.py:540
  4.3 23.5 %collective-permute-start.1 = (f32[17,128,128]{2,1,0:T(8,128)}, f32[17,128,128]{2,1,0:T(8,128)S(1)}, u32[]{:S(2)}, u32[]{:S(2)}) collective-permute-start(f32[17,128,128]{2,1,0:T(8,128)} %get-tuple-element.10.a_first), channel_id=1, source_target_pairs={{1,0},{2,1},{3,2},{4,3},{5,4},{6,5},{7,6},{8,7},{9,8},{10,9},{11,1... | collective-permute-start | bytes 3342344 | tf_op jit(solution)/shard_map/ppermute | solution.py:541
  12.5 15.2 %copy-start = (f32[17,128,128]{2,1,0:T(8,128)S(1)}, f32[17,128,128]{2,1,0:T(8,128)}, u32[]{:S(2)}) copy-start(f32[17,128,128]{2,1,0:T(8,128)} %get-tuple-element.10.a_first) | copy-start | bytes 3342340
  12.5 15.2 %copy-start.1 = (s32[384]{0:T(512)S(1)}, s32[384]{0:T(512)}, u32[]{:S(2)}) copy-start(s32[384]{0:T(512)} %get-tuple-element.8.plan.behind_ref) | copy-start | bytes 4612
  32.4 97.2 %all-to-all-start.1 = ((f32[32,7,64,128]{3,2,1,0:T(8,128)}), f32[32,7,64,128]{3,2,1,0:T(8,128)}, u32[]{:S(2)}, u32[]{:S(2)}) async-start(f32[32,7,64,128]{3,2,1,0:T(8,128)} %edge_rows.2.behind_ref), calls=%async_computation.1 | async-start | bytes 14680064 | tf_op jit(solution)/shard_map/all_to_all | solution.py:572
  37.3 15.2 %copy-start.2 = (s32[384]{0:T(512)S(1)}, s32[384]{0:T(512)}, u32[]{:S(2)}) copy-start(s32[384]{0:T(512)} %get-tuple-element.8.plan.behind_ref) | copy-start | bytes 4612
  57.4 7.2 %copy-start.3 = (s32[2048]{0:T(1024)S(1)}, s32[2048]{0:T(1024)}, u32[]{:S(2)}) copy-start(s32[2048]{0:T(1024)} %param.11) | copy-start | bytes 24580
  61.1 42.7 %collective-permute-start.4 = (f32[4,7,64,128]{3,2,1,0:T(8,128)}, f32[4,7,64,128]{3,2,1,0:T(8,128)S(1)}, u32[]{:S(2)}, u32[]{:S(2)}) collective-permute-start(f32[4,7,64,128]{3,2,1,0:T(8,128)} %get-tuple-element.20), channel_id=1, source_target_pairs={{0,96},{32,0},{64,32},{96,64},{1,97},{33,1},{65,33},{97,65},{2,98}... | collective-permute-start | bytes 2752520 | tf_op jit(solution)/shard_map/ppermute | solution.py:578
  63.8 40.0 %collective-permute-start.3 = (f32[4,7,64,128]{3,2,1,0:T(8,128)}, f32[4,7,64,128]{3,2,1,0:T(8,128)}, u32[]{:S(2)}, u32[]{:S(2)}) collective-permute-start(f32[4,7,64,128]{3,2,1,0:T(8,128)} %get-tuple-element.21), channel_id=1, source_target_pairs={{0,64},{32,96},{64,0},{96,32},{1,65},{33,97},{65,1},{97,33},{2,66}... | collective-permute-start | bytes 2752520 | tf_op jit(solution)/shard_map/ppermute | solution.py:578
  63.8 43.2 %collective-permute-start.2 = (f32[4,7,64,128]{3,2,1,0:T(8,128)S(1)}, f32[4,7,64,128]{3,2,1,0:T(8,128)}, u32[]{:S(2)}, u32[]{:S(2)}) collective-permute-start(f32[4,7,64,128]{3,2,1,0:T(8,128)S(1)} %get-tuple-element.22), channel_id=1, source_target_pairs={{0,32},{32,64},{64,96},{96,0},{1,33},{33,65},{65,97},{97,1},{2,34}... | collective-permute-start | bytes 2752520 | tf_op jit(solution)/shard_map/ppermute | solution.py:578
  129.6 97.4 %all-to-all-start = ((f32[32,7,64,128]{3,2,1,0:T(8,128)}), f32[32,7,64,128]{3,2,1,0:T(8,128)}, u32[]{:S(2)}, u32[]{:S(2)}) async-start(f32[32,7,64,128]{3,2,1,0:T(8,128)} %move_rows.2), calls=%async_computation | async-start | bytes 14680064 | tf_op jit(solution)/shard_map/all_to_all | solution.py:572
  139.8 7.6 %copy-start.4 = (s32[16]{0:T(128)S(1)}, s32[16]{0:T(128)}, u32[]{:S(2)}) copy-start(s32[16]{0:T(128)} %multiply_add_fusion.source_ref.target_ref) | copy-start | bytes 196
  143.4 42.6 %collective-permute-start.7 = (f32[4,7,64,128]{3,2,1,0:T(8,128)}, f32[4,7,64,128]{3,2,1,0:T(8,128)S(1)}, u32[]{:S(2)}, u32[]{:S(2)}) collective-permute-start(f32[4,7,64,128]{3,2,1,0:T(8,128)} %get-tuple-element.16), channel_id=1, source_target_pairs={{0,96},{32,0},{64,32},{96,64},{1,97},{33,1},{65,33},{97,65},{2,98}... | collective-permute-start | bytes 2752520 | tf_op jit(solution)/shard_map/ppermute | solution.py:578
  146.2 39.9 %collective-permute-start.6 = (f32[4,7,64,128]{3,2,1,0:T(8,128)}, f32[4,7,64,128]{3,2,1,0:T(8,128)}, u32[]{:S(2)}, u32[]{:S(2)}) collective-permute-start(f32[4,7,64,128]{3,2,1,0:T(8,128)} %get-tuple-element.17), channel_id=1, source_target_pairs={{0,64},{32,96},{64,0},{96,32},{1,65},{33,97},{65,1},{97,33},{2,66}... | collective-permute-start | bytes 2752520 | tf_op jit(solution)/shard_map/ppermute | solution.py:578
  146.2 43.0 %collective-permute-start.5 = (f32[4,7,64,128]{3,2,1,0:T(8,128)S(1)}, f32[4,7,64,128]{3,2,1,0:T(8,128)}, u32[]{:S(2)}, u32[]{:S(2)}) collective-permute-start(f32[4,7,64,128]{3,2,1,0:T(8,128)S(1)} %get-tuple-element.18), channel_id=1, source_target_pairs={{0,32},{32,64},{64,96},{96,0},{1,33},{33,65},{65,97},{97,1},{2,34}... | collective-permute-start | bytes 2752520 | tf_op jit(solution)/shard_map/ppermute | solution.py:578
